TPU v7x, 512 devices: a whole 4x8x8 slice. The times are simulated.
512 devices in a mesh: ctx: 64 (over x, z, y_hi), head: 8 (over y_lo, core).
Axes of the slice: x: 4, y: 8 (y_hi: 2, y_lo: 4; y = y_hi * 4 + y_lo), z: 8, core: 2. Of those that a mesh axis runs over, the one named last changes fastest.
Arguments:
- pairing: int32 [64], replicated, may hold values from 0 to 63, as said below
- doc_start: int32 [16384], P('ctx'), may hold values from 0 to 16383, as said below
- block_live: int32 [128, 128], replicated, may hold values from 0 to 1, as said below
- query: bfloat16 [16384, 4096], P(('ctx', 'head')), may hold values from -24 to 24
- key: bfloat16 [16384, 1024], P(('ctx', 'head')), may hold values from -24 to 24
- value: bfloat16 [16384, 1024], P(('ctx', 'head')), may hold values from -6 to 6
- grad_out: bfloat16 [16384, 4096], P(('ctx', 'head')), may hold values from -6 to 6
Outputs:
- attended: bfloat16 [16384, 4096], P(('ctx', 'head'))
- grad_query: bfloat16 [16384, 4096], P(('ctx', 'head'))
- grad_key: bfloat16 [16384, 1024], P(('ctx', 'head'))
- grad_value: bfloat16 [16384, 1024], P(('ctx', 'head'))
Inputs may be any that keep to these rules, and one draw needn't show every extreme that they name: pairing[pairing[c]] == c, and pairing[c] differs from c by at most 1. doc_start of a row is the position of the first token of its document; documents are runs of consecutive positions, the first starts at 0, each has 64 to 512 tokens except the last, which may be shorter, and one has exactly 512. block_live[a, b] == 1 exactly when b < a and the first token of global block a has doc_start at or before the last position of global block b.
All inputs are finite; a program needn't handle non-finite values.
Results may differ from a plain program's by a relative error of at most 0.03.
Values may be sent and summed in bfloat16 or wider, within the bound.
No kernel may reach another device: no remote copies, remote signals or barrier semaphores. Data moves between devices by JAX's collectives and lax.ppermute only.
A program may use at most 64 MiB of HBM per device.

v0:
```python
import math

import jax
import jax.numpy as jnp
from jax import lax
from jax.sharding import PartitionSpec as P

HEAD_DIM = 128
REACH = 4


NEGATIVE = -1e30


def shifted(value, axis, by):
    length = lax.axis_size(axis)
    pairs = [(i, i + by) for i in range(length) if 0 <= i + by < length]
    return lax.ppermute(value, axis, pairs)


def block_scores(query_block, packed, kv_count, group_size, factor):
    length = packed.shape[0]
    keys_block = packed[:, : kv_count * HEAD_DIM].reshape(length, kv_count, HEAD_DIM)
    grouped = query_block.reshape(query_block.shape[0], kv_count, group_size, HEAD_DIM)
    return (
        jnp.einsum("qgrd,kgd->grqk", grouped, keys_block, preferred_element_type=jnp.float32)
        * factor
    )


def visibility(query_id, key_id, begins, length):
    offsets = jnp.arange(length, dtype=jnp.int32)
    query_places = query_id * length + offsets
    key_places = key_id * length + offsets
    return (begins[:, None] <= key_places[None, :]) & (key_places[None, :] <= query_places[:, None])


def body(pairing, doc_start, block_live, query, key, value, grad_out):
    arrived = (
        lax.all_to_all(query, "head", split_axis=1, concat_axis=0, tiled=True),
        lax.all_to_all(key, "head", split_axis=1, concat_axis=0, tiled=True),
        lax.all_to_all(value, "head", split_axis=1, concat_axis=0, tiled=True),
        lax.all_to_all(grad_out, "head", split_axis=1, concat_axis=0, tiled=True),
    )
    query_local, key_local, value_local, upstream_local = arrived
    stretch_rows = query_local.shape[0]
    length = stretch_rows // 2
    kv_count = key_local.shape[1] // HEAD_DIM
    group_size = query_local.shape[1] // key_local.shape[1]
    kv_width = kv_count * HEAD_DIM
    factor = 1.0 / math.sqrt(HEAD_DIM)
    ctx_count = lax.axis_size("ctx")
    position = lax.axis_index("ctx")
    block_total = 2 * ctx_count
    packed_local = jnp.concatenate([key_local, value_local], axis=1)
    upward, downward = (REACH + 2, REACH + 2)
    offsets_list = (
        [0] + list(range(1, upward + 1)) + [-distance for distance in range(1, downward + 1)]
    )
    gathered = [packed_local] + [
        shifted(packed_local, "ctx", -distance) for distance in offsets_list[1:]
    ]
    stretch_count = len(offsets_list)
    stacked = jnp.stack(gathered, axis=0).reshape(2 * stretch_count, length, 2 * kv_width)
    neighbours = position + jnp.array(offsets_list, dtype=jnp.int32)
    present = (neighbours >= 0) & (neighbours < ctx_count)
    clipped = jnp.clip(neighbours, 0, ctx_count - 1)
    key_ids = jnp.stack(
        [
            jnp.where(present, clipped, -1),
            jnp.where(present, block_total - 1 - pairing[clipped], -1),
        ],
        axis=1,
    ).reshape(-1)
    query_ids = [position, block_total - 1 - pairing[position]]
    begins_local = doc_start.reshape(2, length)
    query_blocks = query_local.reshape(2, length, query_local.shape[1])
    upstream_blocks = upstream_local.reshape(2, length, upstream_local.shape[1])

    def needed(query_id, key_id):
        listed = block_live[query_id, jnp.clip(key_id, 0, block_total - 1)] == 1
        return (key_id >= 0) & ((key_id == query_id) | (key_id < query_id) & listed)

    def masked_scores(slot_index, query_id, key_id, query_block, begins):
        packed = stacked[slot_index]
        scores = block_scores(query_block, packed, kv_count, group_size, factor)
        visible = visibility(query_id, key_id, begins, length)
        return (jnp.where(visible, scores, NEGATIVE), visible, packed)

    attended_blocks = []
    logsum_blocks = []
    for half_index in range(2):
        query_id = query_ids[half_index]
        query_block = query_blocks[half_index]
        begins = begins_local[half_index]

        def gather_stats(slot_index, loop_state):
            key_id = key_ids[slot_index]

            def include(running):
                row_peak, row_total = running
                masked, visible, packed = masked_scores(
                    slot_index, query_id, key_id, query_block, begins
                )
                new_peak = jnp.maximum(row_peak, jnp.max(masked, axis=-1))
                weights_now = jnp.where(visible, jnp.exp(masked - new_peak[..., None]), 0.0)
                return (
                    new_peak,
                    row_total * jnp.exp(row_peak - new_peak) + jnp.sum(weights_now, axis=-1),
                )

            return lax.cond(needed(query_id, key_id), include, lambda running: running, loop_state)

        stat_shape = (kv_count, group_size, length)
        row_peak, row_total = lax.fori_loop(
            0,
            2 * stretch_count,
            gather_stats,
            (jnp.full(stat_shape, NEGATIVE, jnp.float32), jnp.zeros(stat_shape, jnp.float32)),
        )
        logsum = row_peak + jnp.log(row_total)

        def gather_values(slot_index, loop_state):
            key_id = key_ids[slot_index]

            def include(running):
                masked, visible, packed = masked_scores(
                    slot_index, query_id, key_id, query_block, begins
                )
                weights = jnp.where(visible, jnp.exp(masked - logsum[..., None]), 0.0).astype(
                    jnp.bfloat16
                )
                values_block = packed[:, kv_width:].reshape(length, kv_count, HEAD_DIM)
                return running + jnp.einsum(
                    "grqk,kgd->qgrd", weights, values_block, preferred_element_type=jnp.float32
                )

            return lax.cond(needed(query_id, key_id), include, lambda running: running, loop_state)

        accumulated = lax.fori_loop(
            0,
            2 * stretch_count,
            gather_values,
            jnp.zeros((length, kv_count, group_size, HEAD_DIM), jnp.float32),
        )
        attended_blocks.append(accumulated.astype(jnp.bfloat16).reshape(length, -1))
        logsum_blocks.append(logsum)
    key_grads = jnp.zeros((2 * stretch_count, length, 2 * kv_width), jnp.float32)
    query_grads = []
    for half_index in range(2):
        query_id = query_ids[half_index]
        query_block = query_blocks[half_index]
        begins = begins_local[half_index]
        logsum = logsum_blocks[half_index]
        grouped = query_block.reshape(length, kv_count, group_size, HEAD_DIM)
        upstream = upstream_blocks[half_index].reshape(length, kv_count, group_size, HEAD_DIM)
        stored = attended_blocks[half_index].reshape(length, kv_count, group_size, HEAD_DIM)
        row_delta = jnp.einsum(
            "qgrd,qgrd->grq", upstream, stored, preferred_element_type=jnp.float32
        )

        def backward_step(slot_index, loop_state):
            key_id = key_ids[slot_index]

            def include(running):
                query_part, key_part = running
                masked, visible, packed = masked_scores(
                    slot_index, query_id, key_id, query_block, begins
                )
                probabilities = jnp.where(visible, jnp.exp(masked - logsum[..., None]), 0.0)
                weights = probabilities.astype(jnp.bfloat16)
                keys_block = packed[:, :kv_width].reshape(length, kv_count, HEAD_DIM)
                values_block = packed[:, kv_width:].reshape(length, kv_count, HEAD_DIM)
                dweights = jnp.einsum(
                    "qgrd,kgd->grqk", upstream, values_block, preferred_element_type=jnp.float32
                )
                dscores = (probabilities * (dweights - row_delta[..., None])).astype(jnp.bfloat16)
                query_part = (
                    query_part
                    + jnp.einsum(
                        "grqk,kgd->qgrd", dscores, keys_block, preferred_element_type=jnp.float32
                    )
                    * factor
                )
                key_new = (
                    jnp.einsum(
                        "grqk,qgrd->kgd", dscores, grouped, preferred_element_type=jnp.float32
                    )
                    * factor
                )
                value_new = jnp.einsum(
                    "grqk,qgrd->kgd", weights, upstream, preferred_element_type=jnp.float32
                )
                fresh_rows = jnp.concatenate(
                    [key_new.reshape(length, kv_width), value_new.reshape(length, kv_width)], axis=1
                )
                key_part = lax.dynamic_update_index_in_dim(
                    key_part, key_part[slot_index] + fresh_rows, slot_index, 0
                )
                return (query_part, key_part)

            return lax.cond(needed(query_id, key_id), include, lambda running: running, loop_state)

        query_part, key_grads = lax.fori_loop(
            0,
            2 * stretch_count,
            backward_step,
            (jnp.zeros((length, kv_count, group_size, HEAD_DIM), jnp.float32), key_grads),
        )
        query_grads.append(query_part.astype(jnp.bfloat16).reshape(length, -1))
    partials = key_grads.reshape(stretch_count, stretch_rows, 2 * kv_width)
    summed = partials[0]
    for slot_index in range(1, stretch_count):
        summed = summed + shifted(partials[slot_index], "ctx", offsets_list[slot_index])
    key_grad = summed[:, :kv_width].astype(jnp.bfloat16)
    value_grad = summed[:, kv_width:].astype(jnp.bfloat16)
    attended_all = jnp.concatenate(attended_blocks, axis=0)
    query_grad_all = jnp.concatenate(query_grads, axis=0)
    return (
        lax.all_to_all(attended_all, "head", split_axis=0, concat_axis=1, tiled=True),
        lax.all_to_all(query_grad_all, "head", split_axis=0, concat_axis=1, tiled=True),
        lax.all_to_all(key_grad, "head", split_axis=0, concat_axis=1, tiled=True),
        lax.all_to_all(value_grad, "head", split_axis=0, concat_axis=1, tiled=True),
    )


def solution(mesh):
    in_specs = (
        P(),
        P("ctx"),
        P(),
        P(("ctx", "head"), None),
        P(("ctx", "head"), None),
        P(("ctx", "head"), None),
        P(("ctx", "head"), None),
    )
    out_specs = (
        P(("ctx", "head"), None),
        P(("ctx", "head"), None),
        P(("ctx", "head"), None),
        P(("ctx", "head"), None),
    )
    return jax.shard_map(body, mesh=mesh, in_specs=in_specs, out_specs=out_specs, check_vma=False)
```

profile of v0, /device:TPU:125, one launch (start us, length us, event | category | flops | bytes accessed | tf_op | source)
XLA Modules:
  0.0 1173.4 jit_solution(11273660796477931225)
XLA Ops:
  2.1 6.5 all-to-all-start
  22.2 6.7 all-to-all-start.4
  37.0 13.7 %collective-permute-start.2 = (bf16[256,256]{1,0:T(8,128)(2,1)S(1)}, bf16[256,256]{1,0:T(8,128)(2,1)S(1)}, u32[]{:S(2)}, u32[]{:S(2)}) collective-permute-start(bf16[256,256]{1,0:T(8,128)(2,1)S(1)} %pad_maximum_fusion.2), channel_id=1, source_target_pairs={{24,0},{32,8},{40,16},{48,24},{56,32},{64,40},{72,48},{80,56},{88,... | collective-permute-start | bytes 393224 | tf_op jit(solution)/shard_map/ppermute | solution.py:18
  56.0 7.3 collective-permute-start.5
  63.3 6.8 collective-permute-start.6
  77.9 12.1 %collective-permute-start.10 = (bf16[256,256]{1,0:T(8,128)(2,1)S(1)}, bf16[256,256]{1,0:T(8,128)(2,1)S(1)}, u32[]{:S(2)}, u32[]{:S(2)}) collective-permute-start(bf16[256,256]{1,0:T(8,128)(2,1)S(1)} %pad_maximum_fusion.2), channel_id=1, source_target_pairs={{0,40},{8,48},{16,56},{24,64},{32,72},{40,80},{48,88},{56,96},{64,... | collective-permute-start | bytes 393224 | tf_op jit(solution)/shard_map/ppermute | solution.py:18
  90.1 7.1 collective-permute-start.11
  97.3 11.8 %all-to-all-start.2 = ((bf16[32,8,512]{2,0,1:T(8,128)(2,1)}), bf16[32,8,512]{2,0,1:T(8,128)(2,1)S(1)}, u32[]{:S(2)}, u32[]{:S(2)}) async-start(bf16[32,8,512]{2,0,1:T(8,128)(2,1)} %bitcast.420), calls=%async_computation.2 | async-start | bytes 524288 | tf_op jit(solution)/shard_map/all_to_all | solution.py:40
  109.3 6.9 all-to-all-done.2
  116.3 137.4 %while.104 = (s32[]{:T(128)}, f32[1,4,128]{2,1,0:T(4,128)S(1)}, f32[1,4,128]{2,1,0:T(4,128)S(1)}, s32[26]{0:T(128)S(1)}, s32[]{:T(128)}, /*index=5*/s32[128,128]...) while((s32[]{:T(128)}, f32[1,4,128]{2,1,0:T(4,128)S(1)}, ...), condition=%wide.region_5.6_spmd, body=%wide.region_0.5_spmd.sunk | while | flops 17220880 | bytes 1160085 | solution.py:115
  253.7 137.6 %while.105 = (s32[]{:T(128)}, f32[128,1,4,128]{0,3,2,1:T(8,128)S(1)}, s32[26]{0:T(128)S(1)}, s32[]{:T(128)}, s32[128,128]{1,0:T(8,128)}, /*index=5*/s32[]{:T(128...) while((s32[]{:T(128)}, ...), condition=%wide.region_9.10_spmd, body=%wide.region_6.9_spmd.sunk | while | flops 33997072 | bytes 1151861 | solution.py:140
  394.3 144.4 %while.108 = (s32[]{:T(128)}, f32[128,1,4,128]{0,3,2,1:T(8,128)S(1)}, f32[26,128,256]{1,2,0:T(8,128)}, s32[26]{0:T(128)S(1)}, s32[]{:T(128)}, /*index=5*/s32[128...) while((s32[]{:T(128)}, ...), condition=%wide.region_23.24_spmd, body=%wide.region_20.23_spmd.sunk | while | flops 84672776 | bytes 3283929 | solution.py:204
  538.8 138.6 %while.106 = (s32[]{:T(128)}, f32[1,4,128]{2,1,0:T(4,128)S(1)}, f32[1,4,128]{2,1,0:T(4,128)S(1)}, s32[26]{0:T(128)S(1)}, s32[]{:T(128)}, /*index=5*/s32[128,128]...) while((s32[]{:T(128)}, f32[1,4,128]{2,1,0:T(4,128)S(1)}, ...), condition=%wide.region_15.16_spmd, body=%wide.region_10.15_spmd.sunk | while | flops 17220880 | bytes 1160085 | solution.py:115
  677.4 138.8 %while.107 = (s32[]{:T(128)}, f32[128,1,4,128]{0,3,2,1:T(8,128)S(1)}, s32[26]{0:T(128)S(1)}, s32[]{:T(128)}, s32[128,128]{1,0:T(8,128)}, /*index=5*/s32[]{:T(128...) while((s32[]{:T(128)}, ...), condition=%wide.region_19.20_spmd, body=%wide.region_16.19_spmd.sunk | while | flops 33997072 | bytes 1151861 | solution.py:140
  817.0 147.9 %while.109 = (s32[]{:T(128)}, f32[128,1,4,128]{0,3,2,1:T(8,128)S(1)}, f32[26,128,256]{1,2,0:T(8,128)}, s32[26]{0:T(128)S(1)}, s32[]{:T(128)}, /*index=5*/s32[128...) while((s32[]{:T(128)}, ...), condition=%wide.region_27.28_spmd, body=%wide.region_24.27_spmd.sunk | while | flops 84672776 | bytes 3283929 | solution.py:204
  972.0 13.0 %collective-permute-start.12 = (f32[256,256]{1,0:T(8,128)S(1)}, f32[256,256]{1,0:T(8,128)S(1)}, u32[]{:S(2)}, u32[]{:S(2)}) collective-permute-start(f32[256,256]{1,0:T(8,128)S(1)} %bitcast.477), channel_id=1, source_target_pairs={{0,8},{8,16},{16,24},{24,32},{32,40},{40,48},{48,56},{56,64},{64,7... | collective-permute-start | bytes 786440 | tf_op jit(solution)/shard_map/ppermute | solution.py:18
  987.0 14.7 %collective-permute-start.14 = (f32[256,256]{1,0:T(8,128)S(1)}, f32[256,256]{1,0:T(8,128)S(1)}, u32[]{:S(2)}, u32[]{:S(2)}) collective-permute-start(f32[256,256]{1,0:T(8,128)S(1)} %bitcast.475), channel_id=1, source_target_pairs={{0,24},{8,32},{16,40},{24,48},{32,56},{40,64},{48,72},{56,80},{64,... | collective-permute-start | bytes 786440 | tf_op jit(solution)/shard_map/ppermute | solution.py:18
  1017.6 15.5 %collective-permute-done.15 = f32[256,256]{1,0:T(8,128)S(1)} collective-permute-done((f32[256,256]{1,0:T(8,128)S(1)}, f32[256,256]{1,0:T(8,128)S(1)}, u32[]{:S(2)}, u32[]{:S(2)}) %collective-permute-start.15) | collective-permute-done | bytes 262176 | tf_op jit(solution)/shard_map/ppermute | solution.py:18
  1033.1 25.4 %collective-permute-start.20 = (f32[256,256]{1,0:T(8,128)S(1)}, f32[256,256]{1,0:T(8,128)S(1)}, u32[]{:S(2)}, u32[]{:S(2)}) collective-permute-start(f32[256,256]{1,0:T(8,128)S(1)} %bitcast.469), channel_id=1, source_target_pairs={{24,0},{32,8},{40,16},{48,24},{56,32},{64,40},{72,48},{80,56},{88,... | collective-permute-start | bytes 786440 | tf_op jit(solution)/shard_map/ppermute | solution.py:18
  1060.5 10.7 collective-permute-start.22
  1073.2 40.0 %collective-permute-done.21 = f32[256,256]{1,0:T(8,128)S(1)} collective-permute-done((f32[256,256]{1,0:T(8,128)S(1)}, f32[256,256]{1,0:T(8,128)S(1)}, u32[]{:S(2)}, u32[]{:S(2)}) %collective-permute-start.21) | collective-permute-done | bytes 262176 | tf_op jit(solution)/shard_map/ppermute | solution.py:18
  1113.2 14.7 %collective-permute-done.23 = f32[256,256]{1,0:T(8,128)S(1)} collective-permute-done((f32[256,256]{1,0:T(8,128)S(1)}, f32[256,256]{1,0:T(8,128)S(1)}, u32[]{:S(2)}, u32[]{:S(2)}) %collective-permute-start.23) | collective-permute-done | bytes 262176 | tf_op jit(solution)/shard_map/ppermute | solution.py:18
  1136.6 6.6 all-to-all-start.6
  1145.8 6.7 all-to-all-start.5
  (762 shorter events, 458.7 us)
Async XLA Ops:
  22.2 75.1 %all-to-all-start.4 = ((bf16[32,8,512]{2,0,1:T(8,128)(2,1)}), bf16[32,8,512]{2,0,1:T(8,128)(2,1)S(1)}, u32[]{:S(2)}, u32[]{:S(2)}) async-start(bf16[32,8,512]{2,0,1:T(8,128)(2,1)} %bitcast.419), calls=%async_computation.4 | async-start | bytes 524288 | tf_op jit(solution)/shard_map/all_to_all | solution.py:43
  28.9 27.0 %collective-permute-start = (bf16[256,256]{1,0:T(8,128)(2,1)S(1)}, bf16[256,256]{1,0:T(8,128)(2,1)S(1)}, u32[]{:S(2)}, u32[]{:S(2)}) collective-permute-start(bf16[256,256]{1,0:T(8,128)(2,1)S(1)} %pad_maximum_fusion.2), channel_id=1, source_target_pairs={{8,0},{16,8},{24,16},{32,24},{40,32},{48,40},{56,48},{64,56},{72,6... | collective-permute-start | bytes 393224 | tf_op jit(solution)/shard_map/ppermute | solution.py:18
  35.1 28.2 %collective-permute-start.1 = (bf16[256,256]{1,0:T(8,128)(2,1)S(1)}, bf16[256,256]{1,0:T(8,128)(2,1)S(1)}, u32[]{:S(2)}, u32[]{:S(2)}) collective-permute-start(bf16[256,256]{1,0:T(8,128)(2,1)S(1)} %pad_maximum_fusion.2), channel_id=1, source_target_pairs={{16,0},{24,8},{32,16},{40,24},{48,32},{56,40},{64,48},{72,56},{80,... | collective-permute-start | bytes 393224 | tf_op jit(solution)/shard_map/ppermute | solution.py:18
  37.0 33.1 %collective-permute-start.2 = (bf16[256,256]{1,0:T(8,128)(2,1)S(1)}, bf16[256,256]{1,0:T(8,128)(2,1)S(1)}, u32[]{:S(2)}, u32[]{:S(2)}) collective-permute-start(bf16[256,256]{1,0:T(8,128)(2,1)S(1)} %pad_maximum_fusion.2), channel_id=1, source_target_pairs={{24,0},{32,8},{40,16},{48,24},{56,32},{64,40},{72,48},{80,56},{88,... | collective-permute-start | bytes 393224 | tf_op jit(solution)/shard_map/ppermute | solution.py:18
  50.7 21.3 %collective-permute-start.3 = (bf16[256,256]{1,0:T(8,128)(2,1)S(1)}, bf16[256,256]{1,0:T(8,128)(2,1)S(1)}, u32[]{:S(2)}, u32[]{:S(2)}) collective-permute-start(bf16[256,256]{1,0:T(8,128)(2,1)S(1)} %pad_maximum_fusion.2), channel_id=1, source_target_pairs={{32,0},{40,8},{48,16},{56,24},{64,32},{72,40},{80,48},{88,56},{96,... | collective-permute-start | bytes 393224 | tf_op jit(solution)/shard_map/ppermute | solution.py:18
  52.9 21.1 %collective-permute-start.4 = (bf16[256,256]{1,0:T(8,128)(2,1)S(1)}, bf16[256,256]{1,0:T(8,128)(2,1)S(1)}, u32[]{:S(2)}, u32[]{:S(2)}) collective-permute-start(bf16[256,256]{1,0:T(8,128)(2,1)S(1)} %pad_maximum_fusion.2), channel_id=1, source_target_pairs={{40,0},{48,8},{56,16},{64,24},{72,32},{80,40},{88,48},{96,56},{104... | collective-permute-start | bytes 393224 | tf_op jit(solution)/shard_map/ppermute | solution.py:18
  56.0 21.9 %collective-permute-start.5 = (bf16[256,256]{1,0:T(8,128)(2,1)S(1)}, bf16[256,256]{1,0:T(8,128)(2,1)S(1)}, u32[]{:S(2)}, u32[]{:S(2)}) collective-permute-start(bf16[256,256]{1,0:T(8,128)(2,1)S(1)} %pad_maximum_fusion.2), channel_id=1, source_target_pairs={{48,0},{56,8},{64,16},{72,24},{80,32},{88,40},{96,48},{104,56},{11... | collective-permute-start | bytes 393224 | tf_op jit(solution)/shard_map/ppermute | solution.py:18
  63.3 26.8 %collective-permute-start.6 = (bf16[256,256]{1,0:T(8,128)(2,1)S(1)}, bf16[256,256]{1,0:T(8,128)(2,1)S(1)}, u32[]{:S(2)}, u32[]{:S(2)}) collective-permute-start(bf16[256,256]{1,0:T(8,128)(2,1)S(1)} %pad_maximum_fusion.2), channel_id=1, source_target_pairs={{0,8},{8,16},{16,24},{24,32},{32,40},{40,48},{48,56},{56,64},{64,7... | collective-permute-start | bytes 393224 | tf_op jit(solution)/shard_map/ppermute | solution.py:18
  70.1 27.1 %collective-permute-start.7 = (bf16[256,256]{1,0:T(8,128)(2,1)S(1)}, bf16[256,256]{1,0:T(8,128)(2,1)S(1)}, u32[]{:S(2)}, u32[]{:S(2)}) collective-permute-start(bf16[256,256]{1,0:T(8,128)(2,1)S(1)} %pad_maximum_fusion.2), channel_id=1, source_target_pairs={{0,16},{8,24},{16,32},{24,40},{32,48},{40,56},{48,64},{56,72},{64,... | collective-permute-start | bytes 393224 | tf_op jit(solution)/shard_map/ppermute | solution.py:18
  72.0 25.2 %collective-permute-start.8 = (bf16[256,256]{1,0:T(8,128)(2,1)S(1)}, bf16[256,256]{1,0:T(8,128)(2,1)S(1)}, u32[]{:S(2)}, u32[]{:S(2)}) collective-permute-start(bf16[256,256]{1,0:T(8,128)(2,1)S(1)} %pad_maximum_fusion.2), channel_id=1, source_target_pairs={{0,24},{8,32},{16,40},{24,48},{32,56},{40,64},{48,72},{56,80},{64,... | collective-permute-start | bytes 393224 | tf_op jit(solution)/shard_map/ppermute | solution.py:18
  74.0 23.2 %collective-permute-start.9 = (bf16[256,256]{1,0:T(8,128)(2,1)S(1)}, bf16[256,256]{1,0:T(8,128)(2,1)S(1)}, u32[]{:S(2)}, u32[]{:S(2)}) collective-permute-start(bf16[256,256]{1,0:T(8,128)(2,1)S(1)} %pad_maximum_fusion.2), channel_id=1, source_target_pairs={{0,32},{8,40},{16,48},{24,56},{32,64},{40,72},{48,80},{56,88},{64,... | collective-permute-start | bytes 393224 | tf_op jit(solution)/shard_map/ppermute | solution.py:18
  77.9 19.4 %collective-permute-start.10 = (bf16[256,256]{1,0:T(8,128)(2,1)S(1)}, bf16[256,256]{1,0:T(8,128)(2,1)S(1)}, u32[]{:S(2)}, u32[]{:S(2)}) collective-permute-start(bf16[256,256]{1,0:T(8,128)(2,1)S(1)} %pad_maximum_fusion.2), channel_id=1, source_target_pairs={{0,40},{8,48},{16,56},{24,64},{32,72},{40,80},{48,88},{56,96},{64,... | collective-permute-start | bytes 393224 | tf_op jit(solution)/shard_map/ppermute | solution.py:18
  972.0 33.5 %collective-permute-start.12 = (f32[256,256]{1,0:T(8,128)S(1)}, f32[256,256]{1,0:T(8,128)S(1)}, u32[]{:S(2)}, u32[]{:S(2)}) collective-permute-start(f32[256,256]{1,0:T(8,128)S(1)} %bitcast.477), channel_id=1, source_target_pairs={{0,8},{8,16},{16,24},{24,32},{32,40},{40,48},{48,56},{56,64},{64,7... | collective-permute-start | bytes 786440 | tf_op jit(solution)/shard_map/ppermute | solution.py:18
  985.1 22.5 %collective-permute-start.13 = (f32[256,256]{1,0:T(8,128)S(1)}, f32[256,256]{1,0:T(8,128)S(1)}, u32[]{:S(2)}, u32[]{:S(2)}) collective-permute-start(f32[256,256]{1,0:T(8,128)S(1)} %bitcast.476), channel_id=1, source_target_pairs={{0,16},{8,24},{16,32},{24,40},{32,48},{40,56},{48,64},{56,72},{64,... | collective-permute-start | bytes 786440 | tf_op jit(solution)/shard_map/ppermute | solution.py:18
  987.0 26.3 %collective-permute-start.14 = (f32[256,256]{1,0:T(8,128)S(1)}, f32[256,256]{1,0:T(8,128)S(1)}, u32[]{:S(2)}, u32[]{:S(2)}) collective-permute-start(f32[256,256]{1,0:T(8,128)S(1)} %bitcast.475), channel_id=1, source_target_pairs={{0,24},{8,32},{16,40},{24,48},{32,56},{40,64},{48,72},{56,80},{64,... | collective-permute-start | bytes 786440 | tf_op jit(solution)/shard_map/ppermute | solution.py:18
  1001.7 31.4 %collective-permute-start.15 = (f32[256,256]{1,0:T(8,128)S(1)}, f32[256,256]{1,0:T(8,128)S(1)}, u32[]{:S(2)}, u32[]{:S(2)}) collective-permute-start(f32[256,256]{1,0:T(8,128)S(1)} %bitcast.474), channel_id=1, source_target_pairs={{0,32},{8,40},{16,48},{24,56},{32,64},{40,72},{48,80},{56,88},{64,... | collective-permute-start | bytes 786440 | tf_op jit(solution)/shard_map/ppermute | solution.py:18
  1003.6 54.9 %collective-permute-start.16 = (f32[256,256]{1,0:T(8,128)S(1)}, f32[256,256]{1,0:T(8,128)S(1)}, u32[]{:S(2)}, u32[]{:S(2)}) collective-permute-start(f32[256,256]{1,0:T(8,128)S(1)} %bitcast.473), channel_id=1, source_target_pairs={{0,40},{8,48},{16,56},{24,64},{32,72},{40,80},{48,88},{56,96},{64,... | collective-permute-start | bytes 786440 | tf_op jit(solution)/shard_map/ppermute | solution.py:18
  1005.6 54.9 %collective-permute-start.17 = (f32[256,256]{1,0:T(8,128)S(1)}, f32[256,256]{1,0:T(8,128)S(1)}, u32[]{:S(2)}, u32[]{:S(2)}) collective-permute-start(f32[256,256]{1,0:T(8,128)S(1)} %bitcast.472), channel_id=1, source_target_pairs={{0,48},{8,56},{16,64},{24,72},{32,80},{40,88},{48,96},{56,104},{64... | collective-permute-start | bytes 786440 | tf_op jit(solution)/shard_map/ppermute | solution.py:18
  1007.6 63.7 %collective-permute-start.18 = (f32[256,256]{1,0:T(8,128)S(1)}, f32[256,256]{1,0:T(8,128)S(1)}, u32[]{:S(2)}, u32[]{:S(2)}) collective-permute-start(f32[256,256]{1,0:T(8,128)S(1)} %bitcast.471), channel_id=1, source_target_pairs={{8,0},{16,8},{24,16},{32,24},{40,32},{48,40},{56,48},{64,56},{72,6... | collective-permute-start | bytes 786440 | tf_op jit(solution)/shard_map/ppermute | solution.py:18
  1013.3 59.9 %collective-permute-start.19 = (f32[256,256]{1,0:T(8,128)S(1)}, f32[256,256]{1,0:T(8,128)S(1)}, u32[]{:S(2)}, u32[]{:S(2)}) collective-permute-start(f32[256,256]{1,0:T(8,128)S(1)} %bitcast.470), channel_id=1, source_target_pairs={{16,0},{24,8},{32,16},{40,24},{48,32},{56,40},{64,48},{72,56},{80,... | collective-permute-start | bytes 786440 | tf_op jit(solution)/shard_map/ppermute | solution.py:18
  1033.1 40.1 %collective-permute-start.20 = (f32[256,256]{1,0:T(8,128)S(1)}, f32[256,256]{1,0:T(8,128)S(1)}, u32[]{:S(2)}, u32[]{:S(2)}) collective-permute-start(f32[256,256]{1,0:T(8,128)S(1)} %bitcast.469), channel_id=1, source_target_pairs={{24,0},{32,8},{40,16},{48,24},{56,32},{64,40},{72,48},{80,56},{88,... | collective-permute-start | bytes 786440 | tf_op jit(solution)/shard_map/ppermute | solution.py:18
  1058.5 54.6 %collective-permute-start.21 = (f32[256,256]{1,0:T(8,128)S(1)}, f32[256,256]{1,0:T(8,128)S(1)}, u32[]{:S(2)}, u32[]{:S(2)}) collective-permute-start(f32[256,256]{1,0:T(8,128)S(1)} %bitcast.468), channel_id=1, source_target_pairs={{32,0},{40,8},{48,16},{56,24},{64,32},{72,40},{80,48},{88,56},{96,... | collective-permute-start | bytes 786440 | tf_op jit(solution)/shard_map/ppermute | solution.py:18
  1060.5 52.7 %collective-permute-start.22 = (f32[256,256]{1,0:T(8,128)S(1)}, f32[256,256]{1,0:T(8,128)S(1)}, u32[]{:S(2)}, u32[]{:S(2)}) collective-permute-start(f32[256,256]{1,0:T(8,128)S(1)} %bitcast.467), channel_id=1, source_target_pairs={{40,0},{48,8},{56,16},{64,24},{72,32},{80,40},{88,48},{96,56},{104... | collective-permute-start | bytes 786440 | tf_op jit(solution)/shard_map/ppermute | solution.py:18
  1071.2 56.7 %collective-permute-start.23 = (f32[256,256]{1,0:T(8,128)S(1)}, f32[256,256]{1,0:T(8,128)S(1)}, u32[]{:S(2)}, u32[]{:S(2)}) collective-permute-start(f32[256,256]{1,0:T(8,128)S(1)} %bitcast.466), channel_id=1, source_target_pairs={{48,0},{56,8},{64,16},{72,24},{80,32},{88,40},{96,48},{104,56},{11... | collective-permute-start | bytes 786440 | tf_op jit(solution)/shard_map/ppermute | solution.py:18
  (11 other events, 167.1 us)
where the time goes:
time: 1190 us; the launch traced here: 1170 us
  loops' own time  528 us (44%)
  local copies, waits for them, and re-layouts  315 us (26%)
  starting transfers between devices  202 us (17%)
  waiting for transfers between devices  97.9 us (8%)
  other arithmetic  17.2 us (1%)
    dynamic_slice x156, local copies, waits for them, and re-layouts, needed(): listed = block_live[query_id, jnp.clip(key_id, 0, block_total - 1)] == 1  199 us
    another operation x2, loops' own time, body(): lax.fori_loop(0, 2 * stretch_count, backward_step, (jnp.zeros((length, kv...  171 us
    another operation x2, loops' own time, body(): lax.fori_loop(0, 2 * stretch_count, gather_stats, (jnp.full(stat_shape, N...  171 us
    another operation x2, loops' own time, body(): lax.fori_loop(0, 2 * stretch_count, gather_values, jnp.zeros((length, kv_...  171 us
    ppermute x24, starting transfers between devices, shifted(): return lax.ppermute(value, axis, pairs)  147 us
    ppermute x24, waiting for transfers between devices, shifted(): return lax.ppermute(value, axis, pairs)  73.9 us
    dynamic_slice x52, local copies, waits for them, and re-layouts, gather_stats(): key_id = key_ids[slot_index]  30.5 us
    dynamic_slice x52, local copies, waits for them, and re-layouts, gather_values(): key_id = key_ids[slot_index]  30.5 us
  transfers between devices with their start and end apart: 32, of which 10 were waited for; matrix products, arithmetic and copies ran while one was open for 1% of the time, Pallas kernels for 0%

commit v1 on v0

v1 whole, which is shorter than its diff:
```python
import functools
import math

import jax
import jax.numpy as jnp
from jax import lax
from jax.experimental import pallas as pl
from jax.experimental.pallas import tpu as pltpu
from jax.sharding import Mesh
from jax.sharding import PartitionSpec as P

DIM = 128
BLOCK = 128
REACH = 4
WINDOW = REACH + 1
GROUP = 4
PARTS = 8
ROWS = 2 * BLOCK
PIECE = ROWS // PARTS
SLOTS = 8
NEGATIVE = -1e30
QUERY_WIDE = GROUP * DIM
KEY_AT = 2 * QUERY_WIDE
WIDE = KEY_AT + 2 * DIM
SENT = WIDE + DIM


def dot(a, b, over_a, over_b):
    return lax.dot_general(
        a, b, (((over_a,), (over_b,)), ((), ())), preferred_element_type=jnp.float32
    )


def pieces(whole, split, at, wide):
    return [
        (whole.at[:, pl.ds(h * wide, wide)], split.at[h, :, pl.ds(at, wide)]) for h in range(PARTS)
    ]


def places(q, g, k, v, split):
    return (
        pieces(q, split, 0, QUERY_WIDE)
        + pieces(g, split, QUERY_WIDE, QUERY_WIDE)
        + pieces(k, split, KEY_AT, DIM)
        + pieces(v, split, KEY_AT + DIM, DIM)
    )


def pack_kernel(doc_ref, q_ref, g_ref, k_ref, v_ref, out_ref, doc_here, sems, doc_sem):
    doc_copy = pltpu.make_async_copy(doc_ref, doc_here, doc_sem)
    doc_copy.start()
    copies = [
        pltpu.make_async_copy(rows, split, sems.at[i])
        for i, (rows, split) in enumerate(places(q_ref, g_ref, k_ref, v_ref, out_ref))
    ]
    for copy in copies:
        copy.start()
    doc_copy.wait()
    doc = doc_here[...]
    line = lax.broadcasted_iota(jnp.int32, (PIECE, BLOCK), 0)
    first, second = doc[:, :BLOCK], doc[:, BLOCK:]
    coded = jnp.where(line < 2, first, second)
    coded = jnp.where(line % 2 == 0, coded // BLOCK, coded % BLOCK)
    coded = coded.astype(jnp.float32).astype(jnp.bfloat16)
    for h in range(PARTS):
        out_ref[h, :, WIDE:] = coded
    for copy in copies:
        copy.wait()


def pack(doc, query, grad_out, key, value):
    vmem = pl.BlockSpec(memory_space=pltpu.VMEM)
    hbm = pl.BlockSpec(memory_space=pltpu.HBM)
    return pl.pallas_call(
        pack_kernel,
        out_shape=jax.ShapeDtypeStruct((PARTS, PIECE, SENT), jnp.bfloat16),
        in_specs=[hbm] * 5,
        out_specs=vmem,
        scratch_shapes=[
            pltpu.VMEM((1, ROWS), jnp.int32),
            pltpu.SemaphoreType.DMA((4 * PARTS,)),
            pltpu.SemaphoreType.DMA,
        ],
        compiler_params=pltpu.CompilerParams(vmem_limit_bytes=(63 * 1024 + 256) * 1024),
        name="pack",
    )(doc, query, grad_out, key, value)


def unpack_kernel(split_ref, att_ref, dq_ref, dk_ref, dv_ref, sems):
    copies = [
        pltpu.make_async_copy(split, rows, sems.at[i])
        for i, (rows, split) in enumerate(places(att_ref, dq_ref, dk_ref, dv_ref, split_ref))
    ]
    for copy in copies:
        copy.start()
    for copy in copies:
        copy.wait()


def unpack(split):
    hbm = pl.BlockSpec(memory_space=pltpu.HBM)
    wide = jax.ShapeDtypeStruct((PIECE, PARTS * QUERY_WIDE), jnp.bfloat16)
    narrow = jax.ShapeDtypeStruct((PIECE, PARTS * DIM), jnp.bfloat16)
    return pl.pallas_call(
        unpack_kernel,
        out_shape=(wide, wide, narrow, narrow),
        in_specs=[pl.BlockSpec(memory_space=pl.ANY)],
        out_specs=(hbm,) * 4,
        scratch_shapes=[pltpu.SemaphoreType.DMA((4 * PARTS,))],
        compiler_params=pltpu.CompilerParams(vmem_limit_bytes=16 * 1024 * 1024),
        name="unpack",
    )(split)


def gather_kernel(
    place_ref, pairing_ref, od_ref, own_ref, one_ref, two_ref, three_ref, back_ref, out_ref
):
    pair = place_ref[0]
    later = (place_ref[2] == 0) | (pairing_ref[2 * pair + 1] < pairing_ref[2 * pair])
    out_ref[:, :KEY_AT] = od_ref[...]
    total = own_ref[...] + one_ref[...].astype(jnp.float32) + two_ref[...].astype(jnp.float32)
    three = three_ref[...].astype(jnp.float32)
    lower = total[:BLOCK] + jnp.where(later, 0.0, three)
    upper = total[BLOCK:] + jnp.where(later, three, 0.0) + back_ref[...].astype(jnp.float32)
    out_ref[:BLOCK, KEY_AT:] = lower.astype(jnp.bfloat16)
    out_ref[BLOCK:, KEY_AT:] = upper.astype(jnp.bfloat16)


def gather(place, pairing, od, parts):
    vmem = pl.BlockSpec(memory_space=pltpu.VMEM)
    smem = pl.BlockSpec(memory_space=pltpu.SMEM)
    return pl.pallas_call(
        gather_kernel,
        out_shape=jax.ShapeDtypeStruct((ROWS, WIDE), jnp.bfloat16),
        in_specs=[smem, smem] + [vmem] * 6,
        out_specs=vmem,
        compiler_params=pltpu.CompilerParams(vmem_limit_bytes=16 * 1024 * 1024),
        name="gather",
    )(place, pairing, od, *parts)


def attention_kernel(
    chain,
    place_ref,
    pairing_ref,
    live_ref,
    qg_ref,
    one_ref,
    two_ref,
    three_ref,
    back_ref,
    od_ref,
    own_out,
    one_out,
    two_out,
    three_out,
    back_out,
    kv,
    acc,
):
    pair = place_ref[0]
    half = place_ref[2]
    blocks = 2 * chain
    ctx = chain
    scale = 1.0 / math.sqrt(DIM)
    my_place = jnp.where(half == 0, pair, chain - 1 - pair)

    kv[0:256, :] = qg_ref[:, KEY_AT:WIDE]
    kv[256:512, :] = one_ref[...]
    kv[512:768, :] = two_ref[...]
    kv[768:896, :] = three_ref[...]
    kv[896:1024, :] = back_ref[...]
    acc[...] = jnp.zeros_like(acc)

    keys_down = lax.broadcasted_iota(jnp.int32, (BLOCK, BLOCK), 0)
    rows_along = lax.broadcasted_iota(jnp.int32, (BLOCK, BLOCK), 1)
    lanes = lax.broadcasted_iota(jnp.int32, (1, blocks), 1)

    for b in range(2):
        holder = 2 * pair + b
        block = jnp.where(half == 0, holder, blocks - 1 - pairing_ref[holder])
        doc = qg_ref[b * BLOCK : b * BLOCK + PIECE, WIDE:].astype(jnp.float32)
        doc = jnp.where(half == 0, doc[0:2], doc[2:4])
        begins = (doc[0:1] * BLOCK + doc[1:2]).astype(jnp.int32)
        live_row = live_ref[pl.ds(block, 1), :]
        slots = []
        bias = []
        for w in range(WINDOW):
            key_block = block - w
            mirrored = pairing_ref[jnp.clip(blocks - 1 - key_block, 0, ctx - 1)]
            held_by = jnp.where(key_block < ctx, key_block, mirrored)
            where_held = jnp.where(key_block < ctx, held_by // 2, chain - 1 - held_by // 2)
            away = my_place - where_held
            slot = jnp.where(away == 3, 6, jnp.where(away == -1, 7, 2 * away + held_by % 2))
            slot = jnp.where(key_block >= 0, jnp.clip(slot, 0, SLOTS - 1), 0)
            slots.append(pl.multiple_of(slot * BLOCK, BLOCK))
            reach = begins - key_block * BLOCK
            if w == 0:
                seen = (keys_down >= reach) & (keys_down <= rows_along)
            else:
                listed = jnp.max(
                    jnp.where(lanes == key_block, live_row, 0), axis=1, keepdims=True
                )
                seen = keys_down >= jnp.where(listed == 1, reach, BLOCK)
            bias.append(jnp.where(seen, 0.0, NEGATIVE))
        bias = jnp.concatenate(bias, axis=0)
        bias = jnp.concatenate([bias, bias], axis=1)
        keys = jnp.concatenate([kv[pl.ds(s, BLOCK), :DIM] for s in slots], axis=0)
        values = jnp.concatenate([kv[pl.ds(s, BLOCK), DIM:] for s in slots], axis=0)
        rows = slice(b * BLOCK, (b + 1) * BLOCK)
        key_grad = None
        value_grad = None
        for h in range(0, GROUP, 2):
            first, second = h * DIM, (h + 1) * DIM
            shift = GROUP * DIM
            q = jnp.concatenate(
                [qg_ref[rows, first : first + DIM], qg_ref[rows, second : second + DIM]], axis=0
            )
            g = jnp.concatenate(
                [
                    qg_ref[rows, shift + first : shift + first + DIM],
                    qg_ref[rows, shift + second : shift + second + DIM],
                ],
                axis=0,
            )
            scores = dot(keys, q, 1, 1) + bias
            peak = jnp.max(scores, axis=0, keepdims=True)
            p = jnp.exp2((scores - peak) * (scale * math.log2(math.e)))
            p = p * (1.0 / jnp.sum(p, axis=0, keepdims=True))
            weights = p.astype(jnp.bfloat16)
            out = dot(values, weights, 0, 0)
            g_turned = g.astype(jnp.float32).T
            delta = jnp.sum(
                g_turned * out.astype(jnp.bfloat16).astype(jnp.float32), axis=0, keepdims=True
            )
            dweights = dot(values, g, 1, 1)
            dscores = (p * (dweights - delta)).astype(jnp.bfloat16)
            dq = dot(keys, dscores, 0, 0) * scale
            key_new = dot(dscores, q, 1, 0)
            value_new = dot(weights, g, 1, 0)
            key_grad = key_new if key_grad is None else key_grad + key_new
            value_grad = value_new if value_grad is None else value_grad + value_new
            out = out.T.astype(jnp.bfloat16)
            dq = dq.T.astype(jnp.bfloat16)
            od_ref[rows, first : first + DIM] = out[:BLOCK]
            od_ref[rows, second : second + DIM] = out[BLOCK:]
            od_ref[rows, shift + first : shift + first + DIM] = dq[:BLOCK]
            od_ref[rows, shift + second : shift + second + DIM] = dq[BLOCK:]
        key_grad = key_grad * scale
        for w, s in enumerate(slots):
            part = slice(w * BLOCK, (w + 1) * BLOCK)
            acc[pl.ds(s, BLOCK), :DIM] += key_grad[part]
            acc[pl.ds(s, BLOCK), DIM:] += value_grad[part]

    own_out[...] = acc[0:256, :]
    one_out[...] = acc[256:512, :].astype(jnp.bfloat16)
    two_out[...] = acc[512:768, :].astype(jnp.bfloat16)
    three_out[...] = acc[768:896, :].astype(jnp.bfloat16)
    back_out[...] = acc[896:1024, :].astype(jnp.bfloat16)


def attention(chain, place, pairing, live, qg, halo):
    wide = 2 * DIM
    vmem = pl.BlockSpec(memory_space=pltpu.VMEM)
    smem = pl.BlockSpec(memory_space=pltpu.SMEM)
    return pl.pallas_call(
        functools.partial(attention_kernel, chain),
        out_shape=(
            jax.ShapeDtypeStruct((ROWS, 2 * GROUP * DIM), jnp.bfloat16),
            jax.ShapeDtypeStruct((ROWS, wide), jnp.float32),
            jax.ShapeDtypeStruct((ROWS, wide), jnp.bfloat16),
            jax.ShapeDtypeStruct((ROWS, wide), jnp.bfloat16),
            jax.ShapeDtypeStruct((BLOCK, wide), jnp.bfloat16),
            jax.ShapeDtypeStruct((BLOCK, wide), jnp.bfloat16),
        ),
        in_specs=[smem, smem] + [vmem] * 6,
        out_specs=(vmem,) * 6,
        scratch_shapes=[
            pltpu.VMEM((SLOTS * BLOCK, wide), jnp.bfloat16),
            pltpu.VMEM((SLOTS * BLOCK, wide), jnp.float32),
        ],
        compiler_params=pltpu.CompilerParams(vmem_limit_bytes=32 * 1024 * 1024),
        cost_estimate=pl.CostEstimate(
            flops=2 * 5 * 2 * WINDOW * GROUP * BLOCK * BLOCK * DIM,
            bytes_accessed=3 * 1024 * 1024,
            transcendentals=2 * WINDOW * GROUP * BLOCK * BLOCK,
        ),
        name="attention",
    )(place, pairing, live, qg, *halo)


def body(pairing, doc_start, block_live, query, key, value, grad_out):
    pairs = lax.axis_size("pair")
    chain = 2 * pairs
    blocks = 2 * chain
    pair = lax.axis_index("pair")
    side = lax.axis_index("side")
    half = lax.axis_index("half")

    def linear(place):
        return place * 2 if place < pairs else (chain - 1 - place) * 2 + 1

    def steps(by, first_target):
        return [
            (linear(s - by), linear(s)) for s in range(first_target, chain) if 0 <= s - by < chain
        ]

    forth = [steps(1, 0), steps(2, 0), steps(3, pairs), steps(-1, pairs)]
    back = [[(b, a) for a, b in pairs_of] for pairs_of in forth]

    def move(x, pairs_of):
        return lax.ppermute(x, ("pair", "half"), pairs_of)

    def exchange(x):
        return lax.all_to_all(x, ("side", "lane"), split_axis=0, concat_axis=0, tiled=True)

    split = pack(doc_start.reshape(1, ROWS), query, grad_out, key, value)
    arrived = exchange(split).reshape(ROWS, SENT)
    own = arrived[:, KEY_AT:WIDE]
    later = (half == 0) | (pairing[2 * pair + 1] < pairing[2 * pair])
    halo = (
        move(own, forth[0]),
        move(own, forth[1]),
        move(jnp.where(later, own[BLOCK:], own[:BLOCK]), forth[2]),
        move(own[BLOCK:], forth[3]),
    )
    place = jnp.stack([pair, side, half]).astype(jnp.int32)
    od, own_grad, *partials = attention(chain, place, pairing, block_live, arrived, halo)
    partials = [move(part, pairs_of) for part, pairs_of in zip(partials, back)]
    total = gather(place, pairing, od, (own_grad, *partials))
    return unpack(exchange(total.reshape(PARTS, PIECE, WIDE)))


def solution(mesh):
    ctx, head = mesh.devices.shape
    fine = Mesh(mesh.devices.reshape(ctx // 2, 2, 2, head // 2), ("pair", "side", "half", "lane"))
    tokens = P(("pair", "side", "half", "lane"), None)
    return jax.shard_map(
        body,
        mesh=fine,
        in_specs=(P(), P(("pair", "side")), P(), tokens, tokens, tokens, tokens),
        out_specs=(tokens,) * 4,
        check_vma=False,
    )
```

time: 1190 us -> 101 us (0.08)
  the two profiles are of different devices: /device:TPU:125 before, /device:TPU:23 now
where the time goes in v1:
time: 101 us; the launch traced here: 99.9 us
  starting transfers between devices  43.1 us (43%)
  waiting for transfers between devices  25.3 us (25%)
  blocking collectives  18.9 us (19%)
  Pallas kernels  9.14 us (9%)
  between operations  2.05 us (2%)
  local copies, waits for them, and re-layouts  1.29 us (1%)
    ppermute x8, starting transfers between devices, move(): return lax.ppermute(x, ('pair', 'half'), pairs_of)  37.2 us
    all_to_all x1, waiting for transfers between devices, exchange(): lax.all_to_all(x, ('side', 'lane'), split_axis=0, concat_axis=0, tiled=True)  19.1 us
    all_to_all x1, blocking collectives, exchange(): lax.all_to_all(x, ('side', 'lane'), split_axis=0, concat_axis=0, tiled=True)  18.9 us
    ppermute x8, waiting for transfers between devices, move(): return lax.ppermute(x, ('pair', 'half'), pairs_of)  6.14 us
    all_to_all x1, starting transfers between devices, exchange(): lax.all_to_all(x, ('side', 'lane'), split_axis=0, concat_axis=0, tiled=True)  5.99 us
    pallas_call x1, Pallas kernels, attention(): pl.pallas_call(functools.partial(attention_kernel, chain), out_shape=(jax...  5.16 us
    pallas_call x1, Pallas kernels, pack(): pl.pallas_call(pack_kernel, out_shape=jax.ShapeDtypeStruct((PARTS, PIECE,...  2.22 us
  transfers between devices with their start and end apart: 9, of which 4 were waited for; matrix products, arithmetic and copies ran while one was open for 1% of the time, Pallas kernels for 0%

profile of v1, /device:TPU:23, one launch (start us, length us, event | category | flops | bytes accessed | tf_op | source)
XLA Modules:
  0.0 99.9 jit_solution(15488887968435820656)
XLA Ops:
  0.6 2.2 %pack.1 = bf16[8,32,1408]{2,1,0:T(8,128)(2,1)} custom-call(s32[1,256]{1,0:T(1,128)} %bitcast.11, bf16[32,4096]{1,0:T(8,128)(2,1)} %q_ref.1, bf16[32,4096]{1,0:T(8,128)(2,1)} %g_ref.1, bf16[32,1024]{1,0:T(8,128)(2,1)} %k_ref.1, bf16[32,1024]{1,0:T(8,128)(2,1)} %v_ref.1), custom_call_target="tpu_custom_call" | custom-call | tf_op jit(solution)/shard_map/pack/pallas_call | solution.py:74
  2.9 6.0 %all-to-all-start = ((bf16[8,32,1408]{2,1,0:T(8,128)(2,1)}), bf16[8,32,1408]{2,1,0:T(8,128)(2,1)S(1)}, u32[]{:S(2)}, u32[]{:S(2)}) async-start(bf16[8,32,1408]{2,1,0:T(8,128)(2,1)} %pack.1), calls=%async_computation | async-start | bytes 1441792 | tf_op jit(solution)/shard_map/all_to_all | solution.py:315
  8.8 0.7 copy-done
  9.5 0.6 fusion.1
  11.4 19.1 %all-to-all-done = bf16[8,32,1408]{2,1,0:T(8,128)(2,1)S(1)} async-done(((bf16[8,32,1408]{2,1,0:T(8,128)(2,1)}), bf16[8,32,1408]{2,1,0:T(8,128)(2,1)S(1)}, u32[]{:S(2)}, u32[]{:S(2)}) %all-to-all-start) | async-done | bytes 720928 | tf_op jit(solution)/shard_map/all_to_all | solution.py:315
  30.6 0.0 copy-start.1
  30.6 11.1 %collective-permute-start.1 = (bf16[256,256]{1,0:T(8,128)(2,1)S(1)}, bf16[256,256]{1,0:T(8,128)(2,1)S(1)}, u32[]{:S(2)}, u32[]{:S(2)}) collective-permute-start(bf16[256,256]{1,0:T(8,128)(2,1)S(1)} %slice.15), channel_id=1, source_target_pairs={{0,32},{16,48},{32,64},{48,80},{64,96},{80,112},{96,128},{112,144}... | collective-permute-start | bytes 393224 | tf_op jit(solution)/shard_map/ppermute | solution.py:312
  41.6 2.2 %collective-permute-start = (bf16[256,256]{1,0:T(8,128)(2,1)S(1)}, bf16[256,256]{1,0:T(8,128)(2,1)S(1)}, u32[]{:S(2)}, u32[]{:S(2)}) collective-permute-start(bf16[256,256]{1,0:T(8,128)(2,1)S(1)} %slice.15), channel_id=1, source_target_pairs={{0,16},{16,32},{32,48},{48,64},{64,80},{80,96},{96,112},{112,128},... | collective-permute-start | bytes 393224 | tf_op jit(solution)/shard_map/ppermute | solution.py:312
  43.9 3.1 %collective-permute-start.3 = (bf16[128,256]{1,0:T(8,128)(2,1)S(1)}, bf16[128,256]{1,0:T(8,128)(2,1)S(1)}, u32[]{:S(2)}, u32[]{:S(2)}) collective-permute-start(bf16[128,256]{1,0:T(8,128)(2,1)S(1)} %get-tuple-element.16), channel_id=1, source_target_pairs={{484,500},{468,484},{452,468},{436,452},{420,436},{404,420},{388,4... | collective-permute-start | bytes 196616 | tf_op jit(solution)/shard_map/ppermute | solution.py:312
  47.0 1.9 %collective-permute-start.2 = (bf16[128,256]{1,0:T(8,128)(2,1)S(1)}, bf16[128,256]{1,0:T(8,128)(2,1)S(1)}, u32[]{:S(2)}, u32[]{:S(2)}) collective-permute-start(bf16[128,256]{1,0:T(8,128)(2,1)S(1)} %get-tuple-element.17), channel_id=1, source_target_pairs={{464,500},{480,484},{496,468},{500,452},{484,436},{468,420},{452,4... | collective-permute-start | bytes 196616 | tf_op jit(solution)/shard_map/ppermute | solution.py:312
  48.9 0.1 pad_add_fusion.place_ref
  49.0 2.0 %collective-permute-done.3.back_ref = bf16[128,256]{1,0:T(8,128)(2,1)S(1)} collective-permute-done((bf16[128,256]{1,0:T(8,128)(2,1)S(1)}, bf16[128,256]{1,0:T(8,128)(2,1)S(1)}, u32[]{:S(2)}, u32[]{:S(2)}) %collective-permute-start.3) | collective-permute-done | bytes 65568 | tf_op jit(solution)/shard_map/ppermute | solution.py:312
  51.0 2.8 %collective-permute-done.2.three_ref = bf16[128,256]{1,0:T(8,128)(2,1)S(1)} collective-permute-done((bf16[128,256]{1,0:T(8,128)(2,1)S(1)}, bf16[128,256]{1,0:T(8,128)(2,1)S(1)}, u32[]{:S(2)}, u32[]{:S(2)}) %collective-permute-start.2) | collective-permute-done | bytes 65568 | tf_op jit(solution)/shard_map/ppermute | solution.py:312
  53.8 0.0 collective-permute-done.1.two_ref
  53.8 0.0 collective-permute-done.one_ref
  53.8 5.2 %attention.1 = (bf16[256,1024]{1,0:T(8,128)(2,1)S(1)}, f32[256,256]{1,0:T(8,128)S(1)}, bf16[256,256]{1,0:T(8,128)(2,1)S(1)}, bf16[256,256]{1,0:T(8,128)(2,1)S(1)...) custom-call(s32[3]{0:T(128)S(1)} %pad_add_fusion.place_ref, s32[64]{0:T(128)S(1)} %copy-done, ...), custom_call_target="tpu_custom_call" | custom-call | flops 838860800 | bytes 3145728 | tf_op jit(solution)/shard_map/attention/pallas_call | solution.py:266
  59.0 5.2 %collective-permute-start.4 = (bf16[256,256]{1,0:T(8,128)(2,1)S(1)}, bf16[256,256]{1,0:T(8,128)(2,1)S(1)}, u32[]{:S(2)}, u32[]{:S(2)}) collective-permute-start(bf16[256,256]{1,0:T(8,128)(2,1)S(1)} %get-tuple-element.12), channel_id=1, source_target_pairs={{16,0},{32,16},{48,32},{64,48},{80,64},{96,80},{112,96},{128,112},... | collective-permute-start | bytes 393224 | tf_op jit(solution)/shard_map/ppermute | solution.py:312
  64.2 1.9 %collective-permute-start.5 = (bf16[256,256]{1,0:T(8,128)(2,1)S(1)}, bf16[256,256]{1,0:T(8,128)(2,1)S(1)}, u32[]{:S(2)}, u32[]{:S(2)}) collective-permute-start(bf16[256,256]{1,0:T(8,128)(2,1)S(1)} %get-tuple-element.13), channel_id=1, source_target_pairs={{32,0},{48,16},{64,32},{80,48},{96,64},{112,80},{128,96},{144,112}... | collective-permute-start | bytes 393224 | tf_op jit(solution)/shard_map/ppermute | solution.py:312
  66.1 6.5 %collective-permute-start.6 = (bf16[128,256]{1,0:T(8,128)(2,1)S(1)}, bf16[128,256]{1,0:T(8,128)(2,1)S(1)}, u32[]{:S(2)}, u32[]{:S(2)}) collective-permute-start(bf16[128,256]{1,0:T(8,128)(2,1)S(1)} %get-tuple-element.14), channel_id=1, source_target_pairs={{500,464},{484,480},{468,496},{452,500},{436,484},{420,468},{404,4... | collective-permute-start | bytes 196616 | tf_op jit(solution)/shard_map/ppermute | solution.py:312
  72.7 5.2 %collective-permute-start.7 = (bf16[128,256]{1,0:T(8,128)(2,1)S(1)}, bf16[128,256]{1,0:T(8,128)(2,1)S(1)}, u32[]{:S(2)}, u32[]{:S(2)}) collective-permute-start(bf16[128,256]{1,0:T(8,128)(2,1)S(1)} %get-tuple-element.15), channel_id=1, source_target_pairs={{500,484},{484,468},{468,452},{452,436},{436,420},{420,404},{404,3... | collective-permute-start | bytes 196616 | tf_op jit(solution)/shard_map/ppermute | solution.py:312
  77.9 1.3 %collective-permute-done.7.back_ref = bf16[128,256]{1,0:T(8,128)(2,1)S(1)} collective-permute-done((bf16[128,256]{1,0:T(8,128)(2,1)S(1)}, bf16[128,256]{1,0:T(8,128)(2,1)S(1)}, u32[]{:S(2)}, u32[]{:S(2)}) %collective-permute-start.7) | collective-permute-done | bytes 65568 | tf_op jit(solution)/shard_map/ppermute | solution.py:312
  79.2 0.7 gather.1
  79.9 18.9 %all_to_all.10.split_ref = bf16[8,32,1280]{2,1,0:T(8,128)(2,1)S(1)} all-to-all(bf16[8,32,1280]{2,1,0:T(8,128)(2,1)S(1)} %bitcast.7), channel_id=1, replica_groups=mesh['pair'=32,'side'=2,'half'=2,'lane'=4] {'side','lane'}, dimensions={0} | all-to-all | bytes 1310720 | tf_op jit(solution)/shard_map/all_to_all | solution.py:315
  98.8 1.1 %unpack.1 = (bf16[32,4096]{1,0:T(8,128)(2,1)}, bf16[32,4096]{1,0:T(8,128)(2,1)}, bf16[32,1024]{1,0:T(8,128)(2,1)}, bf16[32,1024]{1,0:T(8,128)(2,1)}) custom-call(bf16[8,32,1280]{2,1,0:T(8,128)(2,1)S(1)} %all_to_all.10.split_ref), custom_call_target="tpu_custom_call" | custom-call | tf_op jit(solution)/shard_map/unpack/pallas_call | solution.py:104
  (7 shorter events, 0.0 us)
Async XLA Ops:
  2.9 27.7 %all-to-all-start = ((bf16[8,32,1408]{2,1,0:T(8,128)(2,1)}), bf16[8,32,1408]{2,1,0:T(8,128)(2,1)S(1)}, u32[]{:S(2)}, u32[]{:S(2)}) async-start(bf16[8,32,1408]{2,1,0:T(8,128)(2,1)} %pack.1), calls=%async_computation | async-start | bytes 1441792 | tf_op jit(solution)/shard_map/all_to_all | solution.py:315
  8.8 0.7 copy-start
  30.6 23.2 %copy-start.1 = (s32[128,128]{1,0:T(8,128)S(1)}, s32[128,128]{1,0:T(8,128)}, u32[]{:S(2)}) copy-start(s32[128,128]{1,0:T(8,128)} %live_ref.1) | copy-start | bytes 196612
  30.6 23.2 %collective-permute-start.1 = (bf16[256,256]{1,0:T(8,128)(2,1)S(1)}, bf16[256,256]{1,0:T(8,128)(2,1)S(1)}, u32[]{:S(2)}, u32[]{:S(2)}) collective-permute-start(bf16[256,256]{1,0:T(8,128)(2,1)S(1)} %slice.15), channel_id=1, source_target_pairs={{0,32},{16,48},{32,64},{48,80},{64,96},{80,112},{96,128},{112,144}... | collective-permute-start | bytes 393224 | tf_op jit(solution)/shard_map/ppermute | solution.py:312
  41.6 12.2 %collective-permute-start = (bf16[256,256]{1,0:T(8,128)(2,1)S(1)}, bf16[256,256]{1,0:T(8,128)(2,1)S(1)}, u32[]{:S(2)}, u32[]{:S(2)}) collective-permute-start(bf16[256,256]{1,0:T(8,128)(2,1)S(1)} %slice.15), channel_id=1, source_target_pairs={{0,16},{16,32},{32,48},{48,64},{64,80},{80,96},{96,112},{112,128},... | collective-permute-start | bytes 393224 | tf_op jit(solution)/shard_map/ppermute | solution.py:312
  43.9 7.1 %collective-permute-start.3 = (bf16[128,256]{1,0:T(8,128)(2,1)S(1)}, bf16[128,256]{1,0:T(8,128)(2,1)S(1)}, u32[]{:S(2)}, u32[]{:S(2)}) collective-permute-start(bf16[128,256]{1,0:T(8,128)(2,1)S(1)} %get-tuple-element.16), channel_id=1, source_target_pairs={{484,500},{468,484},{452,468},{436,452},{420,436},{404,420},{388,4... | collective-permute-start | bytes 196616 | tf_op jit(solution)/shard_map/ppermute | solution.py:312
  47.0 6.8 %collective-permute-start.2 = (bf16[128,256]{1,0:T(8,128)(2,1)S(1)}, bf16[128,256]{1,0:T(8,128)(2,1)S(1)}, u32[]{:S(2)}, u32[]{:S(2)}) collective-permute-start(bf16[128,256]{1,0:T(8,128)(2,1)S(1)} %get-tuple-element.17), channel_id=1, source_target_pairs={{464,500},{480,484},{496,468},{500,452},{484,436},{468,420},{452,4... | collective-permute-start | bytes 196616 | tf_op jit(solution)/shard_map/ppermute | solution.py:312
  59.0 20.2 %collective-permute-start.4 = (bf16[256,256]{1,0:T(8,128)(2,1)S(1)}, bf16[256,256]{1,0:T(8,128)(2,1)S(1)}, u32[]{:S(2)}, u32[]{:S(2)}) collective-permute-start(bf16[256,256]{1,0:T(8,128)(2,1)S(1)} %get-tuple-element.12), channel_id=1, source_target_pairs={{16,0},{32,16},{48,32},{64,48},{80,64},{96,80},{112,96},{128,112},... | collective-permute-start | bytes 393224 | tf_op jit(solution)/shard_map/ppermute | solution.py:312
  64.2 15.0 %collective-permute-start.5 = (bf16[256,256]{1,0:T(8,128)(2,1)S(1)}, bf16[256,256]{1,0:T(8,128)(2,1)S(1)}, u32[]{:S(2)}, u32[]{:S(2)}) collective-permute-start(bf16[256,256]{1,0:T(8,128)(2,1)S(1)} %get-tuple-element.13), channel_id=1, source_target_pairs={{32,0},{48,16},{64,32},{80,48},{96,64},{112,80},{128,96},{144,112}... | collective-permute-start | bytes 393224 | tf_op jit(solution)/shard_map/ppermute | solution.py:312
  66.1 11.8 %collective-permute-start.6 = (bf16[128,256]{1,0:T(8,128)(2,1)S(1)}, bf16[128,256]{1,0:T(8,128)(2,1)S(1)}, u32[]{:S(2)}, u32[]{:S(2)}) collective-permute-start(bf16[128,256]{1,0:T(8,128)(2,1)S(1)} %get-tuple-element.14), channel_id=1, source_target_pairs={{500,464},{484,480},{468,496},{452,500},{436,484},{420,468},{404,4... | collective-permute-start | bytes 196616 | tf_op jit(solution)/shard_map/ppermute | solution.py:312
  72.7 6.5 %collective-permute-start.7 = (bf16[128,256]{1,0:T(8,128)(2,1)S(1)}, bf16[128,256]{1,0:T(8,128)(2,1)S(1)}, u32[]{:S(2)}, u32[]{:S(2)}) collective-permute-start(bf16[128,256]{1,0:T(8,128)(2,1)S(1)} %get-tuple-element.15), channel_id=1, source_target_pairs={{500,484},{484,468},{468,452},{452,436},{436,420},{420,404},{404,3... | collective-permute-start | bytes 196616 | tf_op jit(solution)/shard_map/ppermute | solution.py:312

commit v2 on v1

--- a/solution.py
+++ b/solution.py
@@ -20,9 +20,7 @@
 SLOTS = 8
 NEGATIVE = -1e30
 QUERY_WIDE = GROUP * DIM
-KEY_AT = 2 * QUERY_WIDE
-WIDE = KEY_AT + 2 * DIM
-SENT = WIDE + DIM
+QG_WIDE = 2 * QUERY_WIDE
 
 
 def dot(a, b, over_a, over_b):
@@ -37,60 +35,61 @@
     ]
 
 
-def places(q, g, k, v, split):
-    return (
-        pieces(q, split, 0, QUERY_WIDE)
-        + pieces(g, split, QUERY_WIDE, QUERY_WIDE)
-        + pieces(k, split, KEY_AT, DIM)
-        + pieces(v, split, KEY_AT + DIM, DIM)
-    )
-
-
-def pack_kernel(doc_ref, q_ref, g_ref, k_ref, v_ref, out_ref, doc_here, sems, doc_sem):
-    doc_copy = pltpu.make_async_copy(doc_ref, doc_here, doc_sem)
-    doc_copy.start()
-    copies = [
-        pltpu.make_async_copy(rows, split, sems.at[i])
-        for i, (rows, split) in enumerate(places(q_ref, g_ref, k_ref, v_ref, out_ref))
+def copies_of(first, second, split, at, wide, sems, cut):
+    pairs = pieces(first, split, at, wide) + pieces(second, split, at + wide, wide)
+    return [
+        pltpu.make_async_copy(*((rows, piece) if cut else (piece, rows)), sems.at[i])
+        for i, (rows, piece) in enumerate(pairs)
     ]
+
+
+def pack_kernel(wide, first_ref, second_ref, *refs):
+    if len(refs) == 2:
+        out_ref, sems = refs
+    else:
+        doc_ref, out_ref, sems, doc_here, doc_sem = refs
+        doc_copy = pltpu.make_async_copy(doc_ref, doc_here, doc_sem)
+        doc_copy.start()
+    copies = copies_of(first_ref, second_ref, out_ref, 0, wide, sems, True)
     for copy in copies:
         copy.start()
-    doc_copy.wait()
-    doc = doc_here[...]
-    line = lax.broadcasted_iota(jnp.int32, (PIECE, BLOCK), 0)
-    first, second = doc[:, :BLOCK], doc[:, BLOCK:]
-    coded = jnp.where(line < 2, first, second)
-    coded = jnp.where(line % 2 == 0, coded // BLOCK, coded % BLOCK)
-    coded = coded.astype(jnp.float32).astype(jnp.bfloat16)
-    for h in range(PARTS):
-        out_ref[h, :, WIDE:] = coded
+    if len(refs) > 2:
+        doc_copy.wait()
+        doc = doc_here[...]
+        line = lax.broadcasted_iota(jnp.int32, (PIECE, BLOCK), 0)
+        coded = jnp.where(line < 2, doc[:, :BLOCK], doc[:, BLOCK:])
+        coded = jnp.where(line % 2 == 0, coded // BLOCK, coded % BLOCK)
+        coded = coded.astype(jnp.float32).astype(jnp.bfloat16)
+        for h in range(PARTS):
+            out_ref[h, :, 2 * wide :] = coded
     for copy in copies:
         copy.wait()
 
 
-def pack(doc, query, grad_out, key, value):
-    vmem = pl.BlockSpec(memory_space=pltpu.VMEM)
+def pack(first, second, doc=None):
     hbm = pl.BlockSpec(memory_space=pltpu.HBM)
+    wide = first.shape[1] // PARTS
+    scratch = [pltpu.SemaphoreType.DMA((2 * PARTS,))]
+    arrays = (first, second)
+    sent = 2 * wide
+    if doc is not None:
+        scratch += [pltpu.VMEM((1, ROWS), jnp.int32), pltpu.SemaphoreType.DMA]
+        arrays += (doc,)
+        sent += DIM
     return pl.pallas_call(
-        pack_kernel,
-        out_shape=jax.ShapeDtypeStruct((PARTS, PIECE, SENT), jnp.bfloat16),
-        in_specs=[hbm] * 5,
-        out_specs=vmem,
-        scratch_shapes=[
-            pltpu.VMEM((1, ROWS), jnp.int32),
-            pltpu.SemaphoreType.DMA((4 * PARTS,)),
-            pltpu.SemaphoreType.DMA,
-        ],
+        functools.partial(pack_kernel, wide),
+        out_shape=jax.ShapeDtypeStruct((PARTS, PIECE, sent), jnp.bfloat16),
+        in_specs=[hbm] * len(arrays),
+        out_specs=pl.BlockSpec(memory_space=pltpu.VMEM),
+        scratch_shapes=scratch,
         compiler_params=pltpu.CompilerParams(vmem_limit_bytes=(63 * 1024 + 256) * 1024),
         name="pack",
-    )(doc, query, grad_out, key, value)
+    )(*arrays)
 
 
 def unpack_kernel(split_ref, att_ref, dq_ref, dk_ref, dv_ref, sems):
-    copies = [
-        pltpu.make_async_copy(split, rows, sems.at[i])
-        for i, (rows, split) in enumerate(places(att_ref, dq_ref, dk_ref, dv_ref, split_ref))
-    ]
+    copies = copies_of(att_ref, dq_ref, split_ref, 0, QUERY_WIDE, sems, False)
+    copies += copies_of(dk_ref, dv_ref, split_ref, QG_WIDE, DIM, sems.at[2 * PARTS :], False)
     for copy in copies:
         copy.start()
     for copy in copies:
@@ -117,13 +116,13 @@
 ):
     pair = place_ref[0]
     later = (place_ref[2] == 0) | (pairing_ref[2 * pair + 1] < pairing_ref[2 * pair])
-    out_ref[:, :KEY_AT] = od_ref[...]
+    out_ref[:, :QG_WIDE] = od_ref[...]
     total = own_ref[...] + one_ref[...].astype(jnp.float32) + two_ref[...].astype(jnp.float32)
     three = three_ref[...].astype(jnp.float32)
     lower = total[:BLOCK] + jnp.where(later, 0.0, three)
     upper = total[BLOCK:] + jnp.where(later, three, 0.0) + back_ref[...].astype(jnp.float32)
-    out_ref[:BLOCK, KEY_AT:] = lower.astype(jnp.bfloat16)
-    out_ref[BLOCK:, KEY_AT:] = upper.astype(jnp.bfloat16)
+    out_ref[:BLOCK, QG_WIDE:] = lower.astype(jnp.bfloat16)
+    out_ref[BLOCK:, QG_WIDE:] = upper.astype(jnp.bfloat16)
 
 
 def gather(place, pairing, od, parts):
@@ -131,7 +130,7 @@
     smem = pl.BlockSpec(memory_space=pltpu.SMEM)
     return pl.pallas_call(
         gather_kernel,
-        out_shape=jax.ShapeDtypeStruct((ROWS, WIDE), jnp.bfloat16),
+        out_shape=jax.ShapeDtypeStruct((ROWS, QG_WIDE + 2 * DIM), jnp.bfloat16),
         in_specs=[smem, smem] + [vmem] * 6,
         out_specs=vmem,
         compiler_params=pltpu.CompilerParams(vmem_limit_bytes=16 * 1024 * 1024),
@@ -145,6 +144,7 @@
     pairing_ref,
     live_ref,
     qg_ref,
+    own_ref,
     one_ref,
     two_ref,
     three_ref,
@@ -165,7 +165,7 @@
     scale = 1.0 / math.sqrt(DIM)
     my_place = jnp.where(half == 0, pair, chain - 1 - pair)
 
-    kv[0:256, :] = qg_ref[:, KEY_AT:WIDE]
+    kv[0:256, :] = own_ref[...]
     kv[256:512, :] = one_ref[...]
     kv[512:768, :] = two_ref[...]
     kv[768:896, :] = three_ref[...]
@@ -179,7 +179,7 @@
     for b in range(2):
         holder = 2 * pair + b
         block = jnp.where(half == 0, holder, blocks - 1 - pairing_ref[holder])
-        doc = qg_ref[b * BLOCK : b * BLOCK + PIECE, WIDE:].astype(jnp.float32)
+        doc = qg_ref[b * BLOCK : b * BLOCK + PIECE, QG_WIDE:].astype(jnp.float32)
         doc = jnp.where(half == 0, doc[0:2], doc[2:4])
         begins = (doc[0:1] * BLOCK + doc[1:2]).astype(jnp.int32)
         live_row = live_ref[pl.ds(block, 1), :]
@@ -273,7 +273,7 @@
             jax.ShapeDtypeStruct((BLOCK, wide), jnp.bfloat16),
             jax.ShapeDtypeStruct((BLOCK, wide), jnp.bfloat16),
         ),
-        in_specs=[smem, smem] + [vmem] * 6,
+        in_specs=[smem, smem] + [vmem] * 7,
         out_specs=(vmem,) * 6,
         scratch_shapes=[
             pltpu.VMEM((SLOTS * BLOCK, wide), jnp.bfloat16),
@@ -314,21 +314,25 @@
     def exchange(x):
         return lax.all_to_all(x, ("side", "lane"), split_axis=0, concat_axis=0, tiled=True)
 
-    split = pack(doc_start.reshape(1, ROWS), query, grad_out, key, value)
-    arrived = exchange(split).reshape(ROWS, SENT)
-    own = arrived[:, KEY_AT:WIDE]
     later = (half == 0) | (pairing[2 * pair + 1] < pairing[2 * pair])
+    own = exchange(pack(key, value)).reshape(ROWS, 2 * DIM)
+    split, later = lax.optimization_barrier(
+        (pack(query, grad_out, doc_start.reshape(1, ROWS)), later)
+    )
+    split, own = lax.optimization_barrier((split, own))
+    qg = exchange(split).reshape(ROWS, QG_WIDE + DIM)
     halo = (
+        own,
         move(own, forth[0]),
         move(own, forth[1]),
         move(jnp.where(later, own[BLOCK:], own[:BLOCK]), forth[2]),
         move(own[BLOCK:], forth[3]),
     )
     place = jnp.stack([pair, side, half]).astype(jnp.int32)
-    od, own_grad, *partials = attention(chain, place, pairing, block_live, arrived, halo)
+    od, own_grad, *partials = attention(chain, place, pairing, block_live, qg, halo)
     partials = [move(part, pairs_of) for part, pairs_of in zip(partials, back)]
     total = gather(place, pairing, od, (own_grad, *partials))
-    return unpack(exchange(total.reshape(PARTS, PIECE, WIDE)))
+    return unpack(exchange(total.reshape(PARTS, PIECE, -1)))
 
 
 def solution(mesh):

time: 101 us -> 103 us (1.020)
  waiting for transfers between devices: 25.3 us -> 9.41 us
  starting transfers between devices: 43.1 us -> 51.7 us
  blocking collectives: 18.9 us -> 26.9 us
  Pallas kernels: 9.14 us -> 10.6 us
    all_to_all x1 -> x2, waiting for transfers between devices: 19.1 us -> 3.2 us  [exchange(): lax.all_to_all(x, ('side', 'lane'), split_axis=0, concat_axis=0, tiled=True)]
    all_to_all x1, blocking collectives: 18.9 us -> 26.9 us  [exchange(): lax.all_to_all(x, ('side', 'lane'), split_axis=0, concat_axis=0, tiled=True)]
    all_to_all x1 -> x2, starting transfers between devices: 5.99 us -> 10.3 us  [exchange(): lax.all_to_all(x, ('side', 'lane'), split_axis=0, concat_axis=0, tiled=True)]
    ppermute x8, starting transfers between devices: 37.2 us -> 41.4 us  [move(): return lax.ppermute(x, ('pair', 'half'), pairs_of)]
    pallas_call x2 -> x3, Pallas kernels: 2.87 us -> 4.28 us  [the longest x2 3.63 us: pack(): pl.pallas_call(functools.partial(pack_kernel, wide), out_shape=jax.ShapeD...]
  transfers between devices with their start and end apart: 9 -> 10, of which waited for: 4 -> 4; matrix products, arithmetic and copies ran while one was open for 1% -> 1% of each run, Pallas kernels for 0% -> 2%
where the time goes in v2:
time: 103 us; the launch traced here: 102 us
  starting transfers between devices  51.7 us (50%)
  blocking collectives  26.9 us (26%)
  Pallas kernels  10.6 us (10%)
  waiting for transfers between devices  9.41 us (9%)
  between operations  2.05 us (2%)
  local copies, waits for them, and re-layouts  1.27 us (1%)
    ppermute x8, starting transfers between devices, move(): return lax.ppermute(x, ('pair', 'half'), pairs_of)  41.4 us
    all_to_all x1, blocking collectives, exchange(): lax.all_to_all(x, ('side', 'lane'), split_axis=0, concat_axis=0, tiled=True)  26.9 us
    all_to_all x2, starting transfers between devices, exchange(): lax.all_to_all(x, ('side', 'lane'), split_axis=0, concat_axis=0, tiled=True)  10.3 us
    ppermute x8, waiting for transfers between devices, move(): return lax.ppermute(x, ('pair', 'half'), pairs_of)  6.21 us
    pallas_call x1, Pallas kernels, attention(): pl.pallas_call(functools.partial(attention_kernel, chain), out_shape=(jax...  5.18 us
    pallas_call x2, Pallas kernels, pack(): pl.pallas_call(functools.partial(pack_kernel, wide), out_shape=jax.ShapeD...  3.63 us
    all_to_all x2, waiting for transfers between devices, exchange(): lax.all_to_all(x, ('side', 'lane'), split_axis=0, concat_axis=0, tiled=True)  3.2 us
  transfers between devices with their start and end apart: 10, of which 4 were waited for; matrix products, arithmetic and copies ran while one was open for 1% of the time, Pallas kernels for 2%

profile of v2, /device:TPU:23, one launch (start us, length us, event | category | flops | bytes accessed | tf_op | source)
XLA Modules:
  0.0 102.0 jit_solution(7458474320798999231)
XLA Ops:
  0.6 1.7 %pack.3 = bf16[8,32,256]{2,1,0:T(8,128)(2,1)} custom-call(bf16[32,1024]{1,0:T(8,128)(2,1)} %first_ref.3, bf16[32,1024]{1,0:T(8,128)(2,1)} %second_ref.3), custom_call_target="tpu_custom_call" | custom-call | tf_op jit(solution)/shard_map/pack/pallas_call | solution.py:79
  2.3 6.0 %all-to-all-start = ((bf16[8,32,256]{2,1,0:T(8,128)(2,1)}), bf16[8,32,256]{2,1,0:T(8,128)(2,1)S(1)}, u32[]{:S(2)}, u32[]{:S(2)}) async-start(bf16[8,32,256]{2,1,0:T(8,128)(2,1)} %pack.3), calls=%async_computation | async-start | bytes 262144 | tf_op jit(solution)/shard_map/all_to_all | solution.py:315
  8.3 0.7 copy-done
  8.9 0.6 fusion.1
  10.8 2.0 %pack.2 = bf16[8,32,1152]{2,1,0:T(8,128)(2,1)} custom-call(bf16[32,4096]{1,0:T(8,128)(2,1)} %first_ref.2, bf16[32,4096]{1,0:T(8,128)(2,1)} %second_ref.2, s32[1,256]{1,0:T(1,128)} %bitcast.14), custom_call_target="tpu_custom_call" | custom-call | tf_op jit(solution)/shard_map/pack/pallas_call | solution.py:79
  12.8 3.2 %all-to-all-done = bf16[8,32,256]{2,1,0:T(8,128)(2,1)S(1)} async-done(((bf16[8,32,256]{2,1,0:T(8,128)(2,1)}), bf16[8,32,256]{2,1,0:T(8,128)(2,1)S(1)}, u32[]{:S(2)}, u32[]{:S(2)}) %all-to-all-start) | async-done | bytes 131104 | tf_op jit(solution)/shard_map/all_to_all | solution.py:315
  16.0 4.3 %all-to-all-start.1 = ((bf16[8,32,1152]{2,1,0:T(8,128)(2,1)}), bf16[8,32,1152]{2,1,0:T(8,128)(2,1)S(1)}, u32[]{:S(2)}, u32[]{:S(2)}) async-start(bf16[8,32,1152]{2,1,0:T(8,128)(2,1)} %pack.2), calls=%async_computation.1 | async-start | bytes 1179648 | tf_op jit(solution)/shard_map/all_to_all | solution.py:315
  20.3 11.0 %collective-permute-start.1 = (bf16[256,256]{1,0:T(8,128)(2,1)S(1)}, bf16[256,256]{1,0:T(8,128)(2,1)S(1)}, u32[]{:S(2)}, u32[]{:S(2)}) collective-permute-start(bf16[256,256]{1,0:T(8,128)(2,1)S(1)} %bitcast.10), channel_id=1, source_target_pairs={{0,32},{16,48},{32,64},{48,80},{64,96},{80,112},{96,128},{112,144}... | collective-permute-start | bytes 393224 | tf_op jit(solution)/shard_map/ppermute | solution.py:312
  31.4 2.2 %collective-permute-start = (bf16[256,256]{1,0:T(8,128)(2,1)S(1)}, bf16[256,256]{1,0:T(8,128)(2,1)S(1)}, u32[]{:S(2)}, u32[]{:S(2)}) collective-permute-start(bf16[256,256]{1,0:T(8,128)(2,1)S(1)} %bitcast.11), channel_id=1, source_target_pairs={{0,16},{16,32},{32,48},{48,64},{64,80},{80,96},{96,112},{112,128},... | collective-permute-start | bytes 393224 | tf_op jit(solution)/shard_map/ppermute | solution.py:312
  33.6 3.1 %collective-permute-start.3 = (bf16[128,256]{1,0:T(8,128)(2,1)S(1)}, bf16[128,256]{1,0:T(8,128)(2,1)S(1)}, u32[]{:S(2)}, u32[]{:S(2)}) collective-permute-start(bf16[128,256]{1,0:T(8,128)(2,1)S(1)} %get-tuple-element.24), channel_id=1, source_target_pairs={{484,500},{468,484},{452,468},{436,452},{420,436},{404,420},{388,4... | collective-permute-start | bytes 196616 | tf_op jit(solution)/shard_map/ppermute | solution.py:312
  36.7 1.9 %collective-permute-start.2 = (bf16[128,256]{1,0:T(8,128)(2,1)S(1)}, bf16[128,256]{1,0:T(8,128)(2,1)S(1)}, u32[]{:S(2)}, u32[]{:S(2)}) collective-permute-start(bf16[128,256]{1,0:T(8,128)(2,1)S(1)} %get-tuple-element.25), channel_id=1, source_target_pairs={{464,500},{480,484},{496,468},{500,452},{484,436},{468,420},{452,4... | collective-permute-start | bytes 196616 | tf_op jit(solution)/shard_map/ppermute | solution.py:312
  38.6 0.1 pad_add_fusion.place_ref
  38.7 2.0 %collective-permute-done.3.back_ref = bf16[128,256]{1,0:T(8,128)(2,1)S(1)} collective-permute-done((bf16[128,256]{1,0:T(8,128)(2,1)S(1)}, bf16[128,256]{1,0:T(8,128)(2,1)S(1)}, u32[]{:S(2)}, u32[]{:S(2)}) %collective-permute-start.3) | collective-permute-done | bytes 65568 | tf_op jit(solution)/shard_map/ppermute | solution.py:312
  40.7 2.9 %collective-permute-done.2.three_ref = bf16[128,256]{1,0:T(8,128)(2,1)S(1)} collective-permute-done((bf16[128,256]{1,0:T(8,128)(2,1)S(1)}, bf16[128,256]{1,0:T(8,128)(2,1)S(1)}, u32[]{:S(2)}, u32[]{:S(2)}) %collective-permute-start.2) | collective-permute-done | bytes 65568 | tf_op jit(solution)/shard_map/ppermute | solution.py:312
  43.6 0.0 collective-permute-done.1.two_ref
  43.7 5.2 %attention.1 = (bf16[256,1024]{1,0:T(8,128)(2,1)S(1)}, f32[256,256]{1,0:T(8,128)S(1)}, bf16[256,256]{1,0:T(8,128)(2,1)S(1)}, bf16[256,256]{1,0:T(8,128)(2,1)S(1)...) custom-call(s32[3]{0:T(128)S(1)} %pad_add_fusion.place_ref, s32[64]{0:T(128)S(1)} %copy-done, ...), custom_call_target="tpu_custom_call" | custom-call | flops 838860800 | bytes 3145728 | tf_op jit(solution)/shard_map/attention/pallas_call | solution.py:266
  48.8 6.8 %collective-permute-start.4 = (bf16[256,256]{1,0:T(8,128)(2,1)S(1)}, bf16[256,256]{1,0:T(8,128)(2,1)S(1)}, u32[]{:S(2)}, u32[]{:S(2)}) collective-permute-start(bf16[256,256]{1,0:T(8,128)(2,1)S(1)} %get-tuple-element.20), channel_id=1, source_target_pairs={{16,0},{32,16},{48,32},{64,48},{80,64},{96,80},{112,96},{128,112},... | collective-permute-start | bytes 393224 | tf_op jit(solution)/shard_map/ppermute | solution.py:312
  55.7 1.9 %collective-permute-start.5 = (bf16[256,256]{1,0:T(8,128)(2,1)S(1)}, bf16[256,256]{1,0:T(8,128)(2,1)S(1)}, u32[]{:S(2)}, u32[]{:S(2)}) collective-permute-start(bf16[256,256]{1,0:T(8,128)(2,1)S(1)} %get-tuple-element.21), channel_id=1, source_target_pairs={{32,0},{48,16},{64,32},{80,48},{96,64},{112,80},{128,96},{144,112}... | collective-permute-start | bytes 393224 | tf_op jit(solution)/shard_map/ppermute | solution.py:312
  57.6 8.9 %collective-permute-start.6 = (bf16[128,256]{1,0:T(8,128)(2,1)S(1)}, bf16[128,256]{1,0:T(8,128)(2,1)S(1)}, u32[]{:S(2)}, u32[]{:S(2)}) collective-permute-start(bf16[128,256]{1,0:T(8,128)(2,1)S(1)} %get-tuple-element.22), channel_id=1, source_target_pairs={{500,464},{484,480},{468,496},{452,500},{436,484},{420,468},{404,4... | collective-permute-start | bytes 196616 | tf_op jit(solution)/shard_map/ppermute | solution.py:312
  66.5 5.5 %collective-permute-start.7 = (bf16[128,256]{1,0:T(8,128)(2,1)S(1)}, bf16[128,256]{1,0:T(8,128)(2,1)S(1)}, u32[]{:S(2)}, u32[]{:S(2)}) collective-permute-start(bf16[128,256]{1,0:T(8,128)(2,1)S(1)} %get-tuple-element.23), channel_id=1, source_target_pairs={{500,484},{484,468},{468,452},{452,436},{436,420},{420,404},{404,3... | collective-permute-start | bytes 196616 | tf_op jit(solution)/shard_map/ppermute | solution.py:312
  72.0 1.3 %collective-permute-done.7.back_ref = bf16[128,256]{1,0:T(8,128)(2,1)S(1)} collective-permute-done((bf16[128,256]{1,0:T(8,128)(2,1)S(1)}, bf16[128,256]{1,0:T(8,128)(2,1)S(1)}, u32[]{:S(2)}, u32[]{:S(2)}) %collective-permute-start.7) | collective-permute-done | bytes 65568 | tf_op jit(solution)/shard_map/ppermute | solution.py:312
  73.3 0.7 gather.1
  74.0 26.9 %all_to_all.15.split_ref = bf16[8,32,1280]{2,1,0:T(8,128)(2,1)S(1)} all-to-all(bf16[8,32,1280]{2,1,0:T(8,128)(2,1)S(1)} %bitcast.8), channel_id=1, replica_groups=mesh['pair'=32,'side'=2,'half'=2,'lane'=4] {'side','lane'}, dimensions={0} | all-to-all | bytes 1310720 | tf_op jit(solution)/shard_map/all_to_all | solution.py:315
  100.9 1.1 %unpack.1 = (bf16[32,4096]{1,0:T(8,128)(2,1)}, bf16[32,4096]{1,0:T(8,128)(2,1)}, bf16[32,1024]{1,0:T(8,128)(2,1)}, bf16[32,1024]{1,0:T(8,128)(2,1)}) custom-call(bf16[8,32,1280]{2,1,0:T(8,128)(2,1)S(1)} %all_to_all.15.split_ref), custom_call_target="tpu_custom_call" | custom-call | tf_op jit(solution)/shard_map/unpack/pallas_call | solution.py:103
  (9 shorter events, 0.0 us)
Async XLA Ops:
  2.3 13.7 %all-to-all-start = ((bf16[8,32,256]{2,1,0:T(8,128)(2,1)}), bf16[8,32,256]{2,1,0:T(8,128)(2,1)S(1)}, u32[]{:S(2)}, u32[]{:S(2)}) async-start(bf16[8,32,256]{2,1,0:T(8,128)(2,1)} %pack.3), calls=%async_computation | async-start | bytes 262144 | tf_op jit(solution)/shard_map/all_to_all | solution.py:315
  8.3 0.7 copy-start
  16.0 27.6 %all-to-all-start.1 = ((bf16[8,32,1152]{2,1,0:T(8,128)(2,1)}), bf16[8,32,1152]{2,1,0:T(8,128)(2,1)S(1)}, u32[]{:S(2)}, u32[]{:S(2)}) async-start(bf16[8,32,1152]{2,1,0:T(8,128)(2,1)} %pack.2), calls=%async_computation.1 | async-start | bytes 1179648 | tf_op jit(solution)/shard_map/all_to_all | solution.py:315
  20.3 23.3 %copy-start.1 = (s32[128,128]{1,0:T(8,128)S(1)}, s32[128,128]{1,0:T(8,128)}, u32[]{:S(2)}) copy-start(s32[128,128]{1,0:T(8,128)} %live_ref.1) | copy-start | bytes 196612
  20.3 23.3 %collective-permute-start.1 = (bf16[256,256]{1,0:T(8,128)(2,1)S(1)}, bf16[256,256]{1,0:T(8,128)(2,1)S(1)}, u32[]{:S(2)}, u32[]{:S(2)}) collective-permute-start(bf16[256,256]{1,0:T(8,128)(2,1)S(1)} %bitcast.10), channel_id=1, source_target_pairs={{0,32},{16,48},{32,64},{48,80},{64,96},{80,112},{96,128},{112,144}... | collective-permute-start | bytes 393224 | tf_op jit(solution)/shard_map/ppermute | solution.py:312
  31.4 12.2 %collective-permute-start = (bf16[256,256]{1,0:T(8,128)(2,1)S(1)}, bf16[256,256]{1,0:T(8,128)(2,1)S(1)}, u32[]{:S(2)}, u32[]{:S(2)}) collective-permute-start(bf16[256,256]{1,0:T(8,128)(2,1)S(1)} %bitcast.11), channel_id=1, source_target_pairs={{0,16},{16,32},{32,48},{48,64},{64,80},{80,96},{96,112},{112,128},... | collective-permute-start | bytes 393224 | tf_op jit(solution)/shard_map/ppermute | solution.py:312
  33.6 7.1 %collective-permute-start.3 = (bf16[128,256]{1,0:T(8,128)(2,1)S(1)}, bf16[128,256]{1,0:T(8,128)(2,1)S(1)}, u32[]{:S(2)}, u32[]{:S(2)}) collective-permute-start(bf16[128,256]{1,0:T(8,128)(2,1)S(1)} %get-tuple-element.24), channel_id=1, source_target_pairs={{484,500},{468,484},{452,468},{436,452},{420,436},{404,420},{388,4... | collective-permute-start | bytes 196616 | tf_op jit(solution)/shard_map/ppermute | solution.py:312
  36.7 6.9 %collective-permute-start.2 = (bf16[128,256]{1,0:T(8,128)(2,1)S(1)}, bf16[128,256]{1,0:T(8,128)(2,1)S(1)}, u32[]{:S(2)}, u32[]{:S(2)}) collective-permute-start(bf16[128,256]{1,0:T(8,128)(2,1)S(1)} %get-tuple-element.25), channel_id=1, source_target_pairs={{464,500},{480,484},{496,468},{500,452},{484,436},{468,420},{452,4... | collective-permute-start | bytes 196616 | tf_op jit(solution)/shard_map/ppermute | solution.py:312
  48.8 24.5 %collective-permute-start.4 = (bf16[256,256]{1,0:T(8,128)(2,1)S(1)}, bf16[256,256]{1,0:T(8,128)(2,1)S(1)}, u32[]{:S(2)}, u32[]{:S(2)}) collective-permute-start(bf16[256,256]{1,0:T(8,128)(2,1)S(1)} %get-tuple-element.20), channel_id=1, source_target_pairs={{16,0},{32,16},{48,32},{64,48},{80,64},{96,80},{112,96},{128,112},... | collective-permute-start | bytes 393224 | tf_op jit(solution)/shard_map/ppermute | solution.py:312
  55.7 17.6 %collective-permute-start.5 = (bf16[256,256]{1,0:T(8,128)(2,1)S(1)}, bf16[256,256]{1,0:T(8,128)(2,1)S(1)}, u32[]{:S(2)}, u32[]{:S(2)}) collective-permute-start(bf16[256,256]{1,0:T(8,128)(2,1)S(1)} %get-tuple-element.21), channel_id=1, source_target_pairs={{32,0},{48,16},{64,32},{80,48},{96,64},{112,80},{128,96},{144,112}... | collective-permute-start | bytes 393224 | tf_op jit(solution)/shard_map/ppermute | solution.py:312
  57.6 14.4 %collective-permute-start.6 = (bf16[128,256]{1,0:T(8,128)(2,1)S(1)}, bf16[128,256]{1,0:T(8,128)(2,1)S(1)}, u32[]{:S(2)}, u32[]{:S(2)}) collective-permute-start(bf16[128,256]{1,0:T(8,128)(2,1)S(1)} %get-tuple-element.22), channel_id=1, source_target_pairs={{500,464},{484,480},{468,496},{452,500},{436,484},{420,468},{404,4... | collective-permute-start | bytes 196616 | tf_op jit(solution)/shard_map/ppermute | solution.py:312
  66.5 6.8 %collective-permute-start.7 = (bf16[128,256]{1,0:T(8,128)(2,1)S(1)}, bf16[128,256]{1,0:T(8,128)(2,1)S(1)}, u32[]{:S(2)}, u32[]{:S(2)}) collective-permute-start(bf16[128,256]{1,0:T(8,128)(2,1)S(1)} %get-tuple-element.23), channel_id=1, source_target_pairs={{500,484},{484,468},{468,452},{452,436},{436,420},{420,404},{404,3... | collective-permute-start | bytes 196616 | tf_op jit(solution)/shard_map/ppermute | solution.py:312

commit v3 on v2

--- a/solution.py
+++ b/solution.py
@@ -17,7 +17,6 @@
 PARTS = 8
 ROWS = 2 * BLOCK
 PIECE = ROWS // PARTS
-SLOTS = 8
 NEGATIVE = -1e30
 QUERY_WIDE = GROUP * DIM
 QG_WIDE = 2 * QUERY_WIDE
@@ -111,16 +110,18 @@
     )(split)
 
 
-def gather_kernel(
-    place_ref, pairing_ref, od_ref, own_ref, one_ref, two_ref, three_ref, back_ref, out_ref
-):
-    pair = place_ref[0]
-    later = (place_ref[2] == 0) | (pairing_ref[2 * pair + 1] < pairing_ref[2 * pair])
+def gather_kernel(place_ref, pairing_ref, od_ref, own_ref, one_ref, two_ref, *refs):
+    *extra, out_ref = refs
     out_ref[:, :QG_WIDE] = od_ref[...]
     total = own_ref[...] + one_ref[...].astype(jnp.float32) + two_ref[...].astype(jnp.float32)
-    three = three_ref[...].astype(jnp.float32)
-    lower = total[:BLOCK] + jnp.where(later, 0.0, three)
-    upper = total[BLOCK:] + jnp.where(later, three, 0.0) + back_ref[...].astype(jnp.float32)
+    lower, upper = total[:BLOCK], total[BLOCK:]
+    if extra:
+        three_ref, back_ref = extra
+        pair = place_ref[0]
+        later = (place_ref[2] == 0) | (pairing_ref[2 * pair + 1] < pairing_ref[2 * pair])
+        three = three_ref[...].astype(jnp.float32)
+        lower = lower + jnp.where(later, 0.0, three)
+        upper = upper + jnp.where(later, three, 0.0) + back_ref[...].astype(jnp.float32)
     out_ref[:BLOCK, QG_WIDE:] = lower.astype(jnp.bfloat16)
     out_ref[BLOCK:, QG_WIDE:] = upper.astype(jnp.bfloat16)
 
@@ -131,33 +132,17 @@
     return pl.pallas_call(
         gather_kernel,
         out_shape=jax.ShapeDtypeStruct((ROWS, QG_WIDE + 2 * DIM), jnp.bfloat16),
-        in_specs=[smem, smem] + [vmem] * 6,
+        in_specs=[smem, smem] + [vmem] * (1 + len(parts)),
         out_specs=vmem,
         compiler_params=pltpu.CompilerParams(vmem_limit_bytes=16 * 1024 * 1024),
         name="gather",
     )(place, pairing, od, *parts)
 
 
-def attention_kernel(
-    chain,
-    place_ref,
-    pairing_ref,
-    live_ref,
-    qg_ref,
-    own_ref,
-    one_ref,
-    two_ref,
-    three_ref,
-    back_ref,
-    od_ref,
-    own_out,
-    one_out,
-    two_out,
-    three_out,
-    back_out,
-    kv,
-    acc,
-):
+def attention_kernel(chain, starts, joints, place_ref, pairing_ref, live_ref, qg_ref, *refs):
+    held = refs[: len(starts) - 1]
+    joint = refs[len(starts) - 1 : len(starts) - 1 + joints]
+    od_ref, *parts, kv, acc = refs[len(starts) - 1 + joints :]
     pair = place_ref[0]
     half = place_ref[2]
     blocks = 2 * chain
@@ -165,11 +150,10 @@
     scale = 1.0 / math.sqrt(DIM)
     my_place = jnp.where(half == 0, pair, chain - 1 - pair)
 
-    kv[0:256, :] = own_ref[...]
-    kv[256:512, :] = one_ref[...]
-    kv[512:768, :] = two_ref[...]
-    kv[768:896, :] = three_ref[...]
-    kv[896:1024, :] = back_ref[...]
+    for ref, begin, end in zip(held, starts, starts[1:]):
+        kv[begin:end, :] = ref[...]
+    for ref, begin, end in zip(joint, starts[1:], starts[2:]):
+        kv[begin:end, :] += ref[...]
     acc[...] = jnp.zeros_like(acc)
 
     keys_down = lax.broadcasted_iota(jnp.int32, (BLOCK, BLOCK), 0)
@@ -192,7 +176,7 @@
             where_held = jnp.where(key_block < ctx, held_by // 2, chain - 1 - held_by // 2)
             away = my_place - where_held
             slot = jnp.where(away == 3, 6, jnp.where(away == -1, 7, 2 * away + held_by % 2))
-            slot = jnp.where(key_block >= 0, jnp.clip(slot, 0, SLOTS - 1), 0)
+            slot = jnp.where(key_block >= 0, jnp.clip(slot, 0, starts[-1] // BLOCK - 1), 0)
             slots.append(pl.multiple_of(slot * BLOCK, BLOCK))
             reach = begins - key_block * BLOCK
             if w == 0:
@@ -252,32 +236,29 @@
             acc[pl.ds(s, BLOCK), :DIM] += key_grad[part]
             acc[pl.ds(s, BLOCK), DIM:] += value_grad[part]
 
-    own_out[...] = acc[0:256, :]
-    one_out[...] = acc[256:512, :].astype(jnp.bfloat16)
-    two_out[...] = acc[512:768, :].astype(jnp.bfloat16)
-    three_out[...] = acc[768:896, :].astype(jnp.bfloat16)
-    back_out[...] = acc[896:1024, :].astype(jnp.bfloat16)
-
-
-def attention(chain, place, pairing, live, qg, halo):
+    for ref, begin, end in zip(parts, starts, starts[1:]):
+        ref[...] = acc[begin:end, :].astype(ref.dtype)
+
+
+def attention(chain, place, pairing, live, qg, halo, joint):
     wide = 2 * DIM
     vmem = pl.BlockSpec(memory_space=pltpu.VMEM)
     smem = pl.BlockSpec(memory_space=pltpu.SMEM)
+    starts = [0]
+    for held in halo:
+        starts.append(starts[-1] + held.shape[0])
     return pl.pallas_call(
-        functools.partial(attention_kernel, chain),
+        functools.partial(attention_kernel, chain, starts, len(joint)),
         out_shape=(
-            jax.ShapeDtypeStruct((ROWS, 2 * GROUP * DIM), jnp.bfloat16),
+            jax.ShapeDtypeStruct((ROWS, QG_WIDE), jnp.bfloat16),
             jax.ShapeDtypeStruct((ROWS, wide), jnp.float32),
-            jax.ShapeDtypeStruct((ROWS, wide), jnp.bfloat16),
-            jax.ShapeDtypeStruct((ROWS, wide), jnp.bfloat16),
-            jax.ShapeDtypeStruct((BLOCK, wide), jnp.bfloat16),
-            jax.ShapeDtypeStruct((BLOCK, wide), jnp.bfloat16),
+            *(jax.ShapeDtypeStruct(held.shape, jnp.bfloat16) for held in halo[1:]),
         ),
-        in_specs=[smem, smem] + [vmem] * 7,
-        out_specs=(vmem,) * 6,
+        in_specs=[smem, smem] + [vmem] * (2 + len(halo) + len(joint)),
+        out_specs=(vmem,) * (1 + len(halo)),
         scratch_shapes=[
-            pltpu.VMEM((SLOTS * BLOCK, wide), jnp.bfloat16),
-            pltpu.VMEM((SLOTS * BLOCK, wide), jnp.float32),
+            pltpu.VMEM((starts[-1], wide), jnp.bfloat16),
+            pltpu.VMEM((starts[-1], wide), jnp.float32),
         ],
         compiler_params=pltpu.CompilerParams(vmem_limit_bytes=32 * 1024 * 1024),
         cost_estimate=pl.CostEstimate(
@@ -286,7 +267,7 @@
             transcendentals=2 * WINDOW * GROUP * BLOCK * BLOCK,
         ),
         name="attention",
-    )(place, pairing, live, qg, *halo)
+    )(place, pairing, live, qg, *halo, *joint)
 
 
 def body(pairing, doc_start, block_live, query, key, value, grad_out):
@@ -300,13 +281,16 @@
     def linear(place):
         return place * 2 if place < pairs else (chain - 1 - place) * 2 + 1
 
-    def steps(by, first_target):
-        return [
-            (linear(s - by), linear(s)) for s in range(first_target, chain) if 0 <= s - by < chain
-        ]
-
-    forth = [steps(1, 0), steps(2, 0), steps(3, pairs), steps(-1, pairs)]
-    back = [[(b, a) for a, b in pairs_of] for pairs_of in forth]
+    def steps(by, targets):
+        return [(linear(s - by), linear(s)) for s in targets if 0 <= s - by < chain]
+
+    early, late = range(pairs), range(pairs, chain)
+    inner = [
+        steps(by, early[: (by < 3) * pairs]) + steps(by, late[max(by, 0) :]) for by in (1, 2, 3)
+    ]
+    inner.append(steps(-1, late))
+    outer = [steps(by, late[:by]) for by in (1, 2, 3)] + [[]]
+    back = [[(b, a) for a, b in one + two] for one, two in zip(inner, outer)]
 
     def move(x, pairs_of):
         return lax.ppermute(x, ("pair", "half"), pairs_of)
@@ -314,25 +298,41 @@
     def exchange(x):
         return lax.all_to_all(x, ("side", "lane"), split_axis=0, concat_axis=0, tiled=True)
 
+    place = jnp.stack([pair, side, half]).astype(jnp.int32)
     later = (half == 0) | (pairing[2 * pair + 1] < pairing[2 * pair])
+    crossed = jnp.any(pairing[1 : chain - 1 : 2] == jnp.arange(2, chain, 2, dtype=jnp.int32))
     own = exchange(pack(key, value)).reshape(ROWS, 2 * DIM)
-    split, later = lax.optimization_barrier(
-        (pack(query, grad_out, doc_start.reshape(1, ROWS)), later)
+    split, later, crossed, place = lax.optimization_barrier(
+        (pack(query, grad_out, doc_start.reshape(1, ROWS)), later, crossed, place)
     )
     split, own = lax.optimization_barrier((split, own))
-    qg = exchange(split).reshape(ROWS, QG_WIDE + DIM)
-    halo = (
+
+    def finish(with_crossed, place, later, pairing, block_live, split, own):
+        sent = [own, own]
+        if with_crossed:
+            sent += [jnp.where(later, own[BLOCK:], own[:BLOCK]), own[BLOCK:]]
+        joint = [move(x, pairs_of) for x, pairs_of in zip(sent, outer) if pairs_of]
+        split, joint = lax.optimization_barrier((split, joint))
+        qg = exchange(split).reshape(ROWS, QG_WIDE + DIM)
+        halo = [own] + [move(x, pairs_of) for x, pairs_of in zip(sent, inner)]
+        od, own_grad, *partials = attention(chain, place, pairing, block_live, qg, halo, joint)
+        order = sorted(range(len(partials)), key=[2, 1, 0, 3].__getitem__)
+        moved = {i: move(partials[i], back[i]) for i in order}
+        partials = [moved[i] for i in range(len(partials))]
+        total = gather(place, pairing, od, (own_grad, *partials))
+        return unpack(exchange(total.reshape(PARTS, PIECE, -1)))
+
+    return lax.cond(
+        crossed,
+        functools.partial(finish, True),
+        functools.partial(finish, False),
+        place,
+        later,
+        pairing,
+        block_live,
+        split,
         own,
-        move(own, forth[0]),
-        move(own, forth[1]),
-        move(jnp.where(later, own[BLOCK:], own[:BLOCK]), forth[2]),
-        move(own[BLOCK:], forth[3]),
     )
-    place = jnp.stack([pair, side, half]).astype(jnp.int32)
-    od, own_grad, *partials = attention(chain, place, pairing, block_live, qg, halo)
-    partials = [move(part, pairs_of) for part, pairs_of in zip(partials, back)]
-    total = gather(place, pairing, od, (own_grad, *partials))
-    return unpack(exchange(total.reshape(PARTS, PIECE, -1)))
 
 
 def solution(mesh):

time: 103 us -> 101 us (0.981)
  the two profiles are of different devices: /device:TPU:23 before, /device:TPU:399 now
where the time goes in v3:
time: 101 us; the launch traced here: 100 us
  starting transfers between devices  30.1 us (30%)
  blocking collectives  29 us (29%)
  waiting for transfers between devices  25.8 us (26%)
  Pallas kernels  10.5 us (10%)
  between operations  2.62 us (3%)
  local copies, waits for them, and re-layouts  1.45 us (1%)
    all_to_all x1, blocking collectives, exchange(): lax.all_to_all(x, ('side', 'lane'), split_axis=0, concat_axis=0, tiled=True)  29 us
    ppermute x6, waiting for transfers between devices, move(): return lax.ppermute(x, ('pair', 'half'), pairs_of)  24 us
    ppermute x6, starting transfers between devices, move(): return lax.ppermute(x, ('pair', 'half'), pairs_of)  16.3 us
    all_to_all x2, starting transfers between devices, exchange(): lax.all_to_all(x, ('side', 'lane'), split_axis=0, concat_axis=0, tiled=True)  13.8 us
    pallas_call x1, Pallas kernels, attention(): pl.pallas_call(functools.partial(attention_kernel, chain, starts, len(joi...  5.12 us
    pallas_call x2, Pallas kernels, pack(): pl.pallas_call(functools.partial(pack_kernel, wide), out_shape=jax.ShapeD...  3.67 us
  transfers between devices with their start and end apart: 8, of which 5 were waited for; matrix products, arithmetic and copies ran while one was open for 2% of the time, Pallas kernels for 2%

profile of v3, /device:TPU:399, one launch (start us, length us, event | category | flops | bytes accessed | tf_op | source)
XLA Modules:
  0.0 100.3 jit_solution(14595171511097007485)
XLA Ops:
  0.6 1.7 %pack.3 = bf16[8,32,256]{2,1,0:T(8,128)(2,1)} custom-call(bf16[32,1024]{1,0:T(8,128)(2,1)} %first_ref.3, bf16[32,1024]{1,0:T(8,128)(2,1)} %second_ref.3), custom_call_target="tpu_custom_call" | custom-call | tf_op jit(solution)/shard_map/pack/pallas_call | solution.py:78
  2.3 7.9 %all-to-all-start.4 = ((bf16[8,32,256]{2,1,0:T(8,128)(2,1)}), bf16[8,32,256]{2,1,0:T(8,128)(2,1)S(1)}, u32[]{:S(2)}, u32[]{:S(2)}) async-start(bf16[8,32,256]{2,1,0:T(8,128)(2,1)} %pack.3), calls=%async_computation.4 | async-start | bytes 262144 | tf_op jit(solution)/shard_map/all_to_all | solution.py:299
  10.2 0.7 copy-done
  10.8 0.1 slice.10
  10.9 0.7 fusion.1
  12.9 2.0 %pack.2 = bf16[8,32,1152]{2,1,0:T(8,128)(2,1)} custom-call(bf16[32,4096]{1,0:T(8,128)(2,1)} %first_ref.2, bf16[32,4096]{1,0:T(8,128)(2,1)} %second_ref.2, s32[1,256]{1,0:T(1,128)} %bitcast.16), custom_call_target="tpu_custom_call" | custom-call | tf_op jit(solution)/shard_map/pack/pallas_call | solution.py:78
  15.0 0.6 compare_reduce_fusion
  16.3 1.8 %all-to-all-done.4 = bf16[8,32,256]{2,1,0:T(8,128)(2,1)S(1)} async-done(((bf16[8,32,256]{2,1,0:T(8,128)(2,1)}), bf16[8,32,256]{2,1,0:T(8,128)(2,1)S(1)}, u32[]{:S(2)}, u32[]{:S(2)}) %all-to-all-start.4) | async-done | bytes 131104 | tf_op jit(solution)/shard_map/all_to_all | solution.py:299
  18.2 82.1 %conditional.1 = ((bf16[32,4096]{1,0:T(8,128)(2,1)}, bf16[32,4096]{1,0:T(8,128)(2,1)}, bf16[32,1024]{1,0:T(8,128)(2,1)}, bf16[32,1024]{1,0:T(8,128)(2,1)})) conditional(s32[]{:T(128)} %convert_element_type.3, (bf16[256,256]{1,0:T(8,128)(2,1)S(1)}, bf16[8,32,1152]{2,1,0:T(8,128)(2,1)}, s32[3]{0:T(128)S(1)}, s32[64]{0:T(128)S(1)}, ...), branch_computations={%region_1.0_spmd, %region_2.3_spmd} | conditional | flops 838893568 | bytes 10944993 | solution.py:325
  18.2 2.5 %collective-permute-start.1 = (bf16[256,256]{1,0:T(8,128)(2,1)S(1)}, bf16[256,256]{1,0:T(8,128)(2,1)S(1)}, u32[]{:S(2)}, u32[]{:S(2)}) collective-permute-start(bf16[256,256]{1,0:T(8,128)(2,1)S(1)} %get-tuple-element.26.refs_0_), channel_id=1, source_target_pairs={{480,500},{496,484},{481,501},{497,485},{482,502},{498,486},{483,5... | collective-permute-start | bytes 393224 | tf_op jit(solution)/shard_map/cond/branch_0_fun/ppermute | solution.py:296
  20.6 0.7 collective-permute-start
  21.3 4.9 %collective-permute-done.1.refs_4_ = bf16[256,256]{1,0:T(8,128)(2,1)S(1)} collective-permute-done((bf16[256,256]{1,0:T(8,128)(2,1)S(1)}, bf16[256,256]{1,0:T(8,128)(2,1)S(1)}, u32[]{:S(2)}, u32[]{:S(2)}) %collective-permute-start.1) | collective-permute-done | bytes 131104 | tf_op jit(solution)/shard_map/cond/branch_0_fun/ppermute | solution.py:296
  26.2 5.9 %all-to-all-start = ((bf16[8,32,1152]{2,1,0:T(8,128)(2,1)}), bf16[8,32,1152]{2,1,0:T(8,128)(2,1)S(1)}, u32[]{:S(2)}, u32[]{:S(2)}) async-start(bf16[8,32,1152]{2,1,0:T(8,128)(2,1)} %get-tuple-element.27), calls=%async_computation | async-start | bytes 1179648 | tf_op jit(solution)/shard_map/cond/branch_0_fun/all_to_all | solution.py:299
  32.1 1.3 %collective-permute-start.3 = (bf16[256,256]{1,0:T(8,128)(2,1)S(1)}, bf16[256,256]{1,0:T(8,128)(2,1)S(1)}, u32[]{:S(2)}, u32[]{:S(2)}) collective-permute-start(bf16[256,256]{1,0:T(8,128)(2,1)S(1)} %get-tuple-element.26.refs_0_), channel_id=1, source_target_pairs={{0,32},{16,48},{32,64},{48,80},{64,96},{80,112},{96,128},{112,144}... | collective-permute-start | bytes 393224 | tf_op jit(solution)/shard_map/cond/branch_0_fun/ppermute | solution.py:296
  33.4 7.8 %collective-permute-start.2 = (bf16[256,256]{1,0:T(8,128)(2,1)S(1)}, bf16[256,256]{1,0:T(8,128)(2,1)S(1)}, u32[]{:S(2)}, u32[]{:S(2)}) collective-permute-start(bf16[256,256]{1,0:T(8,128)(2,1)S(1)} %get-tuple-element.26.refs_0_), channel_id=1, source_target_pairs={{0,16},{16,32},{32,48},{48,64},{64,80},{80,96},{96,112},{112,128},... | collective-permute-start | bytes 393224 | tf_op jit(solution)/shard_map/cond/branch_0_fun/ppermute | solution.py:296
  41.2 5.9 %collective-permute-done.2.refs_1_ = bf16[256,256]{1,0:T(8,128)(2,1)S(1)} collective-permute-done((bf16[256,256]{1,0:T(8,128)(2,1)S(1)}, bf16[256,256]{1,0:T(8,128)(2,1)S(1)}, u32[]{:S(2)}, u32[]{:S(2)}) %collective-permute-start.2) | collective-permute-done | bytes 131104 | tf_op jit(solution)/shard_map/cond/branch_0_fun/ppermute | solution.py:296
  47.2 5.1 %attention.2 = (bf16[256,1024]{1,0:T(8,128)(2,1)S(1)}, f32[256,256]{1,0:T(8,128)S(1)}, bf16[256,256]{1,0:T(8,128)(2,1)S(1)}, bf16[256,256]{1,0:T(8,128)(2,1)S(1)}) custom-call(s32[3]{0:T(128)S(1)} %get-tuple-element.22.place_ref, s32[64]{0:T(128)S(1)} %get-tuple-element.23.pairing_ref, s32[128,128]{1,0:T(8,128)S(1)} %get-tuple-element.24.live_ref, ...), custom_call_target="tpu_custom_call" | custom-call | flops 838860800 | bytes 3145728 | tf_op jit(solution)/shard_map/cond/branch_0_fun/attention/pallas_call | solution.py:250
  52.3 2.1 %collective-permute-start.4 = (bf16[256,256]{1,0:T(8,128)(2,1)S(1)}, bf16[256,256]{1,0:T(8,128)(2,1)S(1)}, u32[]{:S(2)}, u32[]{:S(2)}) collective-permute-start(bf16[256,256]{1,0:T(8,128)(2,1)S(1)} %get-tuple-element.32), channel_id=1, source_target_pairs={{16,0},{32,16},{48,32},{64,48},{80,64},{96,80},{112,96},{128,112},... | collective-permute-start | bytes 393224 | tf_op jit(solution)/shard_map/cond/branch_0_fun/ppermute | solution.py:296
  54.5 1.9 %collective-permute-start.5 = (bf16[256,256]{1,0:T(8,128)(2,1)S(1)}, bf16[256,256]{1,0:T(8,128)(2,1)S(1)}, u32[]{:S(2)}, u32[]{:S(2)}) collective-permute-start(bf16[256,256]{1,0:T(8,128)(2,1)S(1)} %get-tuple-element.33), channel_id=1, source_target_pairs={{32,0},{48,16},{64,32},{80,48},{96,64},{112,80},{128,96},{144,112}... | collective-permute-start | bytes 393224 | tf_op jit(solution)/shard_map/cond/branch_0_fun/ppermute | solution.py:296
  56.4 8.0 %collective-permute-done.4.one_ref = bf16[256,256]{1,0:T(8,128)(2,1)S(1)} collective-permute-done((bf16[256,256]{1,0:T(8,128)(2,1)S(1)}, bf16[256,256]{1,0:T(8,128)(2,1)S(1)}, u32[]{:S(2)}, u32[]{:S(2)}) %collective-permute-start.4) | collective-permute-done | bytes 131104 | tf_op jit(solution)/shard_map/cond/branch_0_fun/ppermute | solution.py:296
  64.4 5.1 %collective-permute-done.5.two_ref = bf16[256,256]{1,0:T(8,128)(2,1)S(1)} collective-permute-done((bf16[256,256]{1,0:T(8,128)(2,1)S(1)}, bf16[256,256]{1,0:T(8,128)(2,1)S(1)}, u32[]{:S(2)}, u32[]{:S(2)}) %collective-permute-start.5) | collective-permute-done | bytes 131104 | tf_op jit(solution)/shard_map/cond/branch_0_fun/ppermute | solution.py:296
  69.5 0.6 gather.2
  70.2 29.0 %all_to_all.21.split_ref = bf16[8,32,1280]{2,1,0:T(8,128)(2,1)S(1)} all-to-all(bf16[8,32,1280]{2,1,0:T(8,128)(2,1)S(1)} %bitcast.11), channel_id=1, replica_groups=mesh['pair'=32,'side'=2,'half'=2,'lane'=4] {'side','lane'}, dimensions={0} | all-to-all | bytes 1310720 | tf_op jit(solution)/shard_map/cond/branch_0_fun/all_to_all | solution.py:299
  99.2 1.1 %unpack.2 = (bf16[32,4096]{1,0:T(8,128)(2,1)}, bf16[32,4096]{1,0:T(8,128)(2,1)}, bf16[32,1024]{1,0:T(8,128)(2,1)}, bf16[32,1024]{1,0:T(8,128)(2,1)}) custom-call(bf16[8,32,1280]{2,1,0:T(8,128)(2,1)S(1)} %all_to_all.21.split_ref), custom_call_target="tpu_custom_call" | custom-call | tf_op jit(solution)/shard_map/cond/branch_0_fun/unpack/pallas_call | solution.py:102
  (7 shorter events, 0.1 us)
Async XLA Ops:
  2.3 15.9 %all-to-all-start.4 = ((bf16[8,32,256]{2,1,0:T(8,128)(2,1)}), bf16[8,32,256]{2,1,0:T(8,128)(2,1)S(1)}, u32[]{:S(2)}, u32[]{:S(2)}) async-start(bf16[8,32,256]{2,1,0:T(8,128)(2,1)} %pack.3), calls=%async_computation.4 | async-start | bytes 262144 | tf_op jit(solution)/shard_map/all_to_all | solution.py:299
  10.2 0.7 copy-start
  12.9 5.2 %copy-start.1 = (s32[128,128]{1,0:T(8,128)S(1)}, s32[128,128]{1,0:T(8,128)}, u32[]{:S(2)}) copy-start(s32[128,128]{1,0:T(8,128)} %param.11) | copy-start | bytes 196612
  18.2 8.1 %collective-permute-start.1 = (bf16[256,256]{1,0:T(8,128)(2,1)S(1)}, bf16[256,256]{1,0:T(8,128)(2,1)S(1)}, u32[]{:S(2)}, u32[]{:S(2)}) collective-permute-start(bf16[256,256]{1,0:T(8,128)(2,1)S(1)} %get-tuple-element.26.refs_0_), channel_id=1, source_target_pairs={{480,500},{496,484},{481,501},{497,485},{482,502},{498,486},{483,5... | collective-permute-start | bytes 393224 | tf_op jit(solution)/shard_map/cond/branch_0_fun/ppermute | solution.py:296
  20.6 5.6 %collective-permute-start = (bf16[256,256]{1,0:T(8,128)(2,1)S(1)}, bf16[256,256]{1,0:T(8,128)(2,1)S(1)}, u32[]{:S(2)}, u32[]{:S(2)}) collective-permute-start(bf16[256,256]{1,0:T(8,128)(2,1)S(1)} %get-tuple-element.26.refs_0_), channel_id=1, source_target_pairs={{496,500},{497,501},{498,502},{499,503},{504,508},{505,509},{506,5... | collective-permute-start | bytes 393224 | tf_op jit(solution)/shard_map/cond/branch_0_fun/ppermute | solution.py:296
  26.2 21.0 %all-to-all-start = ((bf16[8,32,1152]{2,1,0:T(8,128)(2,1)}), bf16[8,32,1152]{2,1,0:T(8,128)(2,1)S(1)}, u32[]{:S(2)}, u32[]{:S(2)}) async-start(bf16[8,32,1152]{2,1,0:T(8,128)(2,1)} %get-tuple-element.27), calls=%async_computation | async-start | bytes 1179648 | tf_op jit(solution)/shard_map/cond/branch_0_fun/all_to_all | solution.py:299
  32.1 9.1 %collective-permute-start.3 = (bf16[256,256]{1,0:T(8,128)(2,1)S(1)}, bf16[256,256]{1,0:T(8,128)(2,1)S(1)}, u32[]{:S(2)}, u32[]{:S(2)}) collective-permute-start(bf16[256,256]{1,0:T(8,128)(2,1)S(1)} %get-tuple-element.26.refs_0_), channel_id=1, source_target_pairs={{0,32},{16,48},{32,64},{48,80},{64,96},{80,112},{96,128},{112,144}... | collective-permute-start | bytes 393224 | tf_op jit(solution)/shard_map/cond/branch_0_fun/ppermute | solution.py:296
  33.4 13.7 %collective-permute-start.2 = (bf16[256,256]{1,0:T(8,128)(2,1)S(1)}, bf16[256,256]{1,0:T(8,128)(2,1)S(1)}, u32[]{:S(2)}, u32[]{:S(2)}) collective-permute-start(bf16[256,256]{1,0:T(8,128)(2,1)S(1)} %get-tuple-element.26.refs_0_), channel_id=1, source_target_pairs={{0,16},{16,32},{32,48},{48,64},{64,80},{80,96},{96,112},{112,128},... | collective-permute-start | bytes 393224 | tf_op jit(solution)/shard_map/cond/branch_0_fun/ppermute | solution.py:296
  52.3 12.1 %collective-permute-start.4 = (bf16[256,256]{1,0:T(8,128)(2,1)S(1)}, bf16[256,256]{1,0:T(8,128)(2,1)S(1)}, u32[]{:S(2)}, u32[]{:S(2)}) collective-permute-start(bf16[256,256]{1,0:T(8,128)(2,1)S(1)} %get-tuple-element.32), channel_id=1, source_target_pairs={{16,0},{32,16},{48,32},{64,48},{80,64},{96,80},{112,96},{128,112},... | collective-permute-start | bytes 393224 | tf_op jit(solution)/shard_map/cond/branch_0_fun/ppermute | solution.py:296
  54.5 15.1 %collective-permute-start.5 = (bf16[256,256]{1,0:T(8,128)(2,1)S(1)}, bf16[256,256]{1,0:T(8,128)(2,1)S(1)}, u32[]{:S(2)}, u32[]{:S(2)}) collective-permute-start(bf16[256,256]{1,0:T(8,128)(2,1)S(1)} %get-tuple-element.33), channel_id=1, source_target_pairs={{32,0},{48,16},{64,32},{80,48},{96,64},{112,80},{128,96},{144,112}... | collective-permute-start | bytes 393224 | tf_op jit(solution)/shard_map/cond/branch_0_fun/ppermute | solution.py:296

commit v4 on v3

--- a/solution.py
+++ b/solution.py
@@ -28,9 +28,26 @@
     )
 
 
+def head_of(place, half):
+    return (place + 2 * half) % PARTS
+
+
 def pieces(whole, split, at, wide):
+    if split.shape[0] == PARTS:
+        half = lax.axis_index("half")
+        heads = [head_of(p, half) for p in range(PARTS)]
+    else:
+        lanes = PARTS // 2
+        heads = [
+            head_of(side * lanes + lane, half)
+            for side in range(2)
+            for half in range(2)
+            for lane in range(lanes)
+        ]
+    columns = [pl.multiple_of(head * wide, wide) for head in heads]
     return [
-        (whole.at[:, pl.ds(h * wide, wide)], split.at[h, :, pl.ds(at, wide)]) for h in range(PARTS)
+        (whole.at[:, pl.ds(column, wide)], split.at[p, :, pl.ds(at, wide)])
+        for p, column in enumerate(columns)
     ]
 
 
@@ -65,10 +82,10 @@
         copy.wait()
 
 
-def pack(first, second, doc=None):
+def pack(first, second, parts, doc=None):
     hbm = pl.BlockSpec(memory_space=pltpu.HBM)
     wide = first.shape[1] // PARTS
-    scratch = [pltpu.SemaphoreType.DMA((2 * PARTS,))]
+    scratch = [pltpu.SemaphoreType.DMA((2 * parts,))]
     arrays = (first, second)
     sent = 2 * wide
     if doc is not None:
@@ -77,7 +94,7 @@
         sent += DIM
     return pl.pallas_call(
         functools.partial(pack_kernel, wide),
-        out_shape=jax.ShapeDtypeStruct((PARTS, PIECE, sent), jnp.bfloat16),
+        out_shape=jax.ShapeDtypeStruct((parts, PIECE, sent), jnp.bfloat16),
         in_specs=[hbm] * len(arrays),
         out_specs=pl.BlockSpec(memory_space=pltpu.VMEM),
         scratch_shapes=scratch,
@@ -152,8 +169,20 @@
 
     for ref, begin, end in zip(held, starts, starts[1:]):
         kv[begin:end, :] = ref[...]
-    for ref, begin, end in zip(joint, starts[1:], starts[2:]):
+    near_ref, *far = joint
+    for ref, begin, end in zip(far, starts[2:], starts[3:]):
         kv[begin:end, :] += ref[...]
+
+    @pl.when(my_place == chain // 2)
+    def _():
+        kv[starts[1] : starts[2], :] = near_ref[...]
+
+    if len(starts) > 4:
+
+        @pl.when(my_place == chain // 2 + 1)
+        def _():
+            kv[starts[3] : starts[4], :] = near_ref[BLOCK:, :]
+
     acc[...] = jnp.zeros_like(acc)
 
     keys_down = lax.broadcasted_iota(jnp.int32, (BLOCK, BLOCK), 0)
@@ -278,22 +307,35 @@
     side = lax.axis_index("side")
     half = lax.axis_index("half")
 
-    def linear(place):
-        return place * 2 if place < pairs else (chain - 1 - place) * 2 + 1
+    axes = ("pair", "side", "half", "lane")
+    lanes = lax.axis_size("lane")
+
+    def device(place, head):
+        in_half = int(place >= pairs)
+        in_pair = chain - 1 - place if in_half else place
+        spot = next(p for p in range(PARTS) if head_of(p, in_half) == head)
+        in_side, in_lane = divmod(spot, lanes)
+        return ((in_pair * 2 + in_side) * 2 + in_half) * lanes + in_lane
 
     def steps(by, targets):
-        return [(linear(s - by), linear(s)) for s in targets if 0 <= s - by < chain]
+        return [
+            (device(s - by, head), device(s, head))
+            for s in targets
+            if 0 <= s - by < chain
+            for head in range(PARTS)
+        ]
 
     early, late = range(pairs), range(pairs, chain)
     inner = [
         steps(by, early[: (by < 3) * pairs]) + steps(by, late[max(by, 0) :]) for by in (1, 2, 3)
     ]
     inner.append(steps(-1, late))
-    outer = [steps(by, late[:by]) for by in (1, 2, 3)] + [[]]
+    outer = [steps(by, late[by == 3 : by]) for by in (1, 2, 3)] + [[]]
+    relay = [steps(1, late[1:2]) + steps(-1, late[:1]), steps(2, late[2:3])]
     back = [[(b, a) for a, b in one + two] for one, two in zip(inner, outer)]
 
     def move(x, pairs_of):
-        return lax.ppermute(x, ("pair", "half"), pairs_of)
+        return lax.ppermute(x, axes, pairs_of)
 
     def exchange(x):
         return lax.all_to_all(x, ("side", "lane"), split_axis=0, concat_axis=0, tiled=True)
@@ -301,20 +343,25 @@
     place = jnp.stack([pair, side, half]).astype(jnp.int32)
     later = (half == 0) | (pairing[2 * pair + 1] < pairing[2 * pair])
     crossed = jnp.any(pairing[1 : chain - 1 : 2] == jnp.arange(2, chain, 2, dtype=jnp.int32))
-    own = exchange(pack(key, value)).reshape(ROWS, 2 * DIM)
+    around = lax.all_to_all(
+        pack(key, value, 2 * PARTS), ("side", "half", "lane"), split_axis=0, concat_axis=0, tiled=True
+    ).reshape(2, 2, BLOCK, 2 * DIM)
+    own = jnp.where(half == 0, around[:, 0], around[:, 1]).reshape(ROWS, 2 * DIM)
+    near = jnp.where(half == 0, around[:, 1], around[:, 0]).reshape(ROWS, 2 * DIM)
     split, later, crossed, place = lax.optimization_barrier(
-        (pack(query, grad_out, doc_start.reshape(1, ROWS)), later, crossed, place)
+        (pack(query, grad_out, PARTS, doc_start.reshape(1, ROWS)), later, crossed, place)
     )
-    split, own = lax.optimization_barrier((split, own))
-
-    def finish(with_crossed, place, later, pairing, block_live, split, own):
+    split, own, near = lax.optimization_barrier((split, own, near))
+
+    def finish(with_crossed, place, later, pairing, block_live, split, own, near):
         sent = [own, own]
         if with_crossed:
             sent += [jnp.where(later, own[BLOCK:], own[:BLOCK]), own[BLOCK:]]
-        joint = [move(x, pairs_of) for x, pairs_of in zip(sent, outer) if pairs_of]
-        split, joint = lax.optimization_barrier((split, joint))
         qg = exchange(split).reshape(ROWS, QG_WIDE + DIM)
         halo = [own] + [move(x, pairs_of) for x, pairs_of in zip(sent, inner)]
+        joint = [near, move(near, relay[0])]
+        if with_crossed:
+            joint.append(move(near[BLOCK:], relay[1]))
         od, own_grad, *partials = attention(chain, place, pairing, block_live, qg, halo, joint)
         order = sorted(range(len(partials)), key=[2, 1, 0, 3].__getitem__)
         moved = {i: move(partials[i], back[i]) for i in order}
@@ -332,6 +379,7 @@
         block_live,
         split,
         own,
+        near,
     )
 
 

time: 101 us -> 96.4 us (0.954)
  the two profiles are of different devices: /device:TPU:399 before, /device:TPU:6 now
where the time goes in v4:
time: 96.4 us; the launch traced here: 95.7 us
  starting transfers between devices  29 us (30%)
  blocking collectives  27 us (28%)
  waiting for transfers between devices  23.2 us (24%)
  Pallas kernels  10.8 us (11%)
  between operations  2.59 us (3%)
  local copies, waits for them, and re-layouts  2.21 us (2%)
    all_to_all x1, blocking collectives, exchange(): lax.all_to_all(x, ('side', 'lane'), split_axis=0, concat_axis=0, tiled=True)  27 us
    ppermute x5, starting transfers between devices, move(): return lax.ppermute(x, axes, pairs_of)  18.3 us
    ppermute x5, waiting for transfers between devices, move(): return lax.ppermute(x, axes, pairs_of)  18.1 us
    all_to_all x1, starting transfers between devices, body(): lax.all_to_all(pack(key, value, 2 * PARTS), ('side', 'half', 'lane'), spl...  7.22 us
    pallas_call x1, Pallas kernels, attention(): pl.pallas_call(functools.partial(attention_kernel, chain, starts, len(joi...  5.18 us
    all_to_all x1, waiting for transfers between devices, body(): lax.all_to_all(pack(key, value, 2 * PARTS), ('side', 'half', 'lane'), spl...  5.11 us
    pallas_call x2, Pallas kernels, pack(): pl.pallas_call(functools.partial(pack_kernel, wide), out_shape=jax.ShapeD...  3.94 us
    all_to_all x1, starting transfers between devices, exchange(): lax.all_to_all(x, ('side', 'lane'), split_axis=0, concat_axis=0, tiled=True)  3.54 us
  transfers between devices with their start and end apart: 7, of which 5 were waited for; matrix products, arithmetic and copies ran while one was open for 2% of the time, Pallas kernels for 2%

profile of v4, /device:TPU:6, one launch (start us, length us, event | category | flops | bytes accessed | tf_op | source)
XLA Modules:
  0.0 95.7 jit_solution(3364995172490632949)
XLA Ops:
  0.6 1.9 %pack.3 = bf16[16,32,256]{2,1,0:T(8,128)(2,1)} custom-call(bf16[32,1024]{1,0:T(8,128)(2,1)} %first_ref.3, bf16[32,1024]{1,0:T(8,128)(2,1)} %second_ref.3), custom_call_target="tpu_custom_call" | custom-call | tf_op jit(solution)/shard_map/pack/pallas_call | solution.py:95
  2.6 7.2 %all-to-all-start.4 = ((bf16[16,32,256]{2,1,0:T(8,128)(2,1)}), bf16[16,32,256]{2,1,0:T(8,128)(2,1)S(1)}, u32[]{:S(2)}, u32[]{:S(2)}) async-start(bf16[16,32,256]{2,1,0:T(8,128)(2,1)} %pack.3), calls=%async_computation.4 | async-start | bytes 524288 | tf_op jit(solution)/shard_map/all_to_all | solution.py:346
  9.8 0.6 copy-done
  10.4 0.1 slice.21
  10.6 0.6 fusion.1
  12.4 2.0 %pack.2 = bf16[8,32,1152]{2,1,0:T(8,128)(2,1)} custom-call(bf16[32,4096]{1,0:T(8,128)(2,1)} %first_ref.2, bf16[32,4096]{1,0:T(8,128)(2,1)} %second_ref.2, s32[1,256]{1,0:T(1,128)} %bitcast.21), custom_call_target="tpu_custom_call" | custom-call | tf_op jit(solution)/shard_map/pack/pallas_call | solution.py:95
  14.6 0.6 compare_reduce_fusion
  15.8 5.1 %all-to-all-done.4 = bf16[16,32,256]{2,1,0:T(8,128)(2,1)S(1)} async-done(((bf16[16,32,256]{2,1,0:T(8,128)(2,1)}), bf16[16,32,256]{2,1,0:T(8,128)(2,1)S(1)}, u32[]{:S(2)}, u32[]{:S(2)}) %all-to-all-start.4) | async-done | bytes 262176 | tf_op jit(solution)/shard_map/all_to_all | solution.py:346
  21.0 0.8 copy-done.1
  21.8 73.9 %conditional.1 = ((bf16[32,4096]{1,0:T(8,128)(2,1)}, bf16[32,4096]{1,0:T(8,128)(2,1)}, bf16[32,1024]{1,0:T(8,128)(2,1)}, bf16[32,1024]{1,0:T(8,128)(2,1)})) conditional(s32[]{:T(128)} %convert_element_type.3, (bf16[8,32,1152]{2,1,0:T(8,128)(2,1)}, bf16[256,256]{1,0:T(8,128)(2,1)S(1)}, bf16[256,256]{1,0:T(8,128)(2,1)S(1)}, s32[3]{0:T(128)S(1)}, ...), branch_computations={%region_1.2_spmd, %region_2.3_spmd} | conditional | flops 838893568 | bytes 10551737 | solution.py:372
  21.8 3.5 %all-to-all-start = ((bf16[8,32,1152]{2,1,0:T(8,128)(2,1)}), bf16[8,32,1152]{2,1,0:T(8,128)(2,1)S(1)}, u32[]{:S(2)}, u32[]{:S(2)}) async-start(bf16[8,32,1152]{2,1,0:T(8,128)(2,1)} %get-tuple-element.29), calls=%async_computation | async-start | bytes 1179648 | tf_op jit(solution)/shard_map/cond/branch_0_fun/all_to_all | solution.py:341
  25.3 0.7 collective-permute-start.2
  26.0 6.1 %collective-permute-start.1 = (bf16[256,256]{1,0:T(8,128)(2,1)S(1)}, bf16[256,256]{1,0:T(8,128)(2,1)S(1)}, u32[]{:S(2)}, u32[]{:S(2)}) collective-permute-start(bf16[256,256]{1,0:T(8,128)(2,1)S(1)} %get-tuple-element.30.refs_0_), channel_id=1, source_target_pairs={{0,32},{1,33},{2,34},{3,35},{8,40},{9,41},{10,42},{11,43},{16,48},... | collective-permute-start | bytes 393224 | tf_op jit(solution)/shard_map/cond/branch_0_fun/ppermute | solution.py:338
  32.1 4.3 %collective-permute-start = (bf16[256,256]{1,0:T(8,128)(2,1)S(1)}, bf16[256,256]{1,0:T(8,128)(2,1)S(1)}, u32[]{:S(2)}, u32[]{:S(2)}) collective-permute-start(bf16[256,256]{1,0:T(8,128)(2,1)S(1)} %get-tuple-element.30.refs_0_), channel_id=1, source_target_pairs={{0,16},{1,17},{2,18},{3,19},{8,24},{9,25},{10,26},{11,27},{16,32},... | collective-permute-start | bytes 393224 | tf_op jit(solution)/shard_map/cond/branch_0_fun/ppermute | solution.py:338
  36.4 5.0 %collective-permute-done.1.refs_2_ = bf16[256,256]{1,0:T(8,128)(2,1)S(1)} collective-permute-done((bf16[256,256]{1,0:T(8,128)(2,1)S(1)}, bf16[256,256]{1,0:T(8,128)(2,1)S(1)}, u32[]{:S(2)}, u32[]{:S(2)}) %collective-permute-start.1) | collective-permute-done | bytes 131104 | tf_op jit(solution)/shard_map/cond/branch_0_fun/ppermute | solution.py:338
  41.5 5.7 %collective-permute-done.refs_1_ = bf16[256,256]{1,0:T(8,128)(2,1)S(1)} collective-permute-done((bf16[256,256]{1,0:T(8,128)(2,1)S(1)}, bf16[256,256]{1,0:T(8,128)(2,1)S(1)}, u32[]{:S(2)}, u32[]{:S(2)}) %collective-permute-start) | collective-permute-done | bytes 131104 | tf_op jit(solution)/shard_map/cond/branch_0_fun/ppermute | solution.py:338
  47.2 5.2 %attention.2 = (bf16[256,1024]{1,0:T(8,128)(2,1)S(1)}, f32[256,256]{1,0:T(8,128)S(1)}, bf16[256,256]{1,0:T(8,128)(2,1)S(1)}, bf16[256,256]{1,0:T(8,128)(2,1)S(1)}) custom-call(s32[3]{0:T(128)S(1)} %get-tuple-element.26.place_ref, s32[64]{0:T(128)S(1)} %get-tuple-element.27.pairing_ref, s32[128,128]{1,0:T(8,128)S(1)} %get-tuple-element.28.live_ref, ...), custom_call_target="tpu_custom_call" | custom-call | flops 838860800 | bytes 3145728 | tf_op jit(solution)/shard_map/cond/branch_0_fun/attention/pallas_call | solution.py:279
  52.4 4.7 %collective-permute-start.3 = (bf16[256,256]{1,0:T(8,128)(2,1)S(1)}, bf16[256,256]{1,0:T(8,128)(2,1)S(1)}, u32[]{:S(2)}, u32[]{:S(2)}) collective-permute-start(bf16[256,256]{1,0:T(8,128)(2,1)S(1)} %get-tuple-element.34), channel_id=1, source_target_pairs={{16,0},{17,1},{18,2},{19,3},{24,8},{25,9},{26,10},{27,11},{32,16},... | collective-permute-start | bytes 393224 | tf_op jit(solution)/shard_map/cond/branch_0_fun/ppermute | solution.py:338
  57.0 2.6 %collective-permute-start.4 = (bf16[256,256]{1,0:T(8,128)(2,1)S(1)}, bf16[256,256]{1,0:T(8,128)(2,1)S(1)}, u32[]{:S(2)}, u32[]{:S(2)}) collective-permute-start(bf16[256,256]{1,0:T(8,128)(2,1)S(1)} %get-tuple-element.35), channel_id=1, source_target_pairs={{32,0},{33,1},{34,2},{35,3},{40,8},{41,9},{42,10},{43,11},{48,16},... | collective-permute-start | bytes 393224 | tf_op jit(solution)/shard_map/cond/branch_0_fun/ppermute | solution.py:338
  59.6 0.2 collective-permute-done.3.one_ref
  59.8 7.2 %collective-permute-done.4.two_ref = bf16[256,256]{1,0:T(8,128)(2,1)S(1)} collective-permute-done((bf16[256,256]{1,0:T(8,128)(2,1)S(1)}, bf16[256,256]{1,0:T(8,128)(2,1)S(1)}, u32[]{:S(2)}, u32[]{:S(2)}) %collective-permute-start.4) | collective-permute-done | bytes 131104 | tf_op jit(solution)/shard_map/cond/branch_0_fun/ppermute | solution.py:338
  67.0 0.6 gather.2
  67.6 27.0 %all_to_all.21.split_ref = bf16[8,32,1280]{2,1,0:T(8,128)(2,1)S(1)} all-to-all(bf16[8,32,1280]{2,1,0:T(8,128)(2,1)S(1)} %bitcast.13), channel_id=1, replica_groups=mesh['pair'=32,'side'=2,'half'=2,'lane'=4] {'side','lane'}, dimensions={0} | all-to-all | bytes 1310720 | tf_op jit(solution)/shard_map/cond/branch_0_fun/all_to_all | solution.py:341
  94.6 1.1 %unpack.2 = (bf16[32,4096]{1,0:T(8,128)(2,1)}, bf16[32,4096]{1,0:T(8,128)(2,1)}, bf16[32,1024]{1,0:T(8,128)(2,1)}, bf16[32,1024]{1,0:T(8,128)(2,1)}) custom-call(bf16[8,32,1280]{2,1,0:T(8,128)(2,1)S(1)} %all_to_all.21.split_ref), custom_call_target="tpu_custom_call" | custom-call | tf_op jit(solution)/shard_map/cond/branch_0_fun/unpack/pallas_call | solution.py:119
  (6 shorter events, 0.1 us)
Async XLA Ops:
  2.6 18.4 %all-to-all-start.4 = ((bf16[16,32,256]{2,1,0:T(8,128)(2,1)}), bf16[16,32,256]{2,1,0:T(8,128)(2,1)S(1)}, u32[]{:S(2)}, u32[]{:S(2)}) async-start(bf16[16,32,256]{2,1,0:T(8,128)(2,1)} %pack.3), calls=%async_computation.4 | async-start | bytes 524288 | tf_op jit(solution)/shard_map/all_to_all | solution.py:346
  9.8 0.7 copy-start
  21.0 0.8 copy-start.1
  21.8 25.4 %all-to-all-start = ((bf16[8,32,1152]{2,1,0:T(8,128)(2,1)}), bf16[8,32,1152]{2,1,0:T(8,128)(2,1)S(1)}, u32[]{:S(2)}, u32[]{:S(2)}) async-start(bf16[8,32,1152]{2,1,0:T(8,128)(2,1)} %get-tuple-element.29), calls=%async_computation | async-start | bytes 1179648 | tf_op jit(solution)/shard_map/cond/branch_0_fun/all_to_all | solution.py:341
  25.3 11.1 %collective-permute-start.2 = (bf16[256,256]{1,0:T(8,128)(2,1)S(1)}, bf16[256,256]{1,0:T(8,128)(2,1)S(1)}, u32[]{:S(2)}, u32[]{:S(2)}) collective-permute-start(bf16[256,256]{1,0:T(8,128)(2,1)S(1)} %get-tuple-element.31.refs_3_), channel_id=1, source_target_pairs={{510,494},{511,495},{500,484},{501,485},{502,486},{503,487},{508,4... | collective-permute-start | bytes 393224 | tf_op jit(solution)/shard_map/cond/branch_0_fun/ppermute | solution.py:338
  26.0 15.4 %collective-permute-start.1 = (bf16[256,256]{1,0:T(8,128)(2,1)S(1)}, bf16[256,256]{1,0:T(8,128)(2,1)S(1)}, u32[]{:S(2)}, u32[]{:S(2)}) collective-permute-start(bf16[256,256]{1,0:T(8,128)(2,1)S(1)} %get-tuple-element.30.refs_0_), channel_id=1, source_target_pairs={{0,32},{1,33},{2,34},{3,35},{8,40},{9,41},{10,42},{11,43},{16,48},... | collective-permute-start | bytes 393224 | tf_op jit(solution)/shard_map/cond/branch_0_fun/ppermute | solution.py:338
  32.1 15.1 %collective-permute-start = (bf16[256,256]{1,0:T(8,128)(2,1)S(1)}, bf16[256,256]{1,0:T(8,128)(2,1)S(1)}, u32[]{:S(2)}, u32[]{:S(2)}) collective-permute-start(bf16[256,256]{1,0:T(8,128)(2,1)S(1)} %get-tuple-element.30.refs_0_), channel_id=1, source_target_pairs={{0,16},{1,17},{2,18},{3,19},{8,24},{9,25},{10,26},{11,27},{16,32},... | collective-permute-start | bytes 393224 | tf_op jit(solution)/shard_map/cond/branch_0_fun/ppermute | solution.py:338
  52.4 7.4 %collective-permute-start.3 = (bf16[256,256]{1,0:T(8,128)(2,1)S(1)}, bf16[256,256]{1,0:T(8,128)(2,1)S(1)}, u32[]{:S(2)}, u32[]{:S(2)}) collective-permute-start(bf16[256,256]{1,0:T(8,128)(2,1)S(1)} %get-tuple-element.34), channel_id=1, source_target_pairs={{16,0},{17,1},{18,2},{19,3},{24,8},{25,9},{26,10},{27,11},{32,16},... | collective-permute-start | bytes 393224 | tf_op jit(solution)/shard_map/cond/branch_0_fun/ppermute | solution.py:338
  57.0 9.9 %collective-permute-start.4 = (bf16[256,256]{1,0:T(8,128)(2,1)S(1)}, bf16[256,256]{1,0:T(8,128)(2,1)S(1)}, u32[]{:S(2)}, u32[]{:S(2)}) collective-permute-start(bf16[256,256]{1,0:T(8,128)(2,1)S(1)} %get-tuple-element.35), channel_id=1, source_target_pairs={{32,0},{33,1},{34,2},{35,3},{40,8},{41,9},{42,10},{43,11},{48,16},... | collective-permute-start | bytes 393224 | tf_op jit(solution)/shard_map/cond/branch_0_fun/ppermute | solution.py:338

commit v5 on v3

--- a/solution.py
+++ b/solution.py
@@ -20,6 +20,7 @@
 NEGATIVE = -1e30
 QUERY_WIDE = GROUP * DIM
 QG_WIDE = 2 * QUERY_WIDE
+WIDE = QG_WIDE + 2 * DIM
 
 
 def dot(a, b, over_a, over_b):
@@ -28,9 +29,16 @@
     )
 
 
+def head_of(place, half):
+    return (place + 2 * half) % PARTS
+
+
 def pieces(whole, split, at, wide):
+    half = lax.axis_index("half")
+    columns = [pl.multiple_of(head_of(p, half) * wide, wide) for p in range(PARTS)]
     return [
-        (whole.at[:, pl.ds(h * wide, wide)], split.at[h, :, pl.ds(at, wide)]) for h in range(PARTS)
+        (whole.at[:, pl.ds(column, wide)], split.at[p, :, pl.ds(at, wide)])
+        for p, column in enumerate(columns)
     ]
 
 
@@ -42,48 +50,40 @@
     ]
 
 
-def pack_kernel(wide, first_ref, second_ref, *refs):
-    if len(refs) == 2:
-        out_ref, sems = refs
-    else:
-        doc_ref, out_ref, sems, doc_here, doc_sem = refs
-        doc_copy = pltpu.make_async_copy(doc_ref, doc_here, doc_sem)
-        doc_copy.start()
-    copies = copies_of(first_ref, second_ref, out_ref, 0, wide, sems, True)
+def pack_kernel(doc_ref, q_ref, g_ref, k_ref, v_ref, out_ref, doc_here, sems, doc_sem):
+    doc_copy = pltpu.make_async_copy(doc_ref, doc_here, doc_sem)
+    doc_copy.start()
+    copies = copies_of(q_ref, g_ref, out_ref, 0, QUERY_WIDE, sems, True)
+    copies += copies_of(k_ref, v_ref, out_ref, QG_WIDE, DIM, sems.at[2 * PARTS :], True)
     for copy in copies:
         copy.start()
-    if len(refs) > 2:
-        doc_copy.wait()
-        doc = doc_here[...]
-        line = lax.broadcasted_iota(jnp.int32, (PIECE, BLOCK), 0)
-        coded = jnp.where(line < 2, doc[:, :BLOCK], doc[:, BLOCK:])
-        coded = jnp.where(line % 2 == 0, coded // BLOCK, coded % BLOCK)
-        coded = coded.astype(jnp.float32).astype(jnp.bfloat16)
-        for h in range(PARTS):
-            out_ref[h, :, 2 * wide :] = coded
+    doc_copy.wait()
+    doc = doc_here[...]
+    line = lax.broadcasted_iota(jnp.int32, (PIECE, BLOCK), 0)
+    coded = jnp.where(line < 2, doc[:, :BLOCK], doc[:, BLOCK:])
+    coded = jnp.where(line % 2 == 0, coded // BLOCK, coded % BLOCK)
+    coded = coded.astype(jnp.float32).astype(jnp.bfloat16)
+    for p in range(PARTS):
+        out_ref[p, :, WIDE:] = coded
     for copy in copies:
         copy.wait()
 
 
-def pack(first, second, doc=None):
+def pack(doc, query, grad_out, key, value):
     hbm = pl.BlockSpec(memory_space=pltpu.HBM)
-    wide = first.shape[1] // PARTS
-    scratch = [pltpu.SemaphoreType.DMA((2 * PARTS,))]
-    arrays = (first, second)
-    sent = 2 * wide
-    if doc is not None:
-        scratch += [pltpu.VMEM((1, ROWS), jnp.int32), pltpu.SemaphoreType.DMA]
-        arrays += (doc,)
-        sent += DIM
     return pl.pallas_call(
-        functools.partial(pack_kernel, wide),
-        out_shape=jax.ShapeDtypeStruct((PARTS, PIECE, sent), jnp.bfloat16),
-        in_specs=[hbm] * len(arrays),
+        pack_kernel,
+        out_shape=jax.ShapeDtypeStruct((PARTS, PIECE, WIDE + DIM), jnp.bfloat16),
+        in_specs=[hbm] * 5,
         out_specs=pl.BlockSpec(memory_space=pltpu.VMEM),
-        scratch_shapes=scratch,
+        scratch_shapes=[
+            pltpu.VMEM((1, ROWS), jnp.int32),
+            pltpu.SemaphoreType.DMA((4 * PARTS,)),
+            pltpu.SemaphoreType.DMA,
+        ],
         compiler_params=pltpu.CompilerParams(vmem_limit_bytes=(63 * 1024 + 256) * 1024),
         name="pack",
-    )(*arrays)
+    )(doc, query, grad_out, key, value)
 
 
 def unpack_kernel(split_ref, att_ref, dq_ref, dk_ref, dv_ref, sems):
@@ -139,10 +139,9 @@
     )(place, pairing, od, *parts)
 
 
-def attention_kernel(chain, starts, joints, place_ref, pairing_ref, live_ref, qg_ref, *refs):
+def attention_kernel(chain, starts, place_ref, pairing_ref, live_ref, qg_ref, *refs):
     held = refs[: len(starts) - 1]
-    joint = refs[len(starts) - 1 : len(starts) - 1 + joints]
-    od_ref, *parts, kv, acc = refs[len(starts) - 1 + joints :]
+    od_ref, *parts, kv, acc = refs[len(starts) - 1 :]
     pair = place_ref[0]
     half = place_ref[2]
     blocks = 2 * chain
@@ -152,8 +151,6 @@
 
     for ref, begin, end in zip(held, starts, starts[1:]):
         kv[begin:end, :] = ref[...]
-    for ref, begin, end in zip(joint, starts[1:], starts[2:]):
-        kv[begin:end, :] += ref[...]
     acc[...] = jnp.zeros_like(acc)
 
     keys_down = lax.broadcasted_iota(jnp.int32, (BLOCK, BLOCK), 0)
@@ -163,7 +160,7 @@
     for b in range(2):
         holder = 2 * pair + b
         block = jnp.where(half == 0, holder, blocks - 1 - pairing_ref[holder])
-        doc = qg_ref[b * BLOCK : b * BLOCK + PIECE, QG_WIDE:].astype(jnp.float32)
+        doc = qg_ref[b * BLOCK : b * BLOCK + PIECE, WIDE:].astype(jnp.float32)
         doc = jnp.where(half == 0, doc[0:2], doc[2:4])
         begins = (doc[0:1] * BLOCK + doc[1:2]).astype(jnp.int32)
         live_row = live_ref[pl.ds(block, 1), :]
@@ -240,7 +237,7 @@
         ref[...] = acc[begin:end, :].astype(ref.dtype)
 
 
-def attention(chain, place, pairing, live, qg, halo, joint):
+def attention(chain, place, pairing, live, qg, halo):
     wide = 2 * DIM
     vmem = pl.BlockSpec(memory_space=pltpu.VMEM)
     smem = pl.BlockSpec(memory_space=pltpu.SMEM)
@@ -248,13 +245,13 @@
     for held in halo:
         starts.append(starts[-1] + held.shape[0])
     return pl.pallas_call(
-        functools.partial(attention_kernel, chain, starts, len(joint)),
+        functools.partial(attention_kernel, chain, starts),
         out_shape=(
             jax.ShapeDtypeStruct((ROWS, QG_WIDE), jnp.bfloat16),
             jax.ShapeDtypeStruct((ROWS, wide), jnp.float32),
             *(jax.ShapeDtypeStruct(held.shape, jnp.bfloat16) for held in halo[1:]),
         ),
-        in_specs=[smem, smem] + [vmem] * (2 + len(halo) + len(joint)),
+        in_specs=[smem, smem] + [vmem] * (2 + len(halo)),
         out_specs=(vmem,) * (1 + len(halo)),
         scratch_shapes=[
             pltpu.VMEM((starts[-1], wide), jnp.bfloat16),
@@ -267,7 +264,7 @@
             transcendentals=2 * WINDOW * GROUP * BLOCK * BLOCK,
         ),
         name="attention",
-    )(place, pairing, live, qg, *halo, *joint)
+    )(place, pairing, live, qg, *halo)
 
 
 def body(pairing, doc_start, block_live, query, key, value, grad_out):
@@ -278,47 +275,53 @@
     side = lax.axis_index("side")
     half = lax.axis_index("half")
 
-    def linear(place):
-        return place * 2 if place < pairs else (chain - 1 - place) * 2 + 1
+    axes = ("pair", "side", "half", "lane")
+    lanes = lax.axis_size("lane")
+
+    def device(place, head):
+        in_half = int(place >= pairs)
+        in_pair = chain - 1 - place if in_half else place
+        spot = next(p for p in range(PARTS) if head_of(p, in_half) == head)
+        in_side, in_lane = divmod(spot, lanes)
+        return ((in_pair * 2 + in_side) * 2 + in_half) * lanes + in_lane
 
     def steps(by, targets):
-        return [(linear(s - by), linear(s)) for s in targets if 0 <= s - by < chain]
-
-    early, late = range(pairs), range(pairs, chain)
-    inner = [
-        steps(by, early[: (by < 3) * pairs]) + steps(by, late[max(by, 0) :]) for by in (1, 2, 3)
+        return [
+            (device(s - by, head), device(s, head))
+            for s in targets
+            if 0 <= s - by < chain
+            for head in range(PARTS)
+        ]
+
+    forth = [
+        steps(1, range(chain)),
+        steps(2, range(chain)),
+        steps(3, range(pairs + 1, chain)),
+        steps(-1, range(pairs, chain)),
     ]
-    inner.append(steps(-1, late))
-    outer = [steps(by, late[:by]) for by in (1, 2, 3)] + [[]]
-    back = [[(b, a) for a, b in one + two] for one, two in zip(inner, outer)]
+    back = [[(b, a) for a, b in pairs_of] for pairs_of in forth]
 
     def move(x, pairs_of):
-        return lax.ppermute(x, ("pair", "half"), pairs_of)
+        return lax.ppermute(x, axes, pairs_of)
 
     def exchange(x):
         return lax.all_to_all(x, ("side", "lane"), split_axis=0, concat_axis=0, tiled=True)
 
     place = jnp.stack([pair, side, half]).astype(jnp.int32)
+    split = pack(doc_start.reshape(1, ROWS), query, grad_out, key, value)
+    split, pairing = lax.optimization_barrier((split, pairing))
     later = (half == 0) | (pairing[2 * pair + 1] < pairing[2 * pair])
     crossed = jnp.any(pairing[1 : chain - 1 : 2] == jnp.arange(2, chain, 2, dtype=jnp.int32))
-    own = exchange(pack(key, value)).reshape(ROWS, 2 * DIM)
-    split, later, crossed, place = lax.optimization_barrier(
-        (pack(query, grad_out, doc_start.reshape(1, ROWS)), later, crossed, place)
-    )
-    split, own = lax.optimization_barrier((split, own))
-
-    def finish(with_crossed, place, later, pairing, block_live, split, own):
-        sent = [own, own]
+    arrived = exchange(split).reshape(ROWS, WIDE + DIM)
+
+    def finish(with_crossed, place, later, pairing, block_live, arrived):
+        own = arrived[:, QG_WIDE:WIDE]
+        halo = [own, move(own, forth[0]), move(own, forth[1])]
         if with_crossed:
-            sent += [jnp.where(later, own[BLOCK:], own[:BLOCK]), own[BLOCK:]]
-        joint = [move(x, pairs_of) for x, pairs_of in zip(sent, outer) if pairs_of]
-        split, joint = lax.optimization_barrier((split, joint))
-        qg = exchange(split).reshape(ROWS, QG_WIDE + DIM)
-        halo = [own] + [move(x, pairs_of) for x, pairs_of in zip(sent, inner)]
-        od, own_grad, *partials = attention(chain, place, pairing, block_live, qg, halo, joint)
-        order = sorted(range(len(partials)), key=[2, 1, 0, 3].__getitem__)
-        moved = {i: move(partials[i], back[i]) for i in order}
-        partials = [moved[i] for i in range(len(partials))]
+            halo.append(move(jnp.where(later, own[BLOCK:], own[:BLOCK]), forth[2]))
+            halo.append(move(own[BLOCK:], forth[3]))
+        od, own_grad, *partials = attention(chain, place, pairing, block_live, arrived, halo)
+        partials = [move(part, pairs_of) for part, pairs_of in zip(partials, back)]
         total = gather(place, pairing, od, (own_grad, *partials))
         return unpack(exchange(total.reshape(PARTS, PIECE, -1)))
 
@@ -330,8 +333,7 @@
         later,
         pairing,
         block_live,
-        split,
-        own,
+        arrived,
     )
 
 

time: 101 us -> 103 us (1.020)
  the two profiles are of different devices: /device:TPU:399 before, /device:TPU:23 now
where the time goes in v5:
time: 103 us; the launch traced here: 102 us
  starting transfers between devices  40.4 us (39%)
  waiting for transfers between devices  27.3 us (27%)
  blocking collectives  20.2 us (20%)
  Pallas kernels  9.17 us (9%)
  loops' own time  1.42 us (1%)
  local copies, waits for them, and re-layouts  1.38 us (1%)
  between operations  1.3 us (1%)
    ppermute x8, starting transfers between devices, move(): return lax.ppermute(x, axes, pairs_of)  34.3 us
    all_to_all x1, blocking collectives, exchange(): lax.all_to_all(x, ('side', 'lane'), split_axis=0, concat_axis=0, tiled=True)  20.2 us
    all_to_all x1, waiting for transfers between devices, exchange(): lax.all_to_all(x, ('side', 'lane'), split_axis=0, concat_axis=0, tiled=True)  19.6 us
    ppermute x8, waiting for transfers between devices, move(): return lax.ppermute(x, axes, pairs_of)  7.79 us
    all_to_all x1, starting transfers between devices, exchange(): lax.all_to_all(x, ('side', 'lane'), split_axis=0, concat_axis=0, tiled=True)  6.12 us
    pallas_call x1, Pallas kernels, attention(): pl.pallas_call(functools.partial(attention_kernel, chain, starts), out_sh...  5.15 us
    pallas_call x1, Pallas kernels, pack(): pl.pallas_call(pack_kernel, out_shape=jax.ShapeDtypeStruct((PARTS, PIECE,...  2.26 us
  transfers between devices with their start and end apart: 9, of which 5 were waited for; matrix products, arithmetic and copies ran while one was open for 1% of the time, Pallas kernels for 0%

profile of v5, /device:TPU:23, one launch (start us, length us, event | category | flops | bytes accessed | tf_op | source)
XLA Modules:
  0.0 102.0 jit_solution(14815584556726358372)
XLA Ops:
  0.6 2.3 %pack.1 = bf16[8,32,1408]{2,1,0:T(8,128)(2,1)} custom-call(s32[1,256]{1,0:T(1,128)} %bitcast.12, bf16[32,4096]{1,0:T(8,128)(2,1)} %q_ref.1, bf16[32,4096]{1,0:T(8,128)(2,1)} %g_ref.1, bf16[32,1024]{1,0:T(8,128)(2,1)} %k_ref.1, bf16[32,1024]{1,0:T(8,128)(2,1)} %v_ref.1), custom_call_target="tpu_custom_call" | custom-call | tf_op jit(solution)/shard_map/pack/pallas_call | solution.py:74
  2.9 6.1 %all-to-all-start.2 = ((bf16[8,32,1408]{2,1,0:T(8,128)(2,1)}), bf16[8,32,1408]{2,1,0:T(8,128)(2,1)S(1)}, u32[]{:S(2)}, u32[]{:S(2)}) async-start(bf16[8,32,1408]{2,1,0:T(8,128)(2,1)} %pack.1), calls=%async_computation.2 | async-start | bytes 1441792 | tf_op jit(solution)/shard_map/all_to_all | solution.py:308
  9.0 0.7 copy-done
  9.7 0.1 slice.18
  9.8 0.6 compare_reduce_fusion
  11.2 19.6 %all-to-all-done.2 = bf16[8,32,1408]{2,1,0:T(8,128)(2,1)S(1)} async-done(((bf16[8,32,1408]{2,1,0:T(8,128)(2,1)}), bf16[8,32,1408]{2,1,0:T(8,128)(2,1)S(1)}, u32[]{:S(2)}, u32[]{:S(2)}) %all-to-all-start.2) | async-done | bytes 720928 | tf_op jit(solution)/shard_map/all_to_all | solution.py:308
  30.7 71.3 %conditional.1 = ((bf16[32,4096]{1,0:T(8,128)(2,1)}, bf16[32,4096]{1,0:T(8,128)(2,1)}, bf16[32,1024]{1,0:T(8,128)(2,1)}, bf16[32,1024]{1,0:T(8,128)(2,1)})) conditional(s32[]{:T(128)} %convert_element_type.3, (bf16[256,1408]{1,0:T(8,128)(2,1)S(1)}, s32[3]{0:T(128)S(1)}, s32[64]{0:T(128)S(1)}, s32[128,128]{1,0:T(8,128)S(1)}) %tuple.47, ...), branch_computations={%region_1.0_spmd, %region_2.3_spmd} | conditional | flops 838893568 | bytes 8126930 | solution.py:328
  30.8 10.9 %collective-permute-start.5 = (bf16[256,256]{1,0:T(8,128)(2,1)S(1)}, bf16[256,256]{1,0:T(8,128)(2,1)S(1)}, u32[]{:S(2)}, u32[]{:S(2)}) collective-permute-start(bf16[256,256]{1,0:T(8,128)(2,1)S(1)} %slice.14.refs_0_), channel_id=1, source_target_pairs={{0,32},{1,33},{2,34},{3,35},{8,40},{9,41},{10,42},{11,43},{16,48},... | collective-permute-start | bytes 393224 | tf_op jit(solution)/shard_map/cond/branch_1_fun/ppermute | solution.py:305
  41.7 2.2 %collective-permute-start.4 = (bf16[256,256]{1,0:T(8,128)(2,1)S(1)}, bf16[256,256]{1,0:T(8,128)(2,1)S(1)}, u32[]{:S(2)}, u32[]{:S(2)}) collective-permute-start(bf16[256,256]{1,0:T(8,128)(2,1)S(1)} %slice.14.refs_0_), channel_id=1, source_target_pairs={{0,16},{1,17},{2,18},{3,19},{8,24},{9,25},{10,26},{11,27},{16,32},... | collective-permute-start | bytes 393224 | tf_op jit(solution)/shard_map/cond/branch_1_fun/ppermute | solution.py:305
  43.9 0.6 fusion.1
  45.8 3.1 %collective-permute-start.7 = (bf16[128,256]{1,0:T(8,128)(2,1)S(1)}, bf16[128,256]{1,0:T(8,128)(2,1)S(1)}, u32[]{:S(2)}, u32[]{:S(2)}) collective-permute-start(bf16[128,256]{1,0:T(8,128)(2,1)S(1)} %get-tuple-element.89), channel_id=1, source_target_pairs={{494,510},{495,511},{484,500},{485,501},{486,502},{487,503},{492,5... | collective-permute-start | bytes 196616 | tf_op jit(solution)/shard_map/cond/branch_1_fun/ppermute | solution.py:305
  48.9 1.9 %collective-permute-start.6 = (bf16[128,256]{1,0:T(8,128)(2,1)S(1)}, bf16[128,256]{1,0:T(8,128)(2,1)S(1)}, u32[]{:S(2)}, u32[]{:S(2)}) collective-permute-start(bf16[128,256]{1,0:T(8,128)(2,1)S(1)} %get-tuple-element.90), channel_id=1, source_target_pairs={{480,494},{481,495},{482,484},{483,485},{488,486},{489,487},{490,4... | collective-permute-start | bytes 196616 | tf_op jit(solution)/shard_map/cond/branch_1_fun/ppermute | solution.py:305
  50.8 2.1 %collective-permute-done.7.refs_4_ = bf16[128,256]{1,0:T(8,128)(2,1)S(1)} collective-permute-done((bf16[128,256]{1,0:T(8,128)(2,1)S(1)}, bf16[128,256]{1,0:T(8,128)(2,1)S(1)}, u32[]{:S(2)}, u32[]{:S(2)}) %collective-permute-start.7) | collective-permute-done | bytes 65568 | tf_op jit(solution)/shard_map/cond/branch_1_fun/ppermute | solution.py:305
  52.9 2.8 %collective-permute-done.6.refs_3_ = bf16[128,256]{1,0:T(8,128)(2,1)S(1)} collective-permute-done((bf16[128,256]{1,0:T(8,128)(2,1)S(1)}, bf16[128,256]{1,0:T(8,128)(2,1)S(1)}, u32[]{:S(2)}, u32[]{:S(2)}) %collective-permute-start.6) | collective-permute-done | bytes 65568 | tf_op jit(solution)/shard_map/cond/branch_1_fun/ppermute | solution.py:305
  55.8 5.1 %attention.3 = (bf16[256,1024]{1,0:T(8,128)(2,1)S(1)}, f32[256,256]{1,0:T(8,128)S(1)}, bf16[256,256]{1,0:T(8,128)(2,1)S(1)}, bf16[256,256]{1,0:T(8,128)(2,1)S(1)...) custom-call(s32[3]{0:T(128)S(1)} %get-tuple-element.57.place_ref, s32[64]{0:T(128)S(1)} %get-tuple-element.58.pairing_ref, ...), custom_call_target="tpu_custom_call" | custom-call | flops 838860800 | bytes 3145728 | tf_op jit(solution)/shard_map/cond/branch_1_fun/attention/pallas_call | solution.py:247
  60.9 5.1 %collective-permute-start.8 = (bf16[256,256]{1,0:T(8,128)(2,1)S(1)}, bf16[256,256]{1,0:T(8,128)(2,1)S(1)}, u32[]{:S(2)}, u32[]{:S(2)}) collective-permute-start(bf16[256,256]{1,0:T(8,128)(2,1)S(1)} %get-tuple-element.65), channel_id=1, source_target_pairs={{16,0},{17,1},{18,2},{19,3},{24,8},{25,9},{26,10},{27,11},{32,16},... | collective-permute-start | bytes 393224 | tf_op jit(solution)/shard_map/cond/branch_1_fun/ppermute | solution.py:305
  66.1 1.9 %collective-permute-start.9 = (bf16[256,256]{1,0:T(8,128)(2,1)S(1)}, bf16[256,256]{1,0:T(8,128)(2,1)S(1)}, u32[]{:S(2)}, u32[]{:S(2)}) collective-permute-start(bf16[256,256]{1,0:T(8,128)(2,1)S(1)} %get-tuple-element.66), channel_id=1, source_target_pairs={{32,0},{33,1},{34,2},{35,3},{40,8},{41,9},{42,10},{43,11},{48,16},... | collective-permute-start | bytes 393224 | tf_op jit(solution)/shard_map/cond/branch_1_fun/ppermute | solution.py:305
  68.0 3.9 %collective-permute-start.10 = (bf16[128,256]{1,0:T(8,128)(2,1)S(1)}, bf16[128,256]{1,0:T(8,128)(2,1)S(1)}, u32[]{:S(2)}, u32[]{:S(2)}) collective-permute-start(bf16[128,256]{1,0:T(8,128)(2,1)S(1)} %get-tuple-element.67), channel_id=1, source_target_pairs={{494,480},{495,481},{484,482},{485,483},{486,488},{487,489},{492,4... | collective-permute-start | bytes 196616 | tf_op jit(solution)/shard_map/cond/branch_1_fun/ppermute | solution.py:305
  71.9 5.2 %collective-permute-start.11 = (bf16[128,256]{1,0:T(8,128)(2,1)S(1)}, bf16[128,256]{1,0:T(8,128)(2,1)S(1)}, u32[]{:S(2)}, u32[]{:S(2)}) collective-permute-start(bf16[128,256]{1,0:T(8,128)(2,1)S(1)} %get-tuple-element.68), channel_id=1, source_target_pairs={{510,494},{511,495},{500,484},{501,485},{502,486},{503,487},{508,4... | collective-permute-start | bytes 196616 | tf_op jit(solution)/shard_map/cond/branch_1_fun/ppermute | solution.py:305
  77.2 1.3 %collective-permute-done.11.refs_1_ = bf16[128,256]{1,0:T(8,128)(2,1)S(1)} collective-permute-done((bf16[128,256]{1,0:T(8,128)(2,1)S(1)}, bf16[128,256]{1,0:T(8,128)(2,1)S(1)}, u32[]{:S(2)}, u32[]{:S(2)}) %collective-permute-start.11) | collective-permute-done | bytes 65568 | tf_op jit(solution)/shard_map/cond/branch_1_fun/ppermute | solution.py:305
  78.5 1.6 %collective-permute-done.9.two_ref = bf16[256,256]{1,0:T(8,128)(2,1)S(1)} collective-permute-done((bf16[256,256]{1,0:T(8,128)(2,1)S(1)}, bf16[256,256]{1,0:T(8,128)(2,1)S(1)}, u32[]{:S(2)}, u32[]{:S(2)}) %collective-permute-start.9) | collective-permute-done | bytes 131104 | tf_op jit(solution)/shard_map/cond/branch_1_fun/ppermute | solution.py:305
  80.0 0.6 gather.3
  80.7 20.2 %all_to_all.14.split_ref = bf16[8,32,1280]{2,1,0:T(8,128)(2,1)S(1)} all-to-all(bf16[8,32,1280]{2,1,0:T(8,128)(2,1)S(1)} %bitcast.8), channel_id=1, replica_groups=mesh['pair'=32,'side'=2,'half'=2,'lane'=4] {'side','lane'}, dimensions={0} | all-to-all | bytes 1310720 | tf_op jit(solution)/shard_map/cond/branch_1_fun/all_to_all | solution.py:308
  100.9 1.1 %unpack.3 = (bf16[32,4096]{1,0:T(8,128)(2,1)}, bf16[32,4096]{1,0:T(8,128)(2,1)}, bf16[32,1024]{1,0:T(8,128)(2,1)}, bf16[32,1024]{1,0:T(8,128)(2,1)}) custom-call(bf16[8,32,1280]{2,1,0:T(8,128)(2,1)S(1)} %all_to_all.14.split_ref), custom_call_target="tpu_custom_call" | custom-call | tf_op jit(solution)/shard_map/cond/branch_1_fun/unpack/pallas_call | solution.py:102
  (10 shorter events, 0.1 us)
Async XLA Ops:
  2.9 27.8 %copy-start.1 = (s32[128,128]{1,0:T(8,128)S(1)}, s32[128,128]{1,0:T(8,128)}, u32[]{:S(2)}) copy-start(s32[128,128]{1,0:T(8,128)} %param.11) | copy-start | bytes 196612
  2.9 27.8 %all-to-all-start.2 = ((bf16[8,32,1408]{2,1,0:T(8,128)(2,1)}), bf16[8,32,1408]{2,1,0:T(8,128)(2,1)S(1)}, u32[]{:S(2)}, u32[]{:S(2)}) async-start(bf16[8,32,1408]{2,1,0:T(8,128)(2,1)} %pack.1), calls=%async_computation.2 | async-start | bytes 1441792 | tf_op jit(solution)/shard_map/all_to_all | solution.py:308
  9.0 0.7 copy-start
  30.8 25.0 %collective-permute-start.5 = (bf16[256,256]{1,0:T(8,128)(2,1)S(1)}, bf16[256,256]{1,0:T(8,128)(2,1)S(1)}, u32[]{:S(2)}, u32[]{:S(2)}) collective-permute-start(bf16[256,256]{1,0:T(8,128)(2,1)S(1)} %slice.14.refs_0_), channel_id=1, source_target_pairs={{0,32},{1,33},{2,34},{3,35},{8,40},{9,41},{10,42},{11,43},{16,48},... | collective-permute-start | bytes 393224 | tf_op jit(solution)/shard_map/cond/branch_1_fun/ppermute | solution.py:305
  41.7 14.1 %collective-permute-start.4 = (bf16[256,256]{1,0:T(8,128)(2,1)S(1)}, bf16[256,256]{1,0:T(8,128)(2,1)S(1)}, u32[]{:S(2)}, u32[]{:S(2)}) collective-permute-start(bf16[256,256]{1,0:T(8,128)(2,1)S(1)} %slice.14.refs_0_), channel_id=1, source_target_pairs={{0,16},{1,17},{2,18},{3,19},{8,24},{9,25},{10,26},{11,27},{16,32},... | collective-permute-start | bytes 393224 | tf_op jit(solution)/shard_map/cond/branch_1_fun/ppermute | solution.py:305
  45.8 7.1 %collective-permute-start.7 = (bf16[128,256]{1,0:T(8,128)(2,1)S(1)}, bf16[128,256]{1,0:T(8,128)(2,1)S(1)}, u32[]{:S(2)}, u32[]{:S(2)}) collective-permute-start(bf16[128,256]{1,0:T(8,128)(2,1)S(1)} %get-tuple-element.89), channel_id=1, source_target_pairs={{494,510},{495,511},{484,500},{485,501},{486,502},{487,503},{492,5... | collective-permute-start | bytes 196616 | tf_op jit(solution)/shard_map/cond/branch_1_fun/ppermute | solution.py:305
  48.9 6.8 %collective-permute-start.6 = (bf16[128,256]{1,0:T(8,128)(2,1)S(1)}, bf16[128,256]{1,0:T(8,128)(2,1)S(1)}, u32[]{:S(2)}, u32[]{:S(2)}) collective-permute-start(bf16[128,256]{1,0:T(8,128)(2,1)S(1)} %get-tuple-element.90), channel_id=1, source_target_pairs={{480,494},{481,495},{482,484},{483,485},{488,486},{489,487},{490,4... | collective-permute-start | bytes 196616 | tf_op jit(solution)/shard_map/cond/branch_1_fun/ppermute | solution.py:305
  60.9 17.5 %collective-permute-start.8 = (bf16[256,256]{1,0:T(8,128)(2,1)S(1)}, bf16[256,256]{1,0:T(8,128)(2,1)S(1)}, u32[]{:S(2)}, u32[]{:S(2)}) collective-permute-start(bf16[256,256]{1,0:T(8,128)(2,1)S(1)} %get-tuple-element.65), channel_id=1, source_target_pairs={{16,0},{17,1},{18,2},{19,3},{24,8},{25,9},{26,10},{27,11},{32,16},... | collective-permute-start | bytes 393224 | tf_op jit(solution)/shard_map/cond/branch_1_fun/ppermute | solution.py:305
  66.1 14.0 %collective-permute-start.9 = (bf16[256,256]{1,0:T(8,128)(2,1)S(1)}, bf16[256,256]{1,0:T(8,128)(2,1)S(1)}, u32[]{:S(2)}, u32[]{:S(2)}) collective-permute-start(bf16[256,256]{1,0:T(8,128)(2,1)S(1)} %get-tuple-element.66), channel_id=1, source_target_pairs={{32,0},{33,1},{34,2},{35,3},{40,8},{41,9},{42,10},{43,11},{48,16},... | collective-permute-start | bytes 393224 | tf_op jit(solution)/shard_map/cond/branch_1_fun/ppermute | solution.py:305
  68.0 9.2 %collective-permute-start.10 = (bf16[128,256]{1,0:T(8,128)(2,1)S(1)}, bf16[128,256]{1,0:T(8,128)(2,1)S(1)}, u32[]{:S(2)}, u32[]{:S(2)}) collective-permute-start(bf16[128,256]{1,0:T(8,128)(2,1)S(1)} %get-tuple-element.67), channel_id=1, source_target_pairs={{494,480},{495,481},{484,482},{485,483},{486,488},{487,489},{492,4... | collective-permute-start | bytes 196616 | tf_op jit(solution)/shard_map/cond/branch_1_fun/ppermute | solution.py:305
  71.9 6.5 %collective-permute-start.11 = (bf16[128,256]{1,0:T(8,128)(2,1)S(1)}, bf16[128,256]{1,0:T(8,128)(2,1)S(1)}, u32[]{:S(2)}, u32[]{:S(2)}) collective-permute-start(bf16[128,256]{1,0:T(8,128)(2,1)S(1)} %get-tuple-element.68), channel_id=1, source_target_pairs={{510,494},{511,495},{500,484},{501,485},{502,486},{503,487},{508,4... | collective-permute-start | bytes 196616 | tf_op jit(solution)/shard_map/cond/branch_1_fun/ppermute | solution.py:305

commit v6 on v5

--- a/solution.py
+++ b/solution.py
@@ -33,9 +33,18 @@
     return (place + 2 * half) % PARTS
 
 
+def spot(p):
+    return p % 2 * (PARTS // 2) + p // 2
+
+
+def rows_of(block, lane):
+    first = (2 * lane + block) * PIECE
+    return slice(first, first + PIECE)
+
+
 def pieces(whole, split, at, wide):
     half = lax.axis_index("half")
-    columns = [pl.multiple_of(head_of(p, half) * wide, wide) for p in range(PARTS)]
+    columns = [pl.multiple_of(head_of(spot(p), half) * wide, wide) for p in range(PARTS)]
     return [
         (whole.at[:, pl.ds(column, wide)], split.at[p, :, pl.ds(at, wide)])
         for p, column in enumerate(columns)
@@ -122,8 +131,10 @@
         three = three_ref[...].astype(jnp.float32)
         lower = lower + jnp.where(later, 0.0, three)
         upper = upper + jnp.where(later, three, 0.0) + back_ref[...].astype(jnp.float32)
-    out_ref[:BLOCK, QG_WIDE:] = lower.astype(jnp.bfloat16)
-    out_ref[BLOCK:, QG_WIDE:] = upper.astype(jnp.bfloat16)
+    for b, part in enumerate((lower, upper)):
+        part = part.astype(jnp.bfloat16)
+        for lane in range(PARTS // 2):
+            out_ref[rows_of(b, lane), QG_WIDE:] = part[lane * PIECE : (lane + 1) * PIECE]
 
 
 def gather(place, pairing, od, parts):
@@ -160,7 +171,7 @@
     for b in range(2):
         holder = 2 * pair + b
         block = jnp.where(half == 0, holder, blocks - 1 - pairing_ref[holder])
-        doc = qg_ref[b * BLOCK : b * BLOCK + PIECE, WIDE:].astype(jnp.float32)
+        doc = qg_ref[rows_of(b, 0), WIDE:].astype(jnp.float32)
         doc = jnp.where(half == 0, doc[0:2], doc[2:4])
         begins = (doc[0:1] * BLOCK + doc[1:2]).astype(jnp.int32)
         live_row = live_ref[pl.ds(block, 1), :]
@@ -188,22 +199,16 @@
         bias = jnp.concatenate([bias, bias], axis=1)
         keys = jnp.concatenate([kv[pl.ds(s, BLOCK), :DIM] for s in slots], axis=0)
         values = jnp.concatenate([kv[pl.ds(s, BLOCK), DIM:] for s in slots], axis=0)
-        rows = slice(b * BLOCK, (b + 1) * BLOCK)
+        lanes_of = [rows_of(b, lane) for lane in range(PARTS // 2)]
         key_grad = None
         value_grad = None
         for h in range(0, GROUP, 2):
             first, second = h * DIM, (h + 1) * DIM
             shift = GROUP * DIM
-            q = jnp.concatenate(
-                [qg_ref[rows, first : first + DIM], qg_ref[rows, second : second + DIM]], axis=0
-            )
-            g = jnp.concatenate(
-                [
-                    qg_ref[rows, shift + first : shift + first + DIM],
-                    qg_ref[rows, shift + second : shift + second + DIM],
-                ],
-                axis=0,
-            )
+            columns = [slice(at, at + DIM) for at in (first, second)]
+            g_columns = [slice(shift + at, shift + at + DIM) for at in (first, second)]
+            q = jnp.concatenate([qg_ref[r, c] for c in columns for r in lanes_of], axis=0)
+            g = jnp.concatenate([qg_ref[r, c] for c in g_columns for r in lanes_of], axis=0)
             scores = dot(keys, q, 1, 1) + bias
             peak = jnp.max(scores, axis=0, keepdims=True)
             p = jnp.exp2((scores - peak) * (scale * math.log2(math.e)))
@@ -223,10 +228,10 @@
             value_grad = value_new if value_grad is None else value_grad + value_new
             out = out.T.astype(jnp.bfloat16)
             dq = dq.T.astype(jnp.bfloat16)
-            od_ref[rows, first : first + DIM] = out[:BLOCK]
-            od_ref[rows, second : second + DIM] = out[BLOCK:]
-            od_ref[rows, shift + first : shift + first + DIM] = dq[:BLOCK]
-            od_ref[rows, shift + second : shift + second + DIM] = dq[BLOCK:]
+            places = [(r, c, d) for c, d in zip(columns, g_columns) for r in lanes_of]
+            for i, (r, c, d) in enumerate(places):
+                od_ref[r, c] = out[i * PIECE : (i + 1) * PIECE]
+                od_ref[r, d] = dq[i * PIECE : (i + 1) * PIECE]
         key_grad = key_grad * scale
         for w, s in enumerate(slots):
             part = slice(w * BLOCK, (w + 1) * BLOCK)
@@ -281,8 +286,8 @@
     def device(place, head):
         in_half = int(place >= pairs)
         in_pair = chain - 1 - place if in_half else place
-        spot = next(p for p in range(PARTS) if head_of(p, in_half) == head)
-        in_side, in_lane = divmod(spot, lanes)
+        here = next(p for p in range(PARTS) if head_of(p, in_half) == head)
+        in_side, in_lane = divmod(here, lanes)
         return ((in_pair * 2 + in_side) * 2 + in_half) * lanes + in_lane
 
     def steps(by, targets):
@@ -305,7 +310,10 @@
         return lax.ppermute(x, axes, pairs_of)
 
     def exchange(x):
-        return lax.all_to_all(x, ("side", "lane"), split_axis=0, concat_axis=0, tiled=True)
+        order = [[spot(p) for p in range(PARTS)]]
+        return lax.all_to_all(
+            x, ("side", "lane"), split_axis=0, concat_axis=0, axis_index_groups=order, tiled=True
+        )
 
     place = jnp.stack([pair, side, half]).astype(jnp.int32)
     split = pack(doc_start.reshape(1, ROWS), query, grad_out, key, value)
@@ -315,7 +323,8 @@
     arrived = exchange(split).reshape(ROWS, WIDE + DIM)
 
     def finish(with_crossed, place, later, pairing, block_live, arrived):
-        own = arrived[:, QG_WIDE:WIDE]
+        own = arrived[:, QG_WIDE:WIDE].reshape(lanes, 2, PIECE, 2 * DIM)
+        own = own.transpose(1, 0, 2, 3).reshape(ROWS, 2 * DIM)
         halo = [own, move(own, forth[0]), move(own, forth[1])]
         if with_crossed:
             halo.append(move(jnp.where(later, own[BLOCK:], own[:BLOCK]), forth[2]))

time: 103 us -> 102 us (level)
  waiting for transfers between devices: 27.3 us -> 25.9 us
  transfers between devices with their start and end apart: 9 -> 9, of which waited for: 5 -> 4; matrix products, arithmetic and copies ran while one was open for 1% -> 1% of each run, Pallas kernels for 0% -> 0%
where the time goes in v6:
time: 102 us
  starting transfers between devices  40.7 us (40%)
  waiting for transfers between devices  25.9 us (25%)
  blocking collectives  20.9 us (20%)
  Pallas kernels  9.17 us (9%)
  loops' own time  1.43 us (1%)
  local copies, waits for them, and re-layouts  1.4 us (1%)
  between operations  1.3 us (1%)
    ppermute x8, starting transfers between devices, move(): return lax.ppermute(x, axes, pairs_of)  34.6 us
    all_to_all x1, blocking collectives, exchange(): lax.all_to_all(x, ('side', 'lane'), split_axis=0, concat_axis=0, axis_ind...  20.9 us
    all_to_all x1, waiting for transfers between devices, exchange(): lax.all_to_all(x, ('side', 'lane'), split_axis=0, concat_axis=0, axis_ind...  18.9 us
    ppermute x8, waiting for transfers between devices, move(): return lax.ppermute(x, axes, pairs_of)  6.99 us
    all_to_all x1, starting transfers between devices, exchange(): lax.all_to_all(x, ('side', 'lane'), split_axis=0, concat_axis=0, axis_ind...  6.12 us
    pallas_call x1, Pallas kernels, attention(): pl.pallas_call(functools.partial(attention_kernel, chain, starts), out_sh...  5.15 us
    pallas_call x1, Pallas kernels, pack(): pl.pallas_call(pack_kernel, out_shape=jax.ShapeDtypeStruct((PARTS, PIECE,...  2.27 us
  transfers between devices with their start and end apart: 9, of which 4 were waited for; matrix products, arithmetic and copies ran while one was open for 1% of the time, Pallas kernels for 0%

profile of v6, /device:TPU:23, one launch (start us, length us, event | category | flops | bytes accessed | tf_op | source)
XLA Modules:
  0.0 101.5 jit_solution(8751809044840056329)
XLA Ops:
  0.6 2.3 %pack.1 = bf16[8,32,1408]{2,1,0:T(8,128)(2,1)} custom-call(s32[1,256]{1,0:T(1,128)} %bitcast.36, bf16[32,4096]{1,0:T(8,128)(2,1)} %q_ref.1, bf16[32,4096]{1,0:T(8,128)(2,1)} %g_ref.1, bf16[32,1024]{1,0:T(8,128)(2,1)} %k_ref.1, bf16[32,1024]{1,0:T(8,128)(2,1)} %v_ref.1), custom_call_target="tpu_custom_call" | custom-call | tf_op jit(solution)/shard_map/pack/pallas_call | solution.py:83
  2.9 6.1 %all-to-all-start.2 = ((bf16[8,32,1408]{2,1,0:T(8,128)(2,1)}), bf16[8,32,1408]{2,1,0:T(8,128)(2,1)S(1)}, u32[]{:S(2)}, u32[]{:S(2)}) async-start(bf16[8,32,1408]{2,1,0:T(8,128)(2,1)} %pack.1), calls=%async_computation.2 | async-start | bytes 1441792 | tf_op jit(solution)/shard_map/all_to_all | solution.py:314
  9.0 0.7 copy-done
  9.7 0.1 slice.22
  9.8 0.6 compare_reduce_fusion
  11.1 0.1 pad_add_fusion
  11.2 18.9 %all-to-all-done.2 = bf16[8,32,1408]{2,1,0:T(8,128)(2,1)S(1)} async-done(((bf16[8,32,1408]{2,1,0:T(8,128)(2,1)}), bf16[8,32,1408]{2,1,0:T(8,128)(2,1)S(1)}, u32[]{:S(2)}, u32[]{:S(2)}) %all-to-all-start.2) | async-done | bytes 720928 | tf_op jit(solution)/shard_map/all_to_all | solution.py:314
  30.1 71.5 %conditional.1 = ((bf16[32,4096]{1,0:T(8,128)(2,1)}, bf16[32,4096]{1,0:T(8,128)(2,1)}, bf16[32,1024]{1,0:T(8,128)(2,1)}, bf16[32,1024]{1,0:T(8,128)(2,1)})) conditional(s32[]{:T(128)} %convert_element_type.3, (bf16[256,1408]{1,0:T(8,128)(2,1)S(1)}, s32[3]{0:T(128)S(1)}, s32[64]{0:T(128)S(1)}, s32[128,128]{1,0:T(8,128)S(1)}) %tuple.49, ...), branch_computations={%region_1.0_spmd, %region_2.3_spmd} | conditional | flops 838893568 | bytes 8585682 | solution.py:337
  30.1 10.9 %collective-permute-start.5 = (bf16[256,256]{1,0:T(8,128)(2,1)S(1)}, bf16[256,256]{1,0:T(8,128)(2,1)S(1)}, u32[]{:S(2)}, u32[]{:S(2)}) collective-permute-start(bf16[256,256]{1,0:T(8,128)(2,1)S(1)} %bitcast.24), channel_id=1, source_target_pairs={{0,32},{1,33},{2,34},{3,35},{8,40},{9,41},{10,42},{11,43},{16,48},... | collective-permute-start | bytes 393224 | tf_op jit(solution)/shard_map/cond/branch_1_fun/ppermute | solution.py:310
  41.0 2.2 %collective-permute-start.4 = (bf16[256,256]{1,0:T(8,128)(2,1)S(1)}, bf16[256,256]{1,0:T(8,128)(2,1)S(1)}, u32[]{:S(2)}, u32[]{:S(2)}) collective-permute-start(bf16[256,256]{1,0:T(8,128)(2,1)S(1)} %bitcast.25), channel_id=1, source_target_pairs={{0,16},{1,17},{2,18},{3,19},{8,24},{9,25},{10,26},{11,27},{16,32},... | collective-permute-start | bytes 393224 | tf_op jit(solution)/shard_map/cond/branch_1_fun/ppermute | solution.py:310
  43.3 3.1 %collective-permute-start.7 = (bf16[128,256]{1,0:T(8,128)(2,1)S(1)}, bf16[128,256]{1,0:T(8,128)(2,1)S(1)}, u32[]{:S(2)}, u32[]{:S(2)}) collective-permute-start(bf16[128,256]{1,0:T(8,128)(2,1)S(1)} %bitcast.35), channel_id=1, source_target_pairs={{494,510},{495,511},{484,500},{485,501},{486,502},{487,503},{492,5... | collective-permute-start | bytes 196616 | tf_op jit(solution)/shard_map/cond/branch_1_fun/ppermute | solution.py:310
  46.4 0.6 fusion.1
  48.3 1.9 %collective-permute-start.6 = (bf16[128,256]{1,0:T(8,128)(2,1)S(1)}, bf16[128,256]{1,0:T(8,128)(2,1)S(1)}, u32[]{:S(2)}, u32[]{:S(2)}) collective-permute-start(bf16[128,256]{1,0:T(8,128)(2,1)S(1)} %bitcast_select_fusion), channel_id=1, source_target_pairs={{480,494},{481,495},{482,484},{483,485},{488,486},{489,487},{490,4... | collective-permute-start | bytes 196616 | tf_op jit(solution)/shard_map/cond/branch_1_fun/ppermute | solution.py:310
  50.2 0.1 collective-permute-done.7.refs_4_
  50.4 4.8 %collective-permute-done.6.refs_3_ = bf16[128,256]{1,0:T(8,128)(2,1)S(1)} collective-permute-done((bf16[128,256]{1,0:T(8,128)(2,1)S(1)}, bf16[128,256]{1,0:T(8,128)(2,1)S(1)}, u32[]{:S(2)}, u32[]{:S(2)}) %collective-permute-start.6) | collective-permute-done | bytes 65568 | tf_op jit(solution)/shard_map/cond/branch_1_fun/ppermute | solution.py:310
  55.2 5.1 %attention.3 = (bf16[256,1024]{1,0:T(8,128)(2,1)S(1)}, f32[256,256]{1,0:T(8,128)S(1)}, bf16[256,256]{1,0:T(8,128)(2,1)S(1)}, bf16[256,256]{1,0:T(8,128)(2,1)S(1)...) custom-call(s32[3]{0:T(128)S(1)} %get-tuple-element.57.place_ref, s32[64]{0:T(128)S(1)} %get-tuple-element.58.pairing_ref, ...), custom_call_target="tpu_custom_call" | custom-call | flops 838860800 | bytes 3145728 | tf_op jit(solution)/shard_map/cond/branch_1_fun/attention/pallas_call | solution.py:252
  60.3 5.4 %collective-permute-start.8 = (bf16[256,256]{1,0:T(8,128)(2,1)S(1)}, bf16[256,256]{1,0:T(8,128)(2,1)S(1)}, u32[]{:S(2)}, u32[]{:S(2)}) collective-permute-start(bf16[256,256]{1,0:T(8,128)(2,1)S(1)} %get-tuple-element.65), channel_id=1, source_target_pairs={{16,0},{17,1},{18,2},{19,3},{24,8},{25,9},{26,10},{27,11},{32,16},... | collective-permute-start | bytes 393224 | tf_op jit(solution)/shard_map/cond/branch_1_fun/ppermute | solution.py:310
  65.7 1.9 %collective-permute-start.9 = (bf16[256,256]{1,0:T(8,128)(2,1)S(1)}, bf16[256,256]{1,0:T(8,128)(2,1)S(1)}, u32[]{:S(2)}, u32[]{:S(2)}) collective-permute-start(bf16[256,256]{1,0:T(8,128)(2,1)S(1)} %get-tuple-element.66), channel_id=1, source_target_pairs={{32,0},{33,1},{34,2},{35,3},{40,8},{41,9},{42,10},{43,11},{48,16},... | collective-permute-start | bytes 393224 | tf_op jit(solution)/shard_map/cond/branch_1_fun/ppermute | solution.py:310
  67.6 4.0 %collective-permute-start.10 = (bf16[128,256]{1,0:T(8,128)(2,1)S(1)}, bf16[128,256]{1,0:T(8,128)(2,1)S(1)}, u32[]{:S(2)}, u32[]{:S(2)}) collective-permute-start(bf16[128,256]{1,0:T(8,128)(2,1)S(1)} %get-tuple-element.67), channel_id=1, source_target_pairs={{494,480},{495,481},{484,482},{485,483},{486,488},{487,489},{492,4... | collective-permute-start | bytes 196616 | tf_op jit(solution)/shard_map/cond/branch_1_fun/ppermute | solution.py:310
  71.6 5.2 %collective-permute-start.11 = (bf16[128,256]{1,0:T(8,128)(2,1)S(1)}, bf16[128,256]{1,0:T(8,128)(2,1)S(1)}, u32[]{:S(2)}, u32[]{:S(2)}) collective-permute-start(bf16[128,256]{1,0:T(8,128)(2,1)S(1)} %get-tuple-element.68), channel_id=1, source_target_pairs={{510,494},{511,495},{500,484},{501,485},{502,486},{503,487},{508,4... | collective-permute-start | bytes 196616 | tf_op jit(solution)/shard_map/cond/branch_1_fun/ppermute | solution.py:310
  76.8 2.1 %collective-permute-done.10.refs_0_ = bf16[128,256]{1,0:T(8,128)(2,1)S(1)} collective-permute-done((bf16[128,256]{1,0:T(8,128)(2,1)S(1)}, bf16[128,256]{1,0:T(8,128)(2,1)S(1)}, u32[]{:S(2)}, u32[]{:S(2)}) %collective-permute-start.10) | collective-permute-done | bytes 65568 | tf_op jit(solution)/shard_map/cond/branch_1_fun/ppermute | solution.py:310
  78.9 0.7 gather.3
  79.6 20.9 %all_to_all.14.split_ref = bf16[8,32,1280]{2,1,0:T(8,128)(2,1)S(1)} all-to-all(bf16[8,32,1280]{2,1,0:T(8,128)(2,1)S(1)} %bitcast.22), channel_id=1, replica_groups={{0,8,1,9,2,10,3,11},{4,12,5,13,6,14,7,15},{16,24,17,25,18,26,19,27},{20..., dimensions={0} | all-to-all | bytes 1310720 | tf_op jit(solution)/shard_map/cond/branch_1_fun/all_to_all | solution.py:314
  100.4 1.1 %unpack.3 = (bf16[32,4096]{1,0:T(8,128)(2,1)}, bf16[32,4096]{1,0:T(8,128)(2,1)}, bf16[32,1024]{1,0:T(8,128)(2,1)}, bf16[32,1024]{1,0:T(8,128)(2,1)}) custom-call(bf16[8,32,1280]{2,1,0:T(8,128)(2,1)S(1)} %all_to_all.14.split_ref), custom_call_target="tpu_custom_call" | custom-call | tf_op jit(solution)/shard_map/cond/branch_1_fun/unpack/pallas_call | solution.py:111
  (12 shorter events, 0.1 us)
Async XLA Ops:
  2.9 27.2 %copy-start.1 = (s32[128,128]{1,0:T(8,128)S(1)}, s32[128,128]{1,0:T(8,128)}, u32[]{:S(2)}) copy-start(s32[128,128]{1,0:T(8,128)} %param.11) | copy-start | bytes 196612
  2.9 27.2 %all-to-all-start.2 = ((bf16[8,32,1408]{2,1,0:T(8,128)(2,1)}), bf16[8,32,1408]{2,1,0:T(8,128)(2,1)S(1)}, u32[]{:S(2)}, u32[]{:S(2)}) async-start(bf16[8,32,1408]{2,1,0:T(8,128)(2,1)} %pack.1), calls=%async_computation.2 | async-start | bytes 1441792 | tf_op jit(solution)/shard_map/all_to_all | solution.py:314
  9.0 0.7 copy-start
  30.1 25.0 %collective-permute-start.5 = (bf16[256,256]{1,0:T(8,128)(2,1)S(1)}, bf16[256,256]{1,0:T(8,128)(2,1)S(1)}, u32[]{:S(2)}, u32[]{:S(2)}) collective-permute-start(bf16[256,256]{1,0:T(8,128)(2,1)S(1)} %bitcast.24), channel_id=1, source_target_pairs={{0,32},{1,33},{2,34},{3,35},{8,40},{9,41},{10,42},{11,43},{16,48},... | collective-permute-start | bytes 393224 | tf_op jit(solution)/shard_map/cond/branch_1_fun/ppermute | solution.py:310
  41.0 14.1 %collective-permute-start.4 = (bf16[256,256]{1,0:T(8,128)(2,1)S(1)}, bf16[256,256]{1,0:T(8,128)(2,1)S(1)}, u32[]{:S(2)}, u32[]{:S(2)}) collective-permute-start(bf16[256,256]{1,0:T(8,128)(2,1)S(1)} %bitcast.25), channel_id=1, source_target_pairs={{0,16},{1,17},{2,18},{3,19},{8,24},{9,25},{10,26},{11,27},{16,32},... | collective-permute-start | bytes 393224 | tf_op jit(solution)/shard_map/cond/branch_1_fun/ppermute | solution.py:310
  43.3 7.1 %collective-permute-start.7 = (bf16[128,256]{1,0:T(8,128)(2,1)S(1)}, bf16[128,256]{1,0:T(8,128)(2,1)S(1)}, u32[]{:S(2)}, u32[]{:S(2)}) collective-permute-start(bf16[128,256]{1,0:T(8,128)(2,1)S(1)} %bitcast.35), channel_id=1, source_target_pairs={{494,510},{495,511},{484,500},{485,501},{486,502},{487,503},{492,5... | collective-permute-start | bytes 196616 | tf_op jit(solution)/shard_map/cond/branch_1_fun/ppermute | solution.py:310
  48.3 6.8 %collective-permute-start.6 = (bf16[128,256]{1,0:T(8,128)(2,1)S(1)}, bf16[128,256]{1,0:T(8,128)(2,1)S(1)}, u32[]{:S(2)}, u32[]{:S(2)}) collective-permute-start(bf16[128,256]{1,0:T(8,128)(2,1)S(1)} %bitcast_select_fusion), channel_id=1, source_target_pairs={{480,494},{481,495},{482,484},{483,485},{488,486},{489,487},{490,4... | collective-permute-start | bytes 196616 | tf_op jit(solution)/shard_map/cond/branch_1_fun/ppermute | solution.py:310
  60.3 18.6 %collective-permute-start.8 = (bf16[256,256]{1,0:T(8,128)(2,1)S(1)}, bf16[256,256]{1,0:T(8,128)(2,1)S(1)}, u32[]{:S(2)}, u32[]{:S(2)}) collective-permute-start(bf16[256,256]{1,0:T(8,128)(2,1)S(1)} %get-tuple-element.65), channel_id=1, source_target_pairs={{16,0},{17,1},{18,2},{19,3},{24,8},{25,9},{26,10},{27,11},{32,16},... | collective-permute-start | bytes 393224 | tf_op jit(solution)/shard_map/cond/branch_1_fun/ppermute | solution.py:310
  65.7 13.2 %collective-permute-start.9 = (bf16[256,256]{1,0:T(8,128)(2,1)S(1)}, bf16[256,256]{1,0:T(8,128)(2,1)S(1)}, u32[]{:S(2)}, u32[]{:S(2)}) collective-permute-start(bf16[256,256]{1,0:T(8,128)(2,1)S(1)} %get-tuple-element.66), channel_id=1, source_target_pairs={{32,0},{33,1},{34,2},{35,3},{40,8},{41,9},{42,10},{43,11},{48,16},... | collective-permute-start | bytes 393224 | tf_op jit(solution)/shard_map/cond/branch_1_fun/ppermute | solution.py:310
  67.6 11.2 %collective-permute-start.10 = (bf16[128,256]{1,0:T(8,128)(2,1)S(1)}, bf16[128,256]{1,0:T(8,128)(2,1)S(1)}, u32[]{:S(2)}, u32[]{:S(2)}) collective-permute-start(bf16[128,256]{1,0:T(8,128)(2,1)S(1)} %get-tuple-element.67), channel_id=1, source_target_pairs={{494,480},{495,481},{484,482},{485,483},{486,488},{487,489},{492,4... | collective-permute-start | bytes 196616 | tf_op jit(solution)/shard_map/cond/branch_1_fun/ppermute | solution.py:310
  71.6 7.3 %collective-permute-start.11 = (bf16[128,256]{1,0:T(8,128)(2,1)S(1)}, bf16[128,256]{1,0:T(8,128)(2,1)S(1)}, u32[]{:S(2)}, u32[]{:S(2)}) collective-permute-start(bf16[128,256]{1,0:T(8,128)(2,1)S(1)} %get-tuple-element.68), channel_id=1, source_target_pairs={{510,494},{511,495},{500,484},{501,485},{502,486},{503,487},{508,4... | collective-permute-start | bytes 196616 | tf_op jit(solution)/shard_map/cond/branch_1_fun/ppermute | solution.py:310

commit v7 on v6

--- a/solution.py
+++ b/solution.py
@@ -59,40 +59,26 @@
     ]
 
 
-def pack_kernel(doc_ref, q_ref, g_ref, k_ref, v_ref, out_ref, doc_here, sems, doc_sem):
-    doc_copy = pltpu.make_async_copy(doc_ref, doc_here, doc_sem)
-    doc_copy.start()
+def pack_kernel(q_ref, g_ref, k_ref, v_ref, out_ref, sems):
     copies = copies_of(q_ref, g_ref, out_ref, 0, QUERY_WIDE, sems, True)
     copies += copies_of(k_ref, v_ref, out_ref, QG_WIDE, DIM, sems.at[2 * PARTS :], True)
     for copy in copies:
         copy.start()
-    doc_copy.wait()
-    doc = doc_here[...]
-    line = lax.broadcasted_iota(jnp.int32, (PIECE, BLOCK), 0)
-    coded = jnp.where(line < 2, doc[:, :BLOCK], doc[:, BLOCK:])
-    coded = jnp.where(line % 2 == 0, coded // BLOCK, coded % BLOCK)
-    coded = coded.astype(jnp.float32).astype(jnp.bfloat16)
-    for p in range(PARTS):
-        out_ref[p, :, WIDE:] = coded
     for copy in copies:
         copy.wait()
 
 
-def pack(doc, query, grad_out, key, value):
+def pack(query, grad_out, key, value):
     hbm = pl.BlockSpec(memory_space=pltpu.HBM)
     return pl.pallas_call(
         pack_kernel,
-        out_shape=jax.ShapeDtypeStruct((PARTS, PIECE, WIDE + DIM), jnp.bfloat16),
-        in_specs=[hbm] * 5,
+        out_shape=jax.ShapeDtypeStruct((PARTS, PIECE, WIDE), jnp.bfloat16),
+        in_specs=[hbm] * 4,
         out_specs=pl.BlockSpec(memory_space=pltpu.VMEM),
-        scratch_shapes=[
-            pltpu.VMEM((1, ROWS), jnp.int32),
-            pltpu.SemaphoreType.DMA((4 * PARTS,)),
-            pltpu.SemaphoreType.DMA,
-        ],
+        scratch_shapes=[pltpu.SemaphoreType.DMA((4 * PARTS,))],
         compiler_params=pltpu.CompilerParams(vmem_limit_bytes=(63 * 1024 + 256) * 1024),
         name="pack",
-    )(doc, query, grad_out, key, value)
+    )(query, grad_out, key, value)
 
 
 def unpack_kernel(split_ref, att_ref, dq_ref, dk_ref, dv_ref, sems):
@@ -150,7 +136,9 @@
     )(place, pairing, od, *parts)
 
 
-def attention_kernel(chain, starts, place_ref, pairing_ref, live_ref, qg_ref, *refs):
+def attention_kernel(
+    chain, starts, place_ref, pairing_ref, live_ref, doc_ref, doc_other_ref, qg_ref, *refs
+):
     held = refs[: len(starts) - 1]
     od_ref, *parts, kv, acc = refs[len(starts) - 1 :]
     pair = place_ref[0]
@@ -164,6 +152,9 @@
         kv[begin:end, :] = ref[...]
     acc[...] = jnp.zeros_like(acc)
 
+    side = place_ref[1]
+    mine = jnp.where(half == 0, doc_ref[:, :BLOCK], doc_ref[:, BLOCK:])
+    other = jnp.where(half == 0, doc_other_ref[:, :BLOCK], doc_other_ref[:, BLOCK:])
     keys_down = lax.broadcasted_iota(jnp.int32, (BLOCK, BLOCK), 0)
     rows_along = lax.broadcasted_iota(jnp.int32, (BLOCK, BLOCK), 1)
     lanes = lax.broadcasted_iota(jnp.int32, (1, blocks), 1)
@@ -171,9 +162,7 @@
     for b in range(2):
         holder = 2 * pair + b
         block = jnp.where(half == 0, holder, blocks - 1 - pairing_ref[holder])
-        doc = qg_ref[rows_of(b, 0), WIDE:].astype(jnp.float32)
-        doc = jnp.where(half == 0, doc[0:2], doc[2:4])
-        begins = (doc[0:1] * BLOCK + doc[1:2]).astype(jnp.int32)
+        begins = jnp.where(side == b, mine, other)
         live_row = live_ref[pl.ds(block, 1), :]
         slots = []
         bias = []
@@ -242,7 +231,7 @@
         ref[...] = acc[begin:end, :].astype(ref.dtype)
 
 
-def attention(chain, place, pairing, live, qg, halo):
+def attention(chain, place, pairing, live, docs, qg, halo):
     wide = 2 * DIM
     vmem = pl.BlockSpec(memory_space=pltpu.VMEM)
     smem = pl.BlockSpec(memory_space=pltpu.SMEM)
@@ -256,7 +245,7 @@
             jax.ShapeDtypeStruct((ROWS, wide), jnp.float32),
             *(jax.ShapeDtypeStruct(held.shape, jnp.bfloat16) for held in halo[1:]),
         ),
-        in_specs=[smem, smem] + [vmem] * (2 + len(halo)),
+        in_specs=[smem, smem] + [vmem] * (4 + len(halo)),
         out_specs=(vmem,) * (1 + len(halo)),
         scratch_shapes=[
             pltpu.VMEM((starts[-1], wide), jnp.bfloat16),
@@ -269,7 +258,7 @@
             transcendentals=2 * WINDOW * GROUP * BLOCK * BLOCK,
         ),
         name="attention",
-    )(place, pairing, live, qg, *halo)
+    )(place, pairing, live, *docs, qg, *halo)
 
 
 def body(pairing, doc_start, block_live, query, key, value, grad_out):
@@ -316,20 +305,26 @@
         )
 
     place = jnp.stack([pair, side, half]).astype(jnp.int32)
-    split = pack(doc_start.reshape(1, ROWS), query, grad_out, key, value)
-    split, pairing = lax.optimization_barrier((split, pairing))
+    split = pack(query, grad_out, key, value)
+    split, pairing, doc = lax.optimization_barrier((split, pairing, doc_start.reshape(1, ROWS)))
+    doc_other = lax.ppermute(doc, "side", [(0, 1), (1, 0)])
     later = (half == 0) | (pairing[2 * pair + 1] < pairing[2 * pair])
     crossed = jnp.any(pairing[1 : chain - 1 : 2] == jnp.arange(2, chain, 2, dtype=jnp.int32))
-    arrived = exchange(split).reshape(ROWS, WIDE + DIM)
-
-    def finish(with_crossed, place, later, pairing, block_live, arrived):
+    arrived = exchange(split).reshape(ROWS, WIDE)
+    arrived, later, crossed, doc_other = lax.optimization_barrier(
+        (arrived, later, crossed, doc_other)
+    )
+
+    def finish(with_crossed, place, later, pairing, block_live, doc, doc_other, arrived):
         own = arrived[:, QG_WIDE:WIDE].reshape(lanes, 2, PIECE, 2 * DIM)
         own = own.transpose(1, 0, 2, 3).reshape(ROWS, 2 * DIM)
         halo = [own, move(own, forth[0]), move(own, forth[1])]
         if with_crossed:
             halo.append(move(jnp.where(later, own[BLOCK:], own[:BLOCK]), forth[2]))
             halo.append(move(own[BLOCK:], forth[3]))
-        od, own_grad, *partials = attention(chain, place, pairing, block_live, arrived, halo)
+        od, own_grad, *partials = attention(
+            chain, place, pairing, block_live, (doc, doc_other), arrived, halo
+        )
         partials = [move(part, pairs_of) for part, pairs_of in zip(partials, back)]
         total = gather(place, pairing, od, (own_grad, *partials))
         return unpack(exchange(total.reshape(PARTS, PIECE, -1)))
@@ -342,6 +337,8 @@
         later,
         pairing,
         block_live,
+        doc,
+        doc_other,
         arrived,
     )
 

time: 102 us -> 99.8 us (0.978)
  waiting for transfers between devices: 25.9 us -> 13.8 us
  starting transfers between devices: 40.7 us -> 50.3 us
  between operations: 1.3 us -> 2.65 us
  loops' own time: 1.43 us -> 0.14 us
    all_to_all x1, waiting for transfers between devices: 18.9 us -> 0.01 us  [exchange(): lax.all_to_all(x, ('side', 'lane'), split_axis=0, concat_axis=0, axis_ind...]
    ppermute x0 -> x1, waiting for transfers between devices: none -> 7.66 us  [body(): doc_other = lax.ppermute(doc, 'side', [(0, 1), (1, 0)])]
    ppermute x0 -> x1, starting transfers between devices: none -> 7.19 us  [body(): doc_other = lax.ppermute(doc, 'side', [(0, 1), (1, 0)])]
    ppermute x8, starting transfers between devices: 34.6 us -> 37 us  [move(): return lax.ppermute(x, axes, pairs_of)]
    another operation x1, loops' own time: 1.43 us -> 0.14 us  [body(): lax.cond(crossed, functools.partial(finish, True), functools.partial(fini...]
  transfers between devices with their start and end apart: 9 -> 10, of which waited for: 4 -> 4; matrix products, arithmetic and copies ran while one was open for 1% -> 1% of each run, Pallas kernels for 0% -> 0%
where the time goes in v7:
time: 99.8 us; the launch traced here: 99.2 us
  starting transfers between devices  50.3 us (50%)
  blocking collectives  21 us (21%)
  waiting for transfers between devices  13.8 us (14%)
  Pallas kernels  9.12 us (9%)
  between operations  2.65 us (3%)
  local copies, waits for them, and re-layouts  1.4 us (1%)
    ppermute x8, starting transfers between devices, move(): return lax.ppermute(x, axes, pairs_of)  37 us
    all_to_all x1, blocking collectives, exchange(): lax.all_to_all(x, ('side', 'lane'), split_axis=0, concat_axis=0, axis_ind...  21 us
    ppermute x1, waiting for transfers between devices, body(): doc_other = lax.ppermute(doc, 'side', [(0, 1), (1, 0)])  7.66 us
    ppermute x1, starting transfers between devices, body(): doc_other = lax.ppermute(doc, 'side', [(0, 1), (1, 0)])  7.19 us
    ppermute x8, waiting for transfers between devices, move(): return lax.ppermute(x, axes, pairs_of)  6.19 us
    all_to_all x1, starting transfers between devices, exchange(): lax.all_to_all(x, ('side', 'lane'), split_axis=0, concat_axis=0, axis_ind...  6.12 us
    pallas_call x1, Pallas kernels, attention(): pl.pallas_call(functools.partial(attention_kernel, chain, starts), out_sh...  5.15 us
    pallas_call x1, Pallas kernels, pack(): pl.pallas_call(pack_kernel, out_shape=jax.ShapeDtypeStruct((PARTS, PIECE,...  2.2 us
  transfers between devices with their start and end apart: 10, of which 4 were waited for; matrix products, arithmetic and copies ran while one was open for 1% of the time, Pallas kernels for 0%

profile of v7, /device:TPU:23, one launch (start us, length us, event | category | flops | bytes accessed | tf_op | source)
XLA Modules:
  0.0 99.2 jit_solution(15144940900009430533)
XLA Ops:
  0.6 2.2 %pack.1 = bf16[8,32,1280]{2,1,0:T(8,128)(2,1)} custom-call(bf16[32,4096]{1,0:T(8,128)(2,1)} %q_ref.1, bf16[32,4096]{1,0:T(8,128)(2,1)} %g_ref.1, bf16[32,1024]{1,0:T(8,128)(2,1)} %k_ref.1, bf16[32,1024]{1,0:T(8,128)(2,1)} %v_ref.1), custom_call_target="tpu_custom_call" | custom-call | tf_op jit(solution)/shard_map/pack/pallas_call | solution.py:73
  2.9 6.1 %all-to-all-start.2 = ((bf16[8,32,1280]{2,1,0:T(8,128)(2,1)}), bf16[8,32,1280]{2,1,0:T(8,128)(2,1)S(1)}, u32[]{:S(2)}, u32[]{:S(2)}) async-start(bf16[8,32,1280]{2,1,0:T(8,128)(2,1)} %pack.1), calls=%async_computation.2 | async-start | bytes 1310720 | tf_op jit(solution)/shard_map/all_to_all | solution.py:303
  9.0 7.2 %collective-permute-start.12 = (s32[1,256]{1,0:T(1,128)S(1)}, s32[1,256]{1,0:T(1,128)S(1)}, u32[]{:S(2)}, u32[]{:S(2)}) collective-permute-start(s32[1,256]{1,0:T(1,128)S(1)} %bitcast.36), channel_id=1, source_target_pairs={{0,8},{8,0},{1,9},{9,1},{2,10},{10,2},{3,11},{11,3},{4,12},{12,4},... | collective-permute-start | bytes 3080 | tf_op jit(solution)/shard_map/ppermute | solution.py:310
  16.2 0.6 copy-done
  16.9 0.1 slice.22
  17.0 0.6 compare_reduce_fusion
  17.7 0.6 fusion.1
  19.6 7.7 %collective-permute-done.12 = s32[1,256]{1,0:T(1,128)S(1)} collective-permute-done((s32[1,256]{1,0:T(1,128)S(1)}, s32[1,256]{1,0:T(1,128)S(1)}, u32[]{:S(2)}, u32[]{:S(2)}) %collective-permute-start.12) | collective-permute-done | bytes 1056 | tf_op jit(solution)/shard_map/ppermute | solution.py:310
  27.9 71.3 %conditional.1 = ((bf16[32,4096]{1,0:T(8,128)(2,1)}, bf16[32,4096]{1,0:T(8,128)(2,1)}, bf16[32,1024]{1,0:T(8,128)(2,1)}, bf16[32,1024]{1,0:T(8,128)(2,1)})) conditional(s32[]{:T(128)} %convert_element_type.3, (bf16[256,1280]{1,0:T(8,128)(2,1)S(1)}, s32[3]{0:T(128)S(1)}, s32[64]{0:T(128)S(1)}, s32[128,128]{1,0:T(8,128)S(1)}, s32[1,256]{1,0:T(1,128)S(1)}, ...), branch_computations={%region_1.0_spmd, %region_2.3_spmd} | conditional | flops 838893568 | bytes 8585545 | solution.py:332
  28.0 10.9 %collective-permute-start.5 = (bf16[256,256]{1,0:T(8,128)(2,1)S(1)}, bf16[256,256]{1,0:T(8,128)(2,1)S(1)}, u32[]{:S(2)}, u32[]{:S(2)}) collective-permute-start(bf16[256,256]{1,0:T(8,128)(2,1)S(1)} %bitcast.24), channel_id=1, source_target_pairs={{0,32},{1,33},{2,34},{3,35},{8,40},{9,41},{10,42},{11,43},{16,48},... | collective-permute-start | bytes 393224 | tf_op jit(solution)/shard_map/cond/branch_1_fun/ppermute | solution.py:299
  38.9 2.2 %collective-permute-start.4 = (bf16[256,256]{1,0:T(8,128)(2,1)S(1)}, bf16[256,256]{1,0:T(8,128)(2,1)S(1)}, u32[]{:S(2)}, u32[]{:S(2)}) collective-permute-start(bf16[256,256]{1,0:T(8,128)(2,1)S(1)} %bitcast.25), channel_id=1, source_target_pairs={{0,16},{1,17},{2,18},{3,19},{8,24},{9,25},{10,26},{11,27},{16,32},... | collective-permute-start | bytes 393224 | tf_op jit(solution)/shard_map/cond/branch_1_fun/ppermute | solution.py:299
  41.1 3.1 %collective-permute-start.7 = (bf16[128,256]{1,0:T(8,128)(2,1)S(1)}, bf16[128,256]{1,0:T(8,128)(2,1)S(1)}, u32[]{:S(2)}, u32[]{:S(2)}) collective-permute-start(bf16[128,256]{1,0:T(8,128)(2,1)S(1)} %bitcast.35), channel_id=1, source_target_pairs={{494,510},{495,511},{484,500},{485,501},{486,502},{487,503},{492,5... | collective-permute-start | bytes 196616 | tf_op jit(solution)/shard_map/cond/branch_1_fun/ppermute | solution.py:299
  44.2 1.9 %collective-permute-start.6 = (bf16[128,256]{1,0:T(8,128)(2,1)S(1)}, bf16[128,256]{1,0:T(8,128)(2,1)S(1)}, u32[]{:S(2)}, u32[]{:S(2)}) collective-permute-start(bf16[128,256]{1,0:T(8,128)(2,1)S(1)} %bitcast_select_fusion), channel_id=1, source_target_pairs={{480,494},{481,495},{482,484},{483,485},{488,486},{489,487},{490,4... | collective-permute-start | bytes 196616 | tf_op jit(solution)/shard_map/cond/branch_1_fun/ppermute | solution.py:299
  46.2 2.1 %collective-permute-done.7.refs_4_ = bf16[128,256]{1,0:T(8,128)(2,1)S(1)} collective-permute-done((bf16[128,256]{1,0:T(8,128)(2,1)S(1)}, bf16[128,256]{1,0:T(8,128)(2,1)S(1)}, u32[]{:S(2)}, u32[]{:S(2)}) %collective-permute-start.7) | collective-permute-done | bytes 65568 | tf_op jit(solution)/shard_map/cond/branch_1_fun/ppermute | solution.py:299
  48.2 2.8 %collective-permute-done.6.refs_3_ = bf16[128,256]{1,0:T(8,128)(2,1)S(1)} collective-permute-done((bf16[128,256]{1,0:T(8,128)(2,1)S(1)}, bf16[128,256]{1,0:T(8,128)(2,1)S(1)}, u32[]{:S(2)}, u32[]{:S(2)}) %collective-permute-start.6) | collective-permute-done | bytes 65568 | tf_op jit(solution)/shard_map/cond/branch_1_fun/ppermute | solution.py:299
  51.1 5.2 %attention.3 = (bf16[256,1024]{1,0:T(8,128)(2,1)S(1)}, f32[256,256]{1,0:T(8,128)S(1)}, bf16[256,256]{1,0:T(8,128)(2,1)S(1)}, bf16[256,256]{1,0:T(8,128)(2,1)S(1)...) custom-call(s32[3]{0:T(128)S(1)} %get-tuple-element.36.place_ref, s32[64]{0:T(128)S(1)} %get-tuple-element.37.pairing_ref, ...), custom_call_target="tpu_custom_call" | custom-call | flops 838860800 | bytes 3145728 | tf_op jit(solution)/shard_map/cond/branch_1_fun/attention/pallas_call | solution.py:241
  56.2 5.3 %collective-permute-start.8 = (bf16[256,256]{1,0:T(8,128)(2,1)S(1)}, bf16[256,256]{1,0:T(8,128)(2,1)S(1)}, u32[]{:S(2)}, u32[]{:S(2)}) collective-permute-start(bf16[256,256]{1,0:T(8,128)(2,1)S(1)} %get-tuple-element.45), channel_id=1, source_target_pairs={{16,0},{17,1},{18,2},{19,3},{24,8},{25,9},{26,10},{27,11},{32,16},... | collective-permute-start | bytes 393224 | tf_op jit(solution)/shard_map/cond/branch_1_fun/ppermute | solution.py:299
  61.5 1.9 %collective-permute-start.9 = (bf16[256,256]{1,0:T(8,128)(2,1)S(1)}, bf16[256,256]{1,0:T(8,128)(2,1)S(1)}, u32[]{:S(2)}, u32[]{:S(2)}) collective-permute-start(bf16[256,256]{1,0:T(8,128)(2,1)S(1)} %get-tuple-element.46), channel_id=1, source_target_pairs={{32,0},{33,1},{34,2},{35,3},{40,8},{41,9},{42,10},{43,11},{48,16},... | collective-permute-start | bytes 393224 | tf_op jit(solution)/shard_map/cond/branch_1_fun/ppermute | solution.py:299
  63.4 6.5 %collective-permute-start.10 = (bf16[128,256]{1,0:T(8,128)(2,1)S(1)}, bf16[128,256]{1,0:T(8,128)(2,1)S(1)}, u32[]{:S(2)}, u32[]{:S(2)}) collective-permute-start(bf16[128,256]{1,0:T(8,128)(2,1)S(1)} %get-tuple-element.47), channel_id=1, source_target_pairs={{494,480},{495,481},{484,482},{485,483},{486,488},{487,489},{492,4... | collective-permute-start | bytes 196616 | tf_op jit(solution)/shard_map/cond/branch_1_fun/ppermute | solution.py:299
  70.0 5.2 %collective-permute-start.11 = (bf16[128,256]{1,0:T(8,128)(2,1)S(1)}, bf16[128,256]{1,0:T(8,128)(2,1)S(1)}, u32[]{:S(2)}, u32[]{:S(2)}) collective-permute-start(bf16[128,256]{1,0:T(8,128)(2,1)S(1)} %get-tuple-element.48), channel_id=1, source_target_pairs={{510,494},{511,495},{500,484},{501,485},{502,486},{503,487},{508,4... | collective-permute-start | bytes 196616 | tf_op jit(solution)/shard_map/cond/branch_1_fun/ppermute | solution.py:299
  75.2 1.3 %collective-permute-done.11.refs_1_ = bf16[128,256]{1,0:T(8,128)(2,1)S(1)} collective-permute-done((bf16[128,256]{1,0:T(8,128)(2,1)S(1)}, bf16[128,256]{1,0:T(8,128)(2,1)S(1)}, u32[]{:S(2)}, u32[]{:S(2)}) %collective-permute-start.11) | collective-permute-done | bytes 65568 | tf_op jit(solution)/shard_map/cond/branch_1_fun/ppermute | solution.py:299
  76.5 0.7 gather.3
  77.1 21.0 %all_to_all.14.split_ref = bf16[8,32,1280]{2,1,0:T(8,128)(2,1)S(1)} all-to-all(bf16[8,32,1280]{2,1,0:T(8,128)(2,1)S(1)} %bitcast.22), channel_id=1, replica_groups={{0,8,1,9,2,10,3,11},{4,12,5,13,6,14,7,15},{16,24,17,25,18,26,19,27},{20..., dimensions={0} | all-to-all | bytes 1310720 | tf_op jit(solution)/shard_map/cond/branch_1_fun/all_to_all | solution.py:303
  98.1 1.1 %unpack.3 = (bf16[32,4096]{1,0:T(8,128)(2,1)}, bf16[32,4096]{1,0:T(8,128)(2,1)}, bf16[32,1024]{1,0:T(8,128)(2,1)}, bf16[32,1024]{1,0:T(8,128)(2,1)}) custom-call(bf16[8,32,1280]{2,1,0:T(8,128)(2,1)S(1)} %all_to_all.14.split_ref), custom_call_target="tpu_custom_call" | custom-call | tf_op jit(solution)/shard_map/cond/branch_1_fun/unpack/pallas_call | solution.py:97
  (16 shorter events, 0.2 us)
Async XLA Ops:
  2.8 6.1 %copy-start.2 = (s32[256]{0:T(256)S(1)}, s32[256]{0:T(256)}, u32[]{:S(2)}) copy-start(s32[256]{0:T(256)} %param.10) | copy-start | bytes 3076
  2.9 25.0 %copy-start.1 = (s32[128,128]{1,0:T(8,128)S(1)}, s32[128,128]{1,0:T(8,128)}, u32[]{:S(2)}) copy-start(s32[128,128]{1,0:T(8,128)} %param.11) | copy-start | bytes 196612
  2.9 24.4 %all-to-all-start.2 = ((bf16[8,32,1280]{2,1,0:T(8,128)(2,1)}), bf16[8,32,1280]{2,1,0:T(8,128)(2,1)S(1)}, u32[]{:S(2)}, u32[]{:S(2)}) async-start(bf16[8,32,1280]{2,1,0:T(8,128)(2,1)} %pack.1), calls=%async_computation.2 | async-start | bytes 1310720 | tf_op jit(solution)/shard_map/all_to_all | solution.py:303
  9.0 18.2 %collective-permute-start.12 = (s32[1,256]{1,0:T(1,128)S(1)}, s32[1,256]{1,0:T(1,128)S(1)}, u32[]{:S(2)}, u32[]{:S(2)}) collective-permute-start(s32[1,256]{1,0:T(1,128)S(1)} %bitcast.36), channel_id=1, source_target_pairs={{0,8},{8,0},{1,9},{9,1},{2,10},{10,2},{3,11},{11,3},{4,12},{12,4},... | collective-permute-start | bytes 3080 | tf_op jit(solution)/shard_map/ppermute | solution.py:310
  16.2 0.7 copy-start
  28.0 23.1 %collective-permute-start.5 = (bf16[256,256]{1,0:T(8,128)(2,1)S(1)}, bf16[256,256]{1,0:T(8,128)(2,1)S(1)}, u32[]{:S(2)}, u32[]{:S(2)}) collective-permute-start(bf16[256,256]{1,0:T(8,128)(2,1)S(1)} %bitcast.24), channel_id=1, source_target_pairs={{0,32},{1,33},{2,34},{3,35},{8,40},{9,41},{10,42},{11,43},{16,48},... | collective-permute-start | bytes 393224 | tf_op jit(solution)/shard_map/cond/branch_1_fun/ppermute | solution.py:299
  38.9 12.2 %collective-permute-start.4 = (bf16[256,256]{1,0:T(8,128)(2,1)S(1)}, bf16[256,256]{1,0:T(8,128)(2,1)S(1)}, u32[]{:S(2)}, u32[]{:S(2)}) collective-permute-start(bf16[256,256]{1,0:T(8,128)(2,1)S(1)} %bitcast.25), channel_id=1, source_target_pairs={{0,16},{1,17},{2,18},{3,19},{8,24},{9,25},{10,26},{11,27},{16,32},... | collective-permute-start | bytes 393224 | tf_op jit(solution)/shard_map/cond/branch_1_fun/ppermute | solution.py:299
  41.1 7.1 %collective-permute-start.7 = (bf16[128,256]{1,0:T(8,128)(2,1)S(1)}, bf16[128,256]{1,0:T(8,128)(2,1)S(1)}, u32[]{:S(2)}, u32[]{:S(2)}) collective-permute-start(bf16[128,256]{1,0:T(8,128)(2,1)S(1)} %bitcast.35), channel_id=1, source_target_pairs={{494,510},{495,511},{484,500},{485,501},{486,502},{487,503},{492,5... | collective-permute-start | bytes 196616 | tf_op jit(solution)/shard_map/cond/branch_1_fun/ppermute | solution.py:299
  44.2 6.8 %collective-permute-start.6 = (bf16[128,256]{1,0:T(8,128)(2,1)S(1)}, bf16[128,256]{1,0:T(8,128)(2,1)S(1)}, u32[]{:S(2)}, u32[]{:S(2)}) collective-permute-start(bf16[128,256]{1,0:T(8,128)(2,1)S(1)} %bitcast_select_fusion), channel_id=1, source_target_pairs={{480,494},{481,495},{482,484},{483,485},{488,486},{489,487},{490,4... | collective-permute-start | bytes 196616 | tf_op jit(solution)/shard_map/cond/branch_1_fun/ppermute | solution.py:299
  56.2 20.3 %collective-permute-start.8 = (bf16[256,256]{1,0:T(8,128)(2,1)S(1)}, bf16[256,256]{1,0:T(8,128)(2,1)S(1)}, u32[]{:S(2)}, u32[]{:S(2)}) collective-permute-start(bf16[256,256]{1,0:T(8,128)(2,1)S(1)} %get-tuple-element.45), channel_id=1, source_target_pairs={{16,0},{17,1},{18,2},{19,3},{24,8},{25,9},{26,10},{27,11},{32,16},... | collective-permute-start | bytes 393224 | tf_op jit(solution)/shard_map/cond/branch_1_fun/ppermute | solution.py:299
  61.5 15.0 %collective-permute-start.9 = (bf16[256,256]{1,0:T(8,128)(2,1)S(1)}, bf16[256,256]{1,0:T(8,128)(2,1)S(1)}, u32[]{:S(2)}, u32[]{:S(2)}) collective-permute-start(bf16[256,256]{1,0:T(8,128)(2,1)S(1)} %get-tuple-element.46), channel_id=1, source_target_pairs={{32,0},{33,1},{34,2},{35,3},{40,8},{41,9},{42,10},{43,11},{48,16},... | collective-permute-start | bytes 393224 | tf_op jit(solution)/shard_map/cond/branch_1_fun/ppermute | solution.py:299
  63.4 11.7 %collective-permute-start.10 = (bf16[128,256]{1,0:T(8,128)(2,1)S(1)}, bf16[128,256]{1,0:T(8,128)(2,1)S(1)}, u32[]{:S(2)}, u32[]{:S(2)}) collective-permute-start(bf16[128,256]{1,0:T(8,128)(2,1)S(1)} %get-tuple-element.47), channel_id=1, source_target_pairs={{494,480},{495,481},{484,482},{485,483},{486,488},{487,489},{492,4... | collective-permute-start | bytes 196616 | tf_op jit(solution)/shard_map/cond/branch_1_fun/ppermute | solution.py:299
  70.0 6.5 %collective-permute-start.11 = (bf16[128,256]{1,0:T(8,128)(2,1)S(1)}, bf16[128,256]{1,0:T(8,128)(2,1)S(1)}, u32[]{:S(2)}, u32[]{:S(2)}) collective-permute-start(bf16[128,256]{1,0:T(8,128)(2,1)S(1)} %get-tuple-element.48), channel_id=1, source_target_pairs={{510,494},{511,495},{500,484},{501,485},{502,486},{503,487},{508,4... | collective-permute-start | bytes 196616 | tf_op jit(solution)/shard_map/cond/branch_1_fun/ppermute | solution.py:299

commit v8 on v7

--- a/solution.py
+++ b/solution.py
@@ -134,6 +134,10 @@
         compiler_params=pltpu.CompilerParams(vmem_limit_bytes=16 * 1024 * 1024),
         name="gather",
     )(place, pairing, od, *parts)
+
+
+def output_order(count):
+    return [0, 2, 1, 3, 4][:count]
 
 
 def attention_kernel(
@@ -188,6 +192,8 @@
         bias = jnp.concatenate([bias, bias], axis=1)
         keys = jnp.concatenate([kv[pl.ds(s, BLOCK), :DIM] for s in slots], axis=0)
         values = jnp.concatenate([kv[pl.ds(s, BLOCK), DIM:] for s in slots], axis=0)
+        keys_turned = keys.T
+        values_turned = values.T
         lanes_of = [rows_of(b, lane) for lane in range(PARTS // 2)]
         key_grad = None
         value_grad = None
@@ -203,14 +209,14 @@
             p = jnp.exp2((scores - peak) * (scale * math.log2(math.e)))
             p = p * (1.0 / jnp.sum(p, axis=0, keepdims=True))
             weights = p.astype(jnp.bfloat16)
-            out = dot(values, weights, 0, 0)
+            out = dot(values_turned, weights, 1, 0)
             g_turned = g.astype(jnp.float32).T
             delta = jnp.sum(
                 g_turned * out.astype(jnp.bfloat16).astype(jnp.float32), axis=0, keepdims=True
             )
             dweights = dot(values, g, 1, 1)
             dscores = (p * (dweights - delta)).astype(jnp.bfloat16)
-            dq = dot(keys, dscores, 0, 0) * scale
+            dq = dot(keys_turned, dscores, 1, 0) * scale
             key_new = dot(dscores, q, 1, 0)
             value_new = dot(weights, g, 1, 0)
             key_grad = key_new if key_grad is None else key_grad + key_new
@@ -227,8 +233,8 @@
             acc[pl.ds(s, BLOCK), :DIM] += key_grad[part]
             acc[pl.ds(s, BLOCK), DIM:] += value_grad[part]
 
-    for ref, begin, end in zip(parts, starts, starts[1:]):
-        ref[...] = acc[begin:end, :].astype(ref.dtype)
+    for ref, i in zip(parts, output_order(len(parts))):
+        ref[...] = acc[starts[i] : starts[i + 1], :].astype(ref.dtype)
 
 
 def attention(chain, place, pairing, live, docs, qg, halo):
@@ -243,7 +249,10 @@
         out_shape=(
             jax.ShapeDtypeStruct((ROWS, QG_WIDE), jnp.bfloat16),
             jax.ShapeDtypeStruct((ROWS, wide), jnp.float32),
-            *(jax.ShapeDtypeStruct(held.shape, jnp.bfloat16) for held in halo[1:]),
+            *(
+                jax.ShapeDtypeStruct(halo[i].shape, jnp.bfloat16)
+                for i in output_order(len(halo))[1:]
+            ),
         ),
         in_specs=[smem, smem] + [vmem] * (4 + len(halo)),
         out_specs=(vmem,) * (1 + len(halo)),
@@ -322,11 +331,13 @@
         if with_crossed:
             halo.append(move(jnp.where(later, own[BLOCK:], own[:BLOCK]), forth[2]))
             halo.append(move(own[BLOCK:], forth[3]))
-        od, own_grad, *partials = attention(
+        od, *partials = attention(
             chain, place, pairing, block_live, (doc, doc_other), arrived, halo
         )
-        partials = [move(part, pairs_of) for part, pairs_of in zip(partials, back)]
-        total = gather(place, pairing, od, (own_grad, *partials))
+        moved = {}
+        for i, part in zip(output_order(len(partials)), partials):
+            moved[i] = move(part, back[i - 1]) if i else part
+        total = gather(place, pairing, od, [moved[i] for i in range(len(moved))])
         return unpack(exchange(total.reshape(PARTS, PIECE, -1)))
 
     return lax.cond(

time: 99.8 us -> 99.8 us (level)
  no operation moved by 1% of the time
where the time goes in v8:
time: 99.8 us; the launch traced here: 99.2 us
  starting transfers between devices  50.3 us (50%)
  blocking collectives  21 us (21%)
  waiting for transfers between devices  13.8 us (14%)
  Pallas kernels  9.12 us (9%)
  between operations  2.65 us (3%)
  local copies, waits for them, and re-layouts  1.4 us (1%)
    ppermute x8, starting transfers between devices, move(): return lax.ppermute(x, axes, pairs_of)  37 us
    all_to_all x1, blocking collectives, exchange(): lax.all_to_all(x, ('side', 'lane'), split_axis=0, concat_axis=0, axis_ind...  21 us
    ppermute x1, waiting for transfers between devices, body(): doc_other = lax.ppermute(doc, 'side', [(0, 1), (1, 0)])  7.66 us
    ppermute x1, starting transfers between devices, body(): doc_other = lax.ppermute(doc, 'side', [(0, 1), (1, 0)])  7.19 us
    ppermute x8, waiting for transfers between devices, move(): return lax.ppermute(x, axes, pairs_of)  6.19 us
    all_to_all x1, starting transfers between devices, exchange(): lax.all_to_all(x, ('side', 'lane'), split_axis=0, concat_axis=0, axis_ind...  6.12 us
    pallas_call x1, Pallas kernels, attention(): pl.pallas_call(functools.partial(attention_kernel, chain, starts), out_sh...  5.15 us
    pallas_call x1, Pallas kernels, pack(): pl.pallas_call(pack_kernel, out_shape=jax.ShapeDtypeStruct((PARTS, PIECE,...  2.2 us
  transfers between devices with their start and end apart: 10, of which 4 were waited for; matrix products, arithmetic and copies ran while one was open for 1% of the time, Pallas kernels for 0%

profile of v8, /device:TPU:23, one launch (start us, length us, event | category | flops | bytes accessed | tf_op | source)
XLA Modules:
  0.0 99.2 jit_solution(4241639890212831622)
XLA Ops:
  0.6 2.2 %pack.1 = bf16[8,32,1280]{2,1,0:T(8,128)(2,1)} custom-call(bf16[32,4096]{1,0:T(8,128)(2,1)} %q_ref.1, bf16[32,4096]{1,0:T(8,128)(2,1)} %g_ref.1, bf16[32,1024]{1,0:T(8,128)(2,1)} %k_ref.1, bf16[32,1024]{1,0:T(8,128)(2,1)} %v_ref.1), custom_call_target="tpu_custom_call" | custom-call | tf_op jit(solution)/shard_map/pack/pallas_call | solution.py:73
  2.9 6.1 %all-to-all-start.2 = ((bf16[8,32,1280]{2,1,0:T(8,128)(2,1)}), bf16[8,32,1280]{2,1,0:T(8,128)(2,1)S(1)}, u32[]{:S(2)}, u32[]{:S(2)}) async-start(bf16[8,32,1280]{2,1,0:T(8,128)(2,1)} %pack.1), calls=%async_computation.2 | async-start | bytes 1310720 | tf_op jit(solution)/shard_map/all_to_all | solution.py:312
  9.0 7.2 %collective-permute-start.12 = (s32[1,256]{1,0:T(1,128)S(1)}, s32[1,256]{1,0:T(1,128)S(1)}, u32[]{:S(2)}, u32[]{:S(2)}) collective-permute-start(s32[1,256]{1,0:T(1,128)S(1)} %bitcast.36), channel_id=1, source_target_pairs={{0,8},{8,0},{1,9},{9,1},{2,10},{10,2},{3,11},{11,3},{4,12},{12,4},... | collective-permute-start | bytes 3080 | tf_op jit(solution)/shard_map/ppermute | solution.py:319
  16.2 0.6 copy-done
  16.9 0.1 slice.22
  17.0 0.6 compare_reduce_fusion
  17.7 0.6 fusion.1
  19.6 7.7 %collective-permute-done.12 = s32[1,256]{1,0:T(1,128)S(1)} collective-permute-done((s32[1,256]{1,0:T(1,128)S(1)}, s32[1,256]{1,0:T(1,128)S(1)}, u32[]{:S(2)}, u32[]{:S(2)}) %collective-permute-start.12) | collective-permute-done | bytes 1056 | tf_op jit(solution)/shard_map/ppermute | solution.py:319
  27.9 71.3 %conditional.1 = ((bf16[32,4096]{1,0:T(8,128)(2,1)}, bf16[32,4096]{1,0:T(8,128)(2,1)}, bf16[32,1024]{1,0:T(8,128)(2,1)}, bf16[32,1024]{1,0:T(8,128)(2,1)})) conditional(s32[]{:T(128)} %convert_element_type.3, (bf16[256,1280]{1,0:T(8,128)(2,1)S(1)}, s32[3]{0:T(128)S(1)}, s32[64]{0:T(128)S(1)}, s32[128,128]{1,0:T(8,128)S(1)}, s32[1,256]{1,0:T(1,128)S(1)}, ...), branch_computations={%region_1.0_spmd, %region_2.3_spmd} | conditional | flops 838893568 | bytes 8585545 | solution.py:343
  28.0 10.9 %collective-permute-start.5 = (bf16[256,256]{1,0:T(8,128)(2,1)S(1)}, bf16[256,256]{1,0:T(8,128)(2,1)S(1)}, u32[]{:S(2)}, u32[]{:S(2)}) collective-permute-start(bf16[256,256]{1,0:T(8,128)(2,1)S(1)} %bitcast.24), channel_id=1, source_target_pairs={{0,32},{1,33},{2,34},{3,35},{8,40},{9,41},{10,42},{11,43},{16,48},... | collective-permute-start | bytes 393224 | tf_op jit(solution)/shard_map/cond/branch_1_fun/ppermute | solution.py:308
  38.9 2.2 %collective-permute-start.4 = (bf16[256,256]{1,0:T(8,128)(2,1)S(1)}, bf16[256,256]{1,0:T(8,128)(2,1)S(1)}, u32[]{:S(2)}, u32[]{:S(2)}) collective-permute-start(bf16[256,256]{1,0:T(8,128)(2,1)S(1)} %bitcast.25), channel_id=1, source_target_pairs={{0,16},{1,17},{2,18},{3,19},{8,24},{9,25},{10,26},{11,27},{16,32},... | collective-permute-start | bytes 393224 | tf_op jit(solution)/shard_map/cond/branch_1_fun/ppermute | solution.py:308
  41.1 3.1 %collective-permute-start.7 = (bf16[128,256]{1,0:T(8,128)(2,1)S(1)}, bf16[128,256]{1,0:T(8,128)(2,1)S(1)}, u32[]{:S(2)}, u32[]{:S(2)}) collective-permute-start(bf16[128,256]{1,0:T(8,128)(2,1)S(1)} %bitcast.35), channel_id=1, source_target_pairs={{494,510},{495,511},{484,500},{485,501},{486,502},{487,503},{492,5... | collective-permute-start | bytes 196616 | tf_op jit(solution)/shard_map/cond/branch_1_fun/ppermute | solution.py:308
  44.2 1.9 %collective-permute-start.6 = (bf16[128,256]{1,0:T(8,128)(2,1)S(1)}, bf16[128,256]{1,0:T(8,128)(2,1)S(1)}, u32[]{:S(2)}, u32[]{:S(2)}) collective-permute-start(bf16[128,256]{1,0:T(8,128)(2,1)S(1)} %bitcast_select_fusion), channel_id=1, source_target_pairs={{480,494},{481,495},{482,484},{483,485},{488,486},{489,487},{490,4... | collective-permute-start | bytes 196616 | tf_op jit(solution)/shard_map/cond/branch_1_fun/ppermute | solution.py:308
  46.2 2.1 %collective-permute-done.7.refs_4_ = bf16[128,256]{1,0:T(8,128)(2,1)S(1)} collective-permute-done((bf16[128,256]{1,0:T(8,128)(2,1)S(1)}, bf16[128,256]{1,0:T(8,128)(2,1)S(1)}, u32[]{:S(2)}, u32[]{:S(2)}) %collective-permute-start.7) | collective-permute-done | bytes 65568 | tf_op jit(solution)/shard_map/cond/branch_1_fun/ppermute | solution.py:308
  48.2 2.8 %collective-permute-done.6.refs_3_ = bf16[128,256]{1,0:T(8,128)(2,1)S(1)} collective-permute-done((bf16[128,256]{1,0:T(8,128)(2,1)S(1)}, bf16[128,256]{1,0:T(8,128)(2,1)S(1)}, u32[]{:S(2)}, u32[]{:S(2)}) %collective-permute-start.6) | collective-permute-done | bytes 65568 | tf_op jit(solution)/shard_map/cond/branch_1_fun/ppermute | solution.py:308
  51.1 5.2 %attention.3 = (bf16[256,1024]{1,0:T(8,128)(2,1)S(1)}, f32[256,256]{1,0:T(8,128)S(1)}, bf16[256,256]{1,0:T(8,128)(2,1)S(1)}, bf16[256,256]{1,0:T(8,128)(2,1)S(1)...) custom-call(s32[3]{0:T(128)S(1)} %get-tuple-element.36.place_ref, s32[64]{0:T(128)S(1)} %get-tuple-element.37.pairing_ref, ...), custom_call_target="tpu_custom_call" | custom-call | flops 838860800 | bytes 3145728 | tf_op jit(solution)/shard_map/cond/branch_1_fun/attention/pallas_call | solution.py:247
  56.2 5.3 %collective-permute-start.8 = (bf16[256,256]{1,0:T(8,128)(2,1)S(1)}, bf16[256,256]{1,0:T(8,128)(2,1)S(1)}, u32[]{:S(2)}, u32[]{:S(2)}) collective-permute-start(bf16[256,256]{1,0:T(8,128)(2,1)S(1)} %get-tuple-element.45), channel_id=1, source_target_pairs={{16,0},{17,1},{18,2},{19,3},{24,8},{25,9},{26,10},{27,11},{32,16},... | collective-permute-start | bytes 393224 | tf_op jit(solution)/shard_map/cond/branch_1_fun/ppermute | solution.py:308
  61.5 1.9 %collective-permute-start.9 = (bf16[256,256]{1,0:T(8,128)(2,1)S(1)}, bf16[256,256]{1,0:T(8,128)(2,1)S(1)}, u32[]{:S(2)}, u32[]{:S(2)}) collective-permute-start(bf16[256,256]{1,0:T(8,128)(2,1)S(1)} %get-tuple-element.46), channel_id=1, source_target_pairs={{32,0},{33,1},{34,2},{35,3},{40,8},{41,9},{42,10},{43,11},{48,16},... | collective-permute-start | bytes 393224 | tf_op jit(solution)/shard_map/cond/branch_1_fun/ppermute | solution.py:308
  63.4 6.5 %collective-permute-start.10 = (bf16[128,256]{1,0:T(8,128)(2,1)S(1)}, bf16[128,256]{1,0:T(8,128)(2,1)S(1)}, u32[]{:S(2)}, u32[]{:S(2)}) collective-permute-start(bf16[128,256]{1,0:T(8,128)(2,1)S(1)} %get-tuple-element.47), channel_id=1, source_target_pairs={{494,480},{495,481},{484,482},{485,483},{486,488},{487,489},{492,4... | collective-permute-start | bytes 196616 | tf_op jit(solution)/shard_map/cond/branch_1_fun/ppermute | solution.py:308
  70.0 5.2 %collective-permute-start.11 = (bf16[128,256]{1,0:T(8,128)(2,1)S(1)}, bf16[128,256]{1,0:T(8,128)(2,1)S(1)}, u32[]{:S(2)}, u32[]{:S(2)}) collective-permute-start(bf16[128,256]{1,0:T(8,128)(2,1)S(1)} %get-tuple-element.48), channel_id=1, source_target_pairs={{510,494},{511,495},{500,484},{501,485},{502,486},{503,487},{508,4... | collective-permute-start | bytes 196616 | tf_op jit(solution)/shard_map/cond/branch_1_fun/ppermute | solution.py:308
  75.2 1.3 %collective-permute-done.11.refs_1_ = bf16[128,256]{1,0:T(8,128)(2,1)S(1)} collective-permute-done((bf16[128,256]{1,0:T(8,128)(2,1)S(1)}, bf16[128,256]{1,0:T(8,128)(2,1)S(1)}, u32[]{:S(2)}, u32[]{:S(2)}) %collective-permute-start.11) | collective-permute-done | bytes 65568 | tf_op jit(solution)/shard_map/cond/branch_1_fun/ppermute | solution.py:308
  76.5 0.7 gather.3
  77.1 21.0 %all_to_all.14.split_ref = bf16[8,32,1280]{2,1,0:T(8,128)(2,1)S(1)} all-to-all(bf16[8,32,1280]{2,1,0:T(8,128)(2,1)S(1)} %bitcast.22), channel_id=1, replica_groups={{0,8,1,9,2,10,3,11},{4,12,5,13,6,14,7,15},{16,24,17,25,18,26,19,27},{20..., dimensions={0} | all-to-all | bytes 1310720 | tf_op jit(solution)/shard_map/cond/branch_1_fun/all_to_all | solution.py:312
  98.1 1.1 %unpack.3 = (bf16[32,4096]{1,0:T(8,128)(2,1)}, bf16[32,4096]{1,0:T(8,128)(2,1)}, bf16[32,1024]{1,0:T(8,128)(2,1)}, bf16[32,1024]{1,0:T(8,128)(2,1)}) custom-call(bf16[8,32,1280]{2,1,0:T(8,128)(2,1)S(1)} %all_to_all.14.split_ref), custom_call_target="tpu_custom_call" | custom-call | tf_op jit(solution)/shard_map/cond/branch_1_fun/unpack/pallas_call | solution.py:97
  (16 shorter events, 0.2 us)
Async XLA Ops:
  2.8 6.1 %copy-start.2 = (s32[256]{0:T(256)S(1)}, s32[256]{0:T(256)}, u32[]{:S(2)}) copy-start(s32[256]{0:T(256)} %param.10) | copy-start | bytes 3076
  2.9 25.0 %copy-start.1 = (s32[128,128]{1,0:T(8,128)S(1)}, s32[128,128]{1,0:T(8,128)}, u32[]{:S(2)}) copy-start(s32[128,128]{1,0:T(8,128)} %param.11) | copy-start | bytes 196612
  2.9 24.4 %all-to-all-start.2 = ((bf16[8,32,1280]{2,1,0:T(8,128)(2,1)}), bf16[8,32,1280]{2,1,0:T(8,128)(2,1)S(1)}, u32[]{:S(2)}, u32[]{:S(2)}) async-start(bf16[8,32,1280]{2,1,0:T(8,128)(2,1)} %pack.1), calls=%async_computation.2 | async-start | bytes 1310720 | tf_op jit(solution)/shard_map/all_to_all | solution.py:312
  9.0 18.2 %collective-permute-start.12 = (s32[1,256]{1,0:T(1,128)S(1)}, s32[1,256]{1,0:T(1,128)S(1)}, u32[]{:S(2)}, u32[]{:S(2)}) collective-permute-start(s32[1,256]{1,0:T(1,128)S(1)} %bitcast.36), channel_id=1, source_target_pairs={{0,8},{8,0},{1,9},{9,1},{2,10},{10,2},{3,11},{11,3},{4,12},{12,4},... | collective-permute-start | bytes 3080 | tf_op jit(solution)/shard_map/ppermute | solution.py:319
  16.2 0.7 copy-start
  28.0 23.1 %collective-permute-start.5 = (bf16[256,256]{1,0:T(8,128)(2,1)S(1)}, bf16[256,256]{1,0:T(8,128)(2,1)S(1)}, u32[]{:S(2)}, u32[]{:S(2)}) collective-permute-start(bf16[256,256]{1,0:T(8,128)(2,1)S(1)} %bitcast.24), channel_id=1, source_target_pairs={{0,32},{1,33},{2,34},{3,35},{8,40},{9,41},{10,42},{11,43},{16,48},... | collective-permute-start | bytes 393224 | tf_op jit(solution)/shard_map/cond/branch_1_fun/ppermute | solution.py:308
  38.9 12.2 %collective-permute-start.4 = (bf16[256,256]{1,0:T(8,128)(2,1)S(1)}, bf16[256,256]{1,0:T(8,128)(2,1)S(1)}, u32[]{:S(2)}, u32[]{:S(2)}) collective-permute-start(bf16[256,256]{1,0:T(8,128)(2,1)S(1)} %bitcast.25), channel_id=1, source_target_pairs={{0,16},{1,17},{2,18},{3,19},{8,24},{9,25},{10,26},{11,27},{16,32},... | collective-permute-start | bytes 393224 | tf_op jit(solution)/shard_map/cond/branch_1_fun/ppermute | solution.py:308
  41.1 7.1 %collective-permute-start.7 = (bf16[128,256]{1,0:T(8,128)(2,1)S(1)}, bf16[128,256]{1,0:T(8,128)(2,1)S(1)}, u32[]{:S(2)}, u32[]{:S(2)}) collective-permute-start(bf16[128,256]{1,0:T(8,128)(2,1)S(1)} %bitcast.35), channel_id=1, source_target_pairs={{494,510},{495,511},{484,500},{485,501},{486,502},{487,503},{492,5... | collective-permute-start | bytes 196616 | tf_op jit(solution)/shard_map/cond/branch_1_fun/ppermute | solution.py:308
  44.2 6.8 %collective-permute-start.6 = (bf16[128,256]{1,0:T(8,128)(2,1)S(1)}, bf16[128,256]{1,0:T(8,128)(2,1)S(1)}, u32[]{:S(2)}, u32[]{:S(2)}) collective-permute-start(bf16[128,256]{1,0:T(8,128)(2,1)S(1)} %bitcast_select_fusion), channel_id=1, source_target_pairs={{480,494},{481,495},{482,484},{483,485},{488,486},{489,487},{490,4... | collective-permute-start | bytes 196616 | tf_op jit(solution)/shard_map/cond/branch_1_fun/ppermute | solution.py:308
  56.2 20.3 %collective-permute-start.8 = (bf16[256,256]{1,0:T(8,128)(2,1)S(1)}, bf16[256,256]{1,0:T(8,128)(2,1)S(1)}, u32[]{:S(2)}, u32[]{:S(2)}) collective-permute-start(bf16[256,256]{1,0:T(8,128)(2,1)S(1)} %get-tuple-element.45), channel_id=1, source_target_pairs={{16,0},{17,1},{18,2},{19,3},{24,8},{25,9},{26,10},{27,11},{32,16},... | collective-permute-start | bytes 393224 | tf_op jit(solution)/shard_map/cond/branch_1_fun/ppermute | solution.py:308
  61.5 15.0 %collective-permute-start.9 = (bf16[256,256]{1,0:T(8,128)(2,1)S(1)}, bf16[256,256]{1,0:T(8,128)(2,1)S(1)}, u32[]{:S(2)}, u32[]{:S(2)}) collective-permute-start(bf16[256,256]{1,0:T(8,128)(2,1)S(1)} %get-tuple-element.46), channel_id=1, source_target_pairs={{32,0},{33,1},{34,2},{35,3},{40,8},{41,9},{42,10},{43,11},{48,16},... | collective-permute-start | bytes 393224 | tf_op jit(solution)/shard_map/cond/branch_1_fun/ppermute | solution.py:308
  63.4 11.7 %collective-permute-start.10 = (bf16[128,256]{1,0:T(8,128)(2,1)S(1)}, bf16[128,256]{1,0:T(8,128)(2,1)S(1)}, u32[]{:S(2)}, u32[]{:S(2)}) collective-permute-start(bf16[128,256]{1,0:T(8,128)(2,1)S(1)} %get-tuple-element.47), channel_id=1, source_target_pairs={{494,480},{495,481},{484,482},{485,483},{486,488},{487,489},{492,4... | collective-permute-start | bytes 196616 | tf_op jit(solution)/shard_map/cond/branch_1_fun/ppermute | solution.py:308
  70.0 6.5 %collective-permute-start.11 = (bf16[128,256]{1,0:T(8,128)(2,1)S(1)}, bf16[128,256]{1,0:T(8,128)(2,1)S(1)}, u32[]{:S(2)}, u32[]{:S(2)}) collective-permute-start(bf16[128,256]{1,0:T(8,128)(2,1)S(1)} %get-tuple-element.48), channel_id=1, source_target_pairs={{510,494},{511,495},{500,484},{501,485},{502,486},{503,487},{508,4... | collective-permute-start | bytes 196616 | tf_op jit(solution)/shard_map/cond/branch_1_fun/ppermute | solution.py:308
